TPU v7x, 32 devices: a whole 2x2x4 slice. The times are simulated.
32 devices in a mesh: member: 2 (over y), lat: 4 (over z), lon: 2 (over x), ch: 2 (over core).
Axes of the slice: x: 2, y: 2, z: 4, core: 2. Of those that a mesh axis runs over, the one named last changes fastest.
Arguments:
- grid_latent: bfloat16 [16384, 512], P(('member', 'lat', 'lon', 'ch')), parts along dimension 0, may hold values from -6 to 6
- grid_owner: int32 [16384, 1], P(('member', 'lat', 'lon', 'ch')), parts along dimension 0, may hold values from 0 to 7; in each aligned block of 512 rows (0 to 511, 512 to 1023, ...) at most 128 rows name the same one
- grid_target: int32 [16384, 2], P(('member', 'lat', 'lon', 'ch')), parts along dimension 0, may hold values from 0 to 255
- mesh_latent: bfloat16 [8192, 512], P(('member', 'lat', 'lon', 'ch')), parts along dimension 0, may hold values from -6 to 6
- edge_latent: bfloat16 [16384, 512], P(('member', 'lat', 'lon', 'ch')), parts along dimension 0, may hold values from -6 to 6
- mesh_sender: int32 [16384], P(('member', 'lat', 'lon', 'ch')), parts along dimension 0, may hold values from 0 to 511
- mesh_receiver: int32 [16384], P(('member', 'lat', 'lon', 'ch')), parts along dimension 0, may hold values from 0 to 255
- halo_rows: int32 [2048], P(('member', 'lat', 'lon', 'ch')), parts along dimension 0, may hold values from 0 to 255
- weights: bfloat16 [13, 512, 512], P(None, 'ch'), may hold values from -0.25 to 0.25
- biases: float32 [4, 512], replicated, may hold values from -3 to 3
- gains: float32 [4, 512], replicated, may hold values from 0.5 to 1.5
Outputs:
- mesh_out: bfloat16 [8192, 512], P(('member', 'lat', 'lon', 'ch')), parts along dimension 0
There are 2 independent parts, one for each index of `member`. A program takes and returns all parts, laid end to end along the dimension named above; an argument that names none is the same for every part. Nothing has to cross between parts.
Inputs may be any that keep to these rules, and one draw needn't show every extreme that they name: `grid_owner`: among the rows of one device, no owner is named by more than 128 rows, and in every draw some device names some owner exactly 128 times. `mesh_sender`: entries 256 + p * 64 + i name entry i of the lent list of neighbour p.
All inputs are finite; a program needn't handle non-finite values.
Results may differ from a plain program's by a relative error of at most 0.008.
Values may be sent and summed in bfloat16 or wider, within the bound.
No kernel may reach another device: no remote copies, remote signals or barrier semaphores. Data moves between devices by JAX's collectives and lax.ppermute only.
A program may use at most 128 MiB of HBM per device.

v0:
```python
import jax
import jax.numpy as jnp
from jax import lax
from jax.sharding import PartitionSpec as P

EPSILON = 1e-05


def with_halo(cells, sides, width):
    for axis, dim in sides:
        count = lax.axis_size(axis)
        head = lax.slice_in_dim(cells, 0, width, axis=dim)
        tail = lax.slice_in_dim(cells, cells.shape[dim] - width, cells.shape[dim], axis=dim)
        cells = jnp.concatenate(
            [
                lax.ppermute(tail, axis, [(i, (i + 1) % count) for i in range(count)]),
                cells,
                lax.ppermute(head, axis, [((i + 1) % count, i) for i in range(count)]),
            ],
            axis=dim,
        )
    return cells


def layer_norm(values, scale):
    middle = jnp.mean(values, axis=-1, keepdims=True)
    spread = jnp.mean(jnp.square(values - middle), axis=-1, keepdims=True)
    return (values - middle) * lax.rsqrt(spread + EPSILON) * scale


def project(rows, matrix):
    return jnp.dot(rows, matrix, preferred_element_type=jnp.float32)


def per_device(
    grid_latent,
    grid_owner,
    grid_target,
    mesh_latent,
    edge_latent,
    mesh_sender,
    mesh_receiver,
    halo_rows,
    weights,
    biases,
    gains,
):
    rows_dev = grid_latent.shape[0]
    mesh_dev = mesh_latent.shape[0]
    width = grid_latent.shape[1]
    lat_count = lax.axis_size("lat")
    owners = lat_count * lax.axis_size("lon")
    capacity = max(2, 2 * rows_dev // owners)

    def matrices(first, count):
        return lax.all_gather(weights[first : first + count], "ch", axis=1, tiled=True)

    owner = grid_owner[:, 0]
    onehot = (owner[:, None] == jnp.arange(owners, dtype=jnp.int32)[None, :]).astype(jnp.int32)
    rank = jnp.sum((jnp.cumsum(onehot, axis=0) - onehot) * onehot, axis=1)
    place = owner * capacity + rank
    outgoing = jnp.zeros((owners * capacity, width), jnp.bfloat16).at[place].set(grid_latent)
    targets = jnp.full((owners * capacity, 2), -1, jnp.int32).at[place].set(grid_target)
    encoder_maps = matrices(0, 3)
    mesh_part = project(mesh_latent, encoder_maps[1])
    sent = (outgoing.reshape(owners, capacity, width), targets.reshape(owners, capacity, 2))
    pair = (
        lax.all_to_all(sent[0], ("lat", "lon"), split_axis=0, concat_axis=0, tiled=True),
        lax.all_to_all(sent[1], ("lat", "lon"), split_axis=0, concat_axis=0, tiled=True),
    )
    rows = pair[0]
    lead = rows.shape[:-1]
    flat_rows = rows.reshape(-1, width)
    flat_aims = pair[1].reshape(-1, 2)
    valid = (flat_aims >= 0).astype(jnp.float32)
    spots = jnp.maximum(flat_aims, 0)
    grid_part = project(flat_rows, encoder_maps[0])
    pre = grid_part[:, None, :] + mesh_part[spots] + biases[0]
    hidden = jax.nn.silu(pre).astype(jnp.bfloat16)
    notes = layer_norm(project(hidden.reshape(-1, width), encoder_maps[2]), gains[0])
    notes = notes.reshape(flat_rows.shape[0], 2, width) * valid[:, :, None]
    notes = notes.reshape(lead + (2, width))
    aims = pair[1]
    spots = jnp.maximum(aims.reshape(-1), 0)
    encoded_sum = jax.ops.segment_sum(
        notes.reshape(-1, width), spots, num_segments=mesh_dev
    ).astype(jnp.bfloat16)
    node_maps = matrices(3, 3)
    pre = project(mesh_latent, node_maps[0]) + project(encoded_sum, node_maps[1]) + biases[1]
    node_hidden = jax.nn.silu(pre).astype(jnp.bfloat16)
    mesh_mid = (
        mesh_latent.astype(jnp.float32) + layer_norm(project(node_hidden, node_maps[2]), gains[1])
    ).astype(jnp.bfloat16)
    lent = mesh_mid[halo_rows]
    padded = with_halo(lent[None, None], (("lat", 0), ("lon", 1)), 1)
    table = jnp.concatenate(
        [mesh_mid, padded[0, 1], padded[2, 1], padded[1, 0], padded[1, 2]], axis=0
    )
    edge_maps = matrices(6, 4)
    sender_part = project(table, edge_maps[1])
    receiver_part = project(mesh_mid, edge_maps[2])
    pre = (
        project(edge_latent, edge_maps[0])
        + sender_part[mesh_sender]
        + receiver_part[mesh_receiver]
        + biases[2]
    )
    proc_hidden = jax.nn.silu(pre).astype(jnp.bfloat16)
    proc_message = layer_norm(project(proc_hidden, edge_maps[3]), gains[2])
    processed_sum = jax.ops.segment_sum(proc_message, mesh_receiver, num_segments=mesh_dev).astype(
        jnp.bfloat16
    )
    update_maps = matrices(10, 3)
    pre = project(mesh_mid, update_maps[0]) + project(processed_sum, update_maps[1]) + biases[3]
    update_hidden = jax.nn.silu(pre).astype(jnp.bfloat16)
    return (
        mesh_mid.astype(jnp.float32) + layer_norm(project(update_hidden, update_maps[2]), gains[3])
    ).astype(jnp.bfloat16)


def solution(mesh):
    in_specs = (
        P(("member", "lat", "lon", "ch"), None),
        P(("member", "lat", "lon", "ch"), None),
        P(("member", "lat", "lon", "ch"), None),
        P(("member", "lat", "lon", "ch"), None),
        P(("member", "lat", "lon", "ch"), None),
        P(("member", "lat", "lon", "ch")),
        P(("member", "lat", "lon", "ch")),
        P(("member", "lat", "lon", "ch")),
        P(None, "ch", None),
        P(),
        P(),
    )
    out_specs = P(("member", "lat", "lon", "ch"), None)
    return jax.shard_map(
        per_device, mesh=mesh, in_specs=in_specs, out_specs=out_specs, check_vma=False
    )
```

profile of v0, /device:TPU:0, one launch (start us, length us, event | category | flops | bytes accessed | tf_op | source)
XLA Modules:
  0.0 135.8 jit_solution(428366116170130576)
XLA Ops:
  6.5 3.2 %fusion.38 = (bf16[3,256,512]{2,1,0:T(8,128)(2,1)}, bf16[3,256,512]{2,1,0:T(8,128)(2,1)}, bf16[3,256,512]{2,1,0:T(8,128)(2,1)}) fusion(bf16[13,256,512]{2,1,0:T(8,128)(2,1)} %param.19), kind=kLoop, calls=%fused_computation.99 | loop fusion | bytes 4718592 | tf_op jit(solution)/shard_map/slice | solution.py:56
  11.2 1.1 reduce-window.6
  12.9 1.8 %scatter_custom_fusion = s32[1024,2]{1,0:T(8,128)S(1)} fusion(s32[512]{0:T(512)S(1)} %bitcast.122, s32[512,2]{1,0:T(8,128)S(1)} %copy.21, s32[]{:T(128)} %constant.17.clone.1), kind=kCustom, calls=%fused_computation.57 | custom fusion | bytes 8196 | tf_op jit(solution)/shard_map/scatter | solution.py:63
  15.6 7.3 %all-to-all-start = ((s32[8,128,2]{1,2,0:T(2,128)}), s32[8,128,2]{1,2,0:T(2,128)S(1)}, u32[]{:S(2)}, u32[]{:S(2)}) async-start(s32[8,128,2]{1,2,0:T(2,128)} %copy.22), calls=%async_computation | async-start | bytes 16384 | tf_op jit(solution)/shard_map/all_to_all | solution.py:69
  22.9 2.3 %slice.103 = bf16[4,256,512]{2,1,0:T(8,128)(2,1)} slice(bf16[13,256,512]{2,1,0:T(8,128)(2,1)} %param.19), slice={[6:10], [0:256], [0:512]} | slice | bytes 2097152 | tf_op jit(solution)/shard_map/slice | solution.py:56
  25.3 4.0 %scatter_custom_fusion.1 = bf16[1024,512]{1,0:T(8,128)(2,1)} fusion(s32[512]{0:T(512)S(1)} %bitcast.123, bf16[512,512]{1,0:T(8,128)(2,1)} %param.11, bf16[]{:T(256)} %constant.21.clone.1), kind=kCustom, calls=%fused_computation.49 | custom fusion | bytes 1049088 | tf_op jit(solution)/shard_map/scatter | solution.py:62
  29.3 5.9 %all-to-all-start.1 = ((bf16[8,128,512]{2,1,0:T(8,128)(2,1)}), bf16[8,128,512]{2,1,0:T(8,128)(2,1)S(1)}, u32[]{:S(2)}, u32[]{:S(2)}) async-start(bf16[8,128,512]{2,1,0:T(8,128)(2,1)} %bitcast.8), calls=%async_computation.1 | async-start | bytes 2097152 | tf_op jit(solution)/shard_map/all_to_all | solution.py:68
  36.4 1.3 fusion.11
  37.7 8.9 %gather_fusion = f32[2048,512]{1,0:T(8,128)} fusion(f32[256,512]{1,0:T(8,128)S(1)} %fusion.11, s32[2048]{0:T(1024)S(1)} %broadcast_clamp_fusion), kind=kCustom, calls=%fused_computation | custom fusion | bytes 8396800 | tf_op jit(solution)/shard_map/gather | solution.py:78
  46.6 5.8 %reshape.154 = f32[1024,2,512]{2,1,0:T(2,128)} reshape(f32[2048,512]{1,0:T(8,128)} %gather_fusion) | data formatting | bytes 8388608 | tf_op jit(solution)/shard_map/gather | solution.py:78
  52.4 1.3 fusion.13
  53.8 6.9 %all-to-all-done.1 = bf16[8,128,512]{2,1,0:T(8,128)(2,1)S(1)} async-done(((bf16[8,128,512]{2,1,0:T(8,128)(2,1)}), bf16[8,128,512]{2,1,0:T(8,128)(2,1)S(1)}, u32[]{:S(2)}, u32[]{:S(2)}) %all-to-all-start.1) | async-done | bytes 1048608 | tf_op jit(solution)/shard_map/all_to_all | solution.py:68
  60.6 1.7 %fusion.12 = f32[1024,512]{1,0:T(8,128)S(1)} fusion(bf16[1024,512]{1,0:T(8,128)(2,1)S(1)} %bitcast.109, bf16[3,512,512]{2,1,0:T(8,128)(2,1)} %all-gather.7.cloned.1.call-done), kind=kOutput, calls=%fused_computation.40 | convolution fusion | flops 536870912 | bytes 3670016 | tf_op jit(solution)/shard_map/dot_general | solution.py:32
  62.4 6.9 %fusion = bf16[1024,2,512]{2,1,0:T(2,128)(2,1)} fusion(f32[1024,2,512]{2,1,0:T(2,128)} %reshape.154, f32[512]{0:T(512)S(1)} %bitcast.119, f32[1024,512]{1,0:T(8,128)S(1)} %fusion.12), kind=kLoop, calls=%fused_computation.11 | loop fusion | flops 7340032 | bytes 8390656 | tf_op jit(solution)/shard_map/convert_element_type | solution.py:79
  69.3 2.7 %convert_element_type.61 = bf16[2048,512]{1,0:T(8,128)(2,1)S(1)} reshape(bf16[1024,2,512]{2,1,0:T(2,128)(2,1)} %fusion) | data formatting | bytes 4194304 | tf_op jit(solution)/shard_map/convert_element_type | solution.py:79
  72.1 2.3 %fusion.41 = (f32[2048]{0:T(1024)S(1)}, f32[2048,512]{0,1:T(8,128)S(1)}) fusion(bf16[2048,512]{1,0:T(8,128)(2,1)S(1)} %convert_element_type.61, bf16[3,512,512]{2,1,0:T(8,128)(2,1)} %all-gather.7.cloned.1.call-done), kind=kOutput, calls=%fused_computation.102 | convolution fusion | flops 1074788352 | bytes 6823936 | tf_op jit(solution)/shard_map/dot_general | solution.py:32
  75.0 2.6 %multiply_multiply_fusion = f32[2048,512]{0,1:T(8,128)} fusion(f32[2048,512]{0,1:T(8,128)S(1)} %get-tuple-element.19, f32[2048]{0:T(1024)S(1)} %reshape.152, f32[512]{0:T(512)S(1)} %bitcast.121, f32[2048]{0:T(1024)S(1)} %add_rsqrt_fusion, f32[2048]{0:T(1024)S(1)} %broadcast_multiply_fusion), kind=kLoop, calls=%fused_computation.9 | loop fusion | flops 4194304 | bytes 8415232 | tf_op jit(solution)/shard_map/mul | solution.py:81
  77.6 5.3 %copy.27 = f32[2048,512]{1,0:T(8,128)} copy(f32[2048,512]{0,1:T(8,128)} %multiply_multiply_fusion) | data formatting | bytes 8388608 | tf_op jit(solution)/shard_map/mul | solution.py:81
  82.9 14.8 %scatter_custom_fusion.2 = f32[256,512]{1,0:T(8,128)S(1)} fusion(s32[2048]{0:T(1024)S(1)} %reshape.203, f32[2048,512]{1,0:T(8,128)} %copy.27, f32[]{:T(128)} %constant.16.clone.1), kind=kCustom, calls=%fused_computation.61 | custom fusion | flops 1048576 | bytes 524800 | tf_op jit(solution)/shard_map/scatter-add | solution.py:85
  97.7 1.9 %fusion.42 = (f32[256]{0:T(256)S(1)}, f32[256,512]{1,0:T(8,128)S(1)}) fusion(bf16[3,512,512]{2,1,0:T(8,128)(2,1)} %all-gather.5.cloned.1.call-done, f32[256,512]{1,0:T(8,128)S(1)} %fusion.13, f32[512]{0:T(512)S(1)} %bitcast.126, f32[256,512]{1,0:T(8,128)S(1)} %scatter_custom_fusion.2), kind=kOutput, calls=%fused_computation.103 | convolution fusion | flops 269614848 | bytes 2624512 | tf_op jit(solution)/shard_map/dot_general | solution.py:32
  100.8 3.8 %collective-permute-start.1 = (bf16[1,1,64,512]{3,2,1,0:T(8,128)(2,1)S(1)}, bf16[1,1,64,512]{3,2,1,0:T(8,128)(2,1)S(1)}, u32[]{:S(2)}, u32[]{:S(2)}) collective-permute-start(bf16[1,1,64,512]{3,2,1,0:T(8,128)(2,1)S(1)} %bitcast.112), channel_id=1, source_target_pairs={{4,0},{8,4},{12,8},{0,12},{5,1},{9,5},{13,9},{1,13},{6,2},{10,6},{... | collective-permute-start | bytes 196616 | tf_op jit(solution)/shard_map/ppermute | solution.py:18
  104.6 2.1 %fusion.8 = f32[256,512]{1,0:T(8,128)} fusion(bf16[256,512]{1,0:T(8,128)(2,1)S(1)} %get-tuple-element.6, bf16[3,512,512]{2,1,0:T(8,128)(2,1)} %all-gather.9.cloned.1.call-done), kind=kOutput, calls=%fused_computation.31 | convolution fusion | flops 134217728 | bytes 1310720 | tf_op jit(solution)/shard_map/dot_general | solution.py:32
  107.8 1.2 collective-permute-start.3
  109.0 1.3 fusion.5
  110.4 1.6 %gather_fusion.3 = f32[512,512]{1,0:T(8,128)S(1)} fusion(f32[256,512]{1,0:T(8,128)S(1)} %fusion.5, s32[1024]{0:T(1024)S(1)} %get-tuple-element.26), kind=kCustom, calls=%fused_computation.3 | custom fusion | bytes 2099200 | tf_op jit(solution)/shard_map/gather | solution.py:105
  112.0 1.5 %collective-permute-done.2 = bf16[3,1,64,512]{3,2,1,0:T(8,128)(2,1)} collective-permute-done((bf16[3,1,64,512]{3,2,1,0:T(8,128)(2,1)S(1)}, bf16[3,1,64,512]{3,2,1,0:T(8,128)(2,1)}, u32[]{:S(2)}, u32[]{:S(2)}) %collective-permute-start.2) | collective-permute-done | bytes 196640 | tf_op jit(solution)/shard_map/ppermute | solution.py:16
  114.3 1.2 collective-permute-done.3
  115.5 1.5 %fusion.6 = f32[512,512]{1,0:T(8,128)S(1)} fusion(bf16[512,512]{1,0:T(8,128)(2,1)S(1)} %fusion.30, bf16[4,512,512]{2,1,0:T(8,128)(2,1)} %all-gather.11.cloned.1.call-done), kind=kOutput, calls=%fused_computation.27 | convolution fusion | flops 268435456 | bytes 2097152 | tf_op jit(solution)/shard_map/dot_general | solution.py:32
  117.0 2.3 %gather_fusion.2 = f32[512,512]{1,0:T(8,128)} fusion(f32[512,512]{1,0:T(8,128)S(1)} %fusion.6, s32[1024]{0:T(1024)S(1)} %get-tuple-element.27), kind=kCustom, calls=%fused_computation.2 | custom fusion | bytes 2099200 | tf_op jit(solution)/shard_map/gather | solution.py:104
  119.3 2.5 %fusion.45 = (f32[512]{0:T(512)S(1)}, f32[512,512]{0,1:T(8,128)S(1)}) fusion(bf16[4,512,512]{2,1,0:T(8,128)(2,1)} %all-gather.11.cloned.1.call-done, f32[512,512]{1,0:T(8,128)S(1)} %gather_fusion.3, f32[512,512]{1,0:T(8,128)} %gather_fusion.2, f32[512]{0:T(512)S(1)} %bitcast.125, bf16[512,512]{1,0:T(8,128)(2,1)S(1)} %copy-done), kind=kOutput, calls=%fused_computation.104 | convolution fusion | flops 539229696 | bytes 4722688 | tf_op jit(solution)/shard_map/dot_general | solution.py:32
  122.6 3.7 %scatter_custom_fusion.3 = f32[256,512]{1,0:T(8,128)S(1)} fusion(s32[512]{0:T(512)S(1)} %copy-done.8, f32[512,512]{1,0:T(8,128)S(1)} %copy.28, f32[]{:T(128)} %constant.16.clone.1), kind=kCustom, calls=%fused_computation.59 | custom fusion | flops 262144 | bytes 524292 | tf_op jit(solution)/shard_map/scatter-add | solution.py:110
  126.3 1.9 %fusion.46 = (f32[256]{0:T(256)S(1)}, f32[256,512]{1,0:T(8,128)S(1)}) fusion(bf16[3,512,512]{2,1,0:T(8,128)(2,1)} %all-gather.9.cloned.1.call-done, f32[256,512]{1,0:T(8,128)S(1)} %copy-done.2, f32[512]{0:T(512)S(1)} %bitcast.124, f32[256,512]{1,0:T(8,128)S(1)} %scatter_custom_fusion.3), kind=kOutput, calls=%fused_computation.105 | convolution fusion | flops 269614848 | bytes 2624512 | tf_op jit(solution)/shard_map/dot_general | solution.py:32
  (81 shorter events, 9.4 us)
Async XLA Ops:
  6.5 112.8 %copy-start = (bf16[512,512]{1,0:T(8,128)(2,1)S(1)}, bf16[512,512]{1,0:T(8,128)(2,1)}, u32[]{:S(2)}) copy-start(bf16[512,512]{1,0:T(8,128)(2,1)} %param.15) | copy-start | bytes 1572868
  6.5 4.7 %copy-start.3 = (s32[512,1]{0,1:T(1,128)S(1)}, s32[512,1]{0,1:T(1,128)}, u32[]{:S(2)}) copy-start(s32[512,1]{0,1:T(1,128)} %param.12) | copy-start | bytes 6148
  6.5 6.1 %copy-start.6 = (s32[512,2]{0,1:T(2,128)S(1)}, s32[512,2]{0,1:T(2,128)}, u32[]{:S(2)}) copy-start(s32[512,2]{0,1:T(2,128)} %param.13) | copy-start | bytes 12292
  6.5 29.8 %all-gather.7.cloned.1.call-start = ((), (), s32[]{:S(2)}) async-start(), calls=%async_computation.3 | async-start | bytes 2359296 | tf_op jit(solution)/shard_map/all_gather | solution.py:56
  9.7 15.5 %copy-start.8 = (s32[512]{0:T(512)S(1)}, s32[512]{0:T(512)}, u32[]{:S(2)}) copy-start(s32[512]{0:T(512)} %param.17) | copy-start | bytes 6148
  9.7 15.5 %copy-start.7 = (s32[512]{0:T(512)S(1)}, s32[512]{0:T(512)}, u32[]{:S(2)}) copy-start(s32[512]{0:T(512)} %param.16) | copy-start | bytes 6148
  9.7 15.5 %copy-start.9 = (s32[64]{0:T(128)S(1)}, s32[64]{0:T(128)}, u32[]{:S(2)}) copy-start(s32[64]{0:T(128)} %param.18) | copy-start | bytes 772
  9.7 42.7 %all-gather.5.cloned.1.call-start = ((), (), s32[]{:S(2)}) async-start(), calls=%async_computation.2 | async-start | bytes 2359296 | tf_op jit(solution)/shard_map/all_gather | solution.py:56
  10.5 94.1 %all-gather.9.cloned.1.call-start = ((), (), s32[]{:S(2)}) async-start(), calls=%async_computation.4 | async-start | bytes 2359296 | tf_op jit(solution)/shard_map/all_gather | solution.py:56
  14.8 20.5 %copy-start.4 = (f32[4,512]{1,0:T(4,128)S(1)}, f32[4,512]{1,0:T(4,128)}, u32[]{:S(2)}) copy-start(f32[4,512]{1,0:T(4,128)} %param.20) | copy-start | bytes 24580
  14.8 20.5 %copy-start.5 = (f32[4,512]{1,0:T(4,128)S(1)}, f32[4,512]{1,0:T(4,128)}, u32[]{:S(2)}) copy-start(f32[4,512]{1,0:T(4,128)} %param.21) | copy-start | bytes 24580
  15.6 13.8 %all-to-all-start = ((s32[8,128,2]{1,2,0:T(2,128)}), s32[8,128,2]{1,2,0:T(2,128)S(1)}, u32[]{:S(2)}, u32[]{:S(2)}) async-start(s32[8,128,2]{1,2,0:T(2,128)} %copy.22), calls=%async_computation | async-start | bytes 16384 | tf_op jit(solution)/shard_map/all_to_all | solution.py:69
  22.8 86.2 %all-gather.11.cloned.1.call-start = ((), (), s32[]{:S(2)}) async-start(), calls=%async_computation.5 | async-start | bytes 3145728 | tf_op jit(solution)/shard_map/all_gather | solution.py:56
  25.2 11.2 %copy-start.1 = (bf16[256,512]{1,0:T(8,128)(2,1)S(1)}, bf16[256,512]{1,0:T(8,128)(2,1)}, u32[]{:S(2)}) copy-start(bf16[256,512]{1,0:T(8,128)(2,1)} %param.14) | copy-start | bytes 786436
  29.3 31.3 %all-to-all-start.1 = ((bf16[8,128,512]{2,1,0:T(8,128)(2,1)}), bf16[8,128,512]{2,1,0:T(8,128)(2,1)S(1)}, u32[]{:S(2)}, u32[]{:S(2)}) async-start(bf16[8,128,512]{2,1,0:T(8,128)(2,1)} %bitcast.8), calls=%async_computation.1 | async-start | bytes 2097152 | tf_op jit(solution)/shard_map/all_to_all | solution.py:68
  100.7 6.1 %collective-permute-start = (bf16[1,1,64,512]{3,2,1,0:T(8,128)(2,1)S(1)}, bf16[1,1,64,512]{3,2,1,0:T(8,128)(2,1)S(1)}, u32[]{:S(2)}, u32[]{:S(2)}) collective-permute-start(bf16[1,1,64,512]{3,2,1,0:T(8,128)(2,1)S(1)} %bitcast.111), channel_id=1, source_target_pairs={{0,4},{4,8},{8,12},{12,0},{1,5},{5,9},{9,13},{13,1},{2,6},{6,10},{... | collective-permute-start | bytes 196616 | tf_op jit(solution)/shard_map/ppermute | solution.py:16
  100.8 6.1 %collective-permute-start.1 = (bf16[1,1,64,512]{3,2,1,0:T(8,128)(2,1)S(1)}, bf16[1,1,64,512]{3,2,1,0:T(8,128)(2,1)S(1)}, u32[]{:S(2)}, u32[]{:S(2)}) collective-permute-start(bf16[1,1,64,512]{3,2,1,0:T(8,128)(2,1)S(1)} %bitcast.112), channel_id=1, source_target_pairs={{4,0},{8,4},{12,8},{0,12},{5,1},{9,5},{13,9},{1,13},{6,2},{10,6},{... | collective-permute-start | bytes 196616 | tf_op jit(solution)/shard_map/ppermute | solution.py:18
  106.9 6.6 %collective-permute-start.2 = (bf16[3,1,64,512]{3,2,1,0:T(8,128)(2,1)S(1)}, bf16[3,1,64,512]{3,2,1,0:T(8,128)(2,1)}, u32[]{:S(2)}, u32[]{:S(2)}) collective-permute-start(bf16[3,1,64,512]{3,2,1,0:T(8,128)(2,1)S(1)} %pad_maximum_fusion), channel_id=1, source_target_pairs={{0,2},{2,0},{1,3},{3,1},{4,6},{6,4},{5,7},{7,5},{8,10},{10,8},{9,1... | collective-permute-start | bytes 589832 | tf_op jit(solution)/shard_map/ppermute | solution.py:16
  107.8 7.7 %collective-permute-start.3 = (bf16[3,1,64,512]{3,2,1,0:T(8,128)(2,1)S(1)}, bf16[3,1,64,512]{3,2,1,0:T(8,128)(2,1)S(1)}, u32[]{:S(2)}, u32[]{:S(2)}) collective-permute-start(bf16[3,1,64,512]{3,2,1,0:T(8,128)(2,1)S(1)} %pad_maximum_fusion), channel_id=1, source_target_pairs={{2,0},{0,2},{3,1},{1,3},{6,4},{4,6},{7,5},{5,7},{10,8},{8,10},{11,... | collective-permute-start | bytes 589832 | tf_op jit(solution)/shard_map/ppermute | solution.py:18
  121.9 4.4 %copy-start.2 = (f32[256,512]{1,0:T(8,128)S(1)}, f32[256,512]{1,0:T(8,128)}, u32[]{:S(2)}) copy-start(f32[256,512]{1,0:T(8,128)} %fusion.8) | copy-start | bytes 1572868
Sparse Core Ops, SparseCore 0:
  9.9 12.4 all-gather.6
  23.9 10.9 all-gather.4
  36.5 10.9 all-gather.8
  48.9 11.7 all-gather.10
where the time goes:
time: 137 us; the launch traced here: 136 us
  local copies, waits for them, and re-layouts  42.2 us (31%)
  other arithmetic  31.8 us (23%)
  starting transfers between devices  19.2 us (14%)
  matrix products  18 us (13%)
  between operations  13.5 us (10%)
  waiting for transfers between devices  11.1 us (8%)
    dot_general x10, matrix products, project(): return jnp.dot(rows, matrix, preferred_element_type=jnp.float32)  18 us
    scatter-add x1, other arithmetic, per_device(): jax.ops.segment_sum(notes.reshape(-1, width), spots, num_segments=mesh_dev)  14.8 us
    gather x2, local copies, waits for them, and re-layouts, per_device(): pre = grid_part[:, None, :] + mesh_part[spots] + biases[0]  14.7 us
    all_to_all x1, starting transfers between devices, per_device(): lax.all_to_all(sent[1], ('lat', 'lon'), split_axis=0, concat_axis=0, tile...  7.25 us
    convert_element_type x1, other arithmetic, per_device(): hidden = jax.nn.silu(pre).astype(jnp.bfloat16)  6.94 us
    all_to_all x1, waiting for transfers between devices, per_device(): lax.all_to_all(sent[0], ('lat', 'lon'), split_axis=0, concat_axis=0, tile...  6.85 us
    all_to_all x1, starting transfers between devices, per_device(): lax.all_to_all(sent[0], ('lat', 'lon'), split_axis=0, concat_axis=0, tile...  5.86 us
    slice x2, local copies, waits for them, and re-layouts, matrices(): weights[first:first + count]  5.47 us
  transfers between devices with their start and end apart: 10, of which 5 were waited for; matrix products, arithmetic and copies ran while one was open for 55% of the time, Pallas kernels for 0%

commit v1 on v0

v1 whole, which is shorter than its diff:
```python
import functools

import jax
import jax.numpy as jnp
from jax import lax
from jax.experimental import pallas as pl
from jax.experimental.pallas import tpu as pltpu
from jax.sharding import PartitionSpec as P

EPSILON = 1e-05
LANES = 128
AIM_ROWS = 16
F32 = jnp.float32
BF16 = jnp.bfloat16
ANY = pl.BlockSpec(memory_space=pl.ANY)
VMEM = pl.BlockSpec(memory_space=pltpu.VMEM)
VMEM_LIMIT = 24 * 1024 * 1024


def mm(left, right):
    return jnp.dot(left, right, preferred_element_type=F32)


def mm_nt(left, right):
    return lax.dot_general(left, right, (((1,), (1,)), ((), ())), preferred_element_type=F32)


def silu(values):
    half = 0.5 * values
    return (half + half * jnp.tanh(half)).astype(BF16)


def normed(values):
    middle = jnp.mean(values, axis=-1, keepdims=True)
    centred = values - middle
    spread = jnp.mean(centred * centred, axis=-1, keepdims=True)
    return centred * lax.rsqrt(spread + EPSILON)


def as_bf16(mask):
    return jnp.where(mask, 1.0, 0.0).astype(BF16)


def down(row, count):
    return as_bf16(lax.broadcasted_iota(jnp.int32, (count, row.shape[1]), 0) == row)


def along(column, count):
    return as_bf16(lax.broadcasted_iota(jnp.int32, (column.shape[0], count), 1) == column)


def turned(row):
    wide = jnp.broadcast_to(row.astype(F32), (8, row.shape[1]))
    return jnp.transpose(wide)[:, :1].astype(jnp.int32)


def fetch(mine_ref, other_ref, into, sems, picks):
    half = mine_ref.shape[1]
    core = lax.axis_index("ch")
    copies = []
    for i, (pick, place) in enumerate(picks):
        for j, (ref, at) in enumerate(((mine_ref, core), (other_ref, 1 - core))):
            rows = pl.ds(pl.multiple_of(at * half, half), half)
            copy = pltpu.make_async_copy(
                ref.at[pick], into[place].at[rows, :], sems.at[2 * i + j]
            )
            copy.start()
            copies.append(copy)
    return copies


def arrive(copies, count=1):
    for copy in copies[: 2 * count]:
        copy.wait()
    del copies[: 2 * count]


def dispatch_kernel(owners, capacity, exchange, owner_ref, target_ref, latent_ref, *outs):
    rows, width = latent_ref.shape
    padded = max(16, owners)
    number = lax.broadcasted_iota(jnp.int32, (padded, rows), 0)
    named = number == owner_ref[...]
    before = as_bf16(
        lax.broadcasted_iota(jnp.int32, (rows, rows), 0)
        < lax.broadcasted_iota(jnp.int32, (rows, rows), 1)
    )
    rank = mm(as_bf16(named), before).astype(jnp.int32)
    place = jnp.sum(jnp.where(named, number * capacity + rank, 0), axis=0, keepdims=True)
    aims = jnp.concatenate(
        [
            (target_ref[...] + 1).astype(F32),
            jnp.zeros((AIM_ROWS - target_ref.shape[0], rows), F32),
        ],
        axis=0,
    ).astype(BF16)
    latent = latent_ref[...]
    me = lax.axis_index("lat") * lax.axis_size("lon") + lax.axis_index("lon")
    for q, out in enumerate(outs):
        base = (me ^ q) * capacity if exchange else q * LANES
        pick = as_bf16(lax.broadcasted_iota(jnp.int32, (LANES, rows), 0) + base == place)
        data = mm(pick, latent).astype(BF16)
        for j in range(width // LANES):
            out[j * LANES : (j + 1) * LANES, :] = data[:, j * LANES : (j + 1) * LANES]
        out[width : width + AIM_ROWS, :] = mm_nt(aims, pick).astype(BF16)


def encode(chunks, first, third, mesh_part, bias):
    width = first.shape[0]
    nodes = mesh_part.shape[0]
    total = None
    for chunk in chunks:
        rows = jnp.concatenate(
            [chunk[j * LANES : (j + 1) * LANES, :] for j in range(width // LANES)], axis=1
        )
        aims = chunk[width : width + AIM_ROWS, :].astype(F32)
        columns = jnp.transpose(aims).astype(jnp.int32) - 1
        lines = aims.astype(jnp.int32) - 1
        part = mm(rows, first) + bias
        hidden = jnp.concatenate(
            [silu(part + mm(along(columns[:, k : k + 1], nodes), mesh_part)) for k in range(2)],
            axis=0,
        )
        notes = normed(mm(hidden, third)).astype(BF16)
        spread = jnp.concatenate([down(lines[k : k + 1, :], nodes) for k in range(2)], axis=1)
        partial = mm(spread, notes)
        total = partial if total is None else total + partial
    return total


def first_kernel(mine, other, mesh, chunk, biases, sum_out, part_out, first_out, third_out, second, sems):
    into = [first_out, second, third_out]
    copies = fetch(mine, other, into, sems, [(1, 1), (0, 0), (2, 2)])
    arrive(copies)
    part = mm(mesh[...], second[...]).astype(BF16)
    part_out[...] = part
    arrive(copies, 2)
    sum_out[...] = encode([chunk], first_out[...], third_out[...], part, biases[0:1, :])


def more_kernel(total, part, first, third, biases, *rest):
    *chunks, out = rest
    out[...] = total[...] + encode(chunks, first[...], third[...], part[...], biases[0:1, :])


def node_kernel(total, part, first, third, biases, gains, mine, other, mesh, lend, *rest):
    *chunks, mid_out, lent_out, node_maps, sems = rest
    maps = [node_maps.at[0], node_maps.at[1], node_maps.at[2]]
    copies = fetch(mine, other, maps, sems, [(3, 0), (4, 1), (5, 2)])
    sums = total[...] + encode(chunks, first[...], third[...], part[...], biases[0:1, :])
    encoded = (sums * gains[0:1, :]).astype(BF16)
    arrive(copies, 3)
    latent = mesh[...]
    hidden = silu(mm(latent, node_maps[0]) + mm(encoded, node_maps[1]) + biases[1:2, :])
    mid = (
        latent.astype(F32) + normed(mm(hidden, node_maps[2])) * gains[1:2, :]
    ).astype(BF16)
    mid_out[...] = mid
    picks = along(turned(lend[...]), mid.shape[0])
    lent_out[...] = mm(picks, mid).astype(BF16)


def local_kernel(mid_ref, edges, sender, receiver, biases, mine, other, pre_out, maps, sems):
    into = [maps.at[0], maps.at[1], maps.at[2]]
    copies = fetch(mine, other, into, sems, [(6, 0), (7, 1), (8, 2)])
    mid = mid_ref[...]
    nodes = mid.shape[0]
    at_sender = along(turned(sender[...]), nodes)
    at_receiver = along(turned(receiver[...]), nodes)
    arrive(copies, 3)
    pre = mm(edges[...], maps[0]) + biases[2:3, :]
    pre = pre + mm(at_sender, mm(mid, maps[1]).astype(BF16))
    pre_out[...] = pre + mm(at_receiver, mm(mid, maps[2]).astype(BF16))


def process_kernel(pre, mid_ref, sender, receiver, biases, gains, mine, other, *rest):
    *lent, out, maps, sems = rest
    into = [maps.at[i] for i in range(5)]
    copies = fetch(
        mine, other, into, sems, [(7, 0), (9, 1), (10, 2), (11, 3), (12, 4)]
    )
    mid = mid_ref[...]
    nodes = mid.shape[0]
    table = jnp.concatenate([ref[...] for ref in lent], axis=0)
    depth = lent[0].shape[0]
    entry = sender[...] - nodes
    if len(lent) == 3:
        entry = jnp.where(entry >= 3 * depth, entry - depth, entry)
    from_halo = along(turned(entry), len(lent) * depth)
    arrive(copies)
    halo = mm(table, maps[0]).astype(BF16)
    hidden = silu(pre[...] + mm(from_halo, halo))
    arrive(copies)
    notes = normed(mm(hidden, maps[1])).astype(BF16)
    sums = mm(down(receiver[...], nodes), notes)
    processed = (sums * gains[2:3, :]).astype(BF16)
    arrive(copies, 3)
    hidden = silu(mm(mid, maps[2]) + mm(processed, maps[3]) + biases[3:4, :])
    out[...] = (
        mid.astype(F32) + normed(mm(hidden, maps[4])) * gains[3:4, :]
    ).astype(BF16)


def call(kernel, outs, ins, specs, scratch=(), flops=0, moved=0):
    return pl.pallas_call(
        kernel,
        out_shape=[jax.ShapeDtypeStruct(shape, kind) for shape, kind in outs],
        in_specs=specs,
        out_specs=[VMEM] * len(outs),
        scratch_shapes=list(scratch),
        compiler_params=pltpu.CompilerParams(vmem_limit_bytes=VMEM_LIMIT),
        cost_estimate=pl.CostEstimate(flops=flops, bytes_accessed=moved, transcendentals=0),
    )(*ins)


def swap(value, axes, step):
    count = lax.axis_size(axes)
    return lax.ppermute(value, axes, [(i, i ^ step) for i in range(count)])


def shift(value, axis, step):
    count = lax.axis_size(axis)
    return lax.ppermute(value, axis, [(i, (i + step) % count) for i in range(count)])


def sent_whole(chunks, owners, capacity, width):
    count = len(chunks)
    stack = jnp.stack(chunks)
    rows = stack[:, :width].reshape(count, width // LANES, LANES, LANES)
    rows = rows.transpose(0, 2, 1, 3).reshape(owners, capacity, width)
    aims = stack[:, width:].transpose(0, 2, 1).reshape(owners, capacity, AIM_ROWS)
    rows, aims = (
        lax.all_to_all(part, ("lat", "lon"), split_axis=0, concat_axis=0, tiled=True)
        for part in (rows, aims)
    )
    rows = rows.reshape(count, LANES, width // LANES, LANES).transpose(0, 2, 1, 3)
    aims = aims.reshape(count, LANES, AIM_ROWS).transpose(0, 2, 1)
    stack = jnp.concatenate([rows.reshape(count, width, LANES), aims], axis=1)
    return [stack[i] for i in range(count)]


def per_device(
    grid_latent,
    grid_owner,
    grid_target,
    mesh_latent,
    edge_latent,
    mesh_sender,
    mesh_receiver,
    halo_rows,
    weights,
    biases,
    gains,
):
    rows_dev, width = grid_latent.shape
    nodes = mesh_latent.shape[0]
    edges = edge_latent.shape[0]
    lon_count = lax.axis_size("lon")
    owners = lax.axis_size("lat") * lon_count
    capacity = max(2, 2 * rows_dev // owners)
    exchange = capacity == LANES and owners <= 16 and owners & (owners - 1) == 0
    square = (width, width)

    other = swap(weights, "ch", 1)

    count = owners * capacity // LANES
    chunk_shape = ((width + AIM_ROWS, LANES), BF16)
    chunks = call(
        functools.partial(dispatch_kernel, owners, capacity, exchange),
        [chunk_shape] * count,
        (grid_owner.T, grid_target.T, grid_latent),
        [VMEM] * 3,
        flops=10**9,
        moved=2 * 10**6,
    )
    if exchange:
        arrived = {0: chunks[0]}
        for step in [4, 5, 6, 7, 2, 3, 1] if owners == 8 else range(1, owners):
            arrived[step] = swap(chunks[step], ("lat", "lon"), step)
        groups = [[0], [4, 5], [6, 7, 2], [3, 1]] if owners == 8 else [[0], list(range(1, owners))]
    else:
        arrived = dict(enumerate(sent_whole(chunks, owners, capacity, width)))
        groups = [[0], list(range(1, count))]

    sems = lambda n: pltpu.SemaphoreType.DMA((2 * n,))
    total, part, first, third = call(
        first_kernel,
        [((nodes, width), F32), ((nodes, width), BF16), (square, BF16), (square, BF16)],
        (weights, other, mesh_latent, arrived[0], biases),
        [ANY, ANY, VMEM, VMEM, VMEM],
        [pltpu.VMEM(square, BF16), sems(3)],
        flops=5 * 10**8,
        moved=3 * 10**6,
    )
    for group in groups[1:-1]:
        (total,) = call(
            more_kernel,
            [((nodes, width), F32)],
            (total, part, first, third, biases, *[arrived[i] for i in group]),
            [VMEM] * (5 + len(group)),
            flops=4 * 10**8 * len(group),
            moved=2 * 10**6,
        )
    mid, lent = call(
        node_kernel,
        [((nodes, width), BF16), ((halo_rows.shape[0], width), BF16)],
        (total, part, first, third, biases, gains, weights, other, mesh_latent)
        + (halo_rows.reshape(1, -1), *[arrived[i] for i in groups[-1]]),
        [VMEM] * 6 + [ANY, ANY, VMEM, VMEM] + [VMEM] * len(groups[-1]),
        [pltpu.VMEM((3, *square), BF16), sems(3)],
        flops=10**9,
        moved=3 * 10**6,
    )
    halo = [shift(lent, "lat", 1), shift(lent, "lat", -1), shift(lent, "lon", 1)]
    if lon_count != 2:
        halo.append(shift(lent, "lon", -1))
    sender, receiver = mesh_sender.reshape(1, -1), mesh_receiver.reshape(1, -1)
    (pre,) = call(
        local_kernel,
        [((edges, width), F32)],
        (mid, edge_latent, sender, receiver, biases, weights, other),
        [VMEM] * 5 + [ANY, ANY],
        [pltpu.VMEM((3, *square), BF16), sems(3)],
        flops=10**9,
        moved=3 * 10**6,
    )
    (out,) = call(
        process_kernel,
        [((nodes, width), BF16)],
        (pre, mid, sender, receiver, biases, gains, weights, other, *halo),
        [VMEM] * 6 + [ANY, ANY] + [VMEM] * len(halo),
        [pltpu.VMEM((5, *square), BF16), sems(5)],
        flops=10**9,
        moved=3 * 10**6,
    )
    return out


def solution(mesh):
    in_specs = (
        P(("member", "lat", "lon", "ch"), None),
        P(("member", "lat", "lon", "ch"), None),
        P(("member", "lat", "lon", "ch"), None),
        P(("member", "lat", "lon", "ch"), None),
        P(("member", "lat", "lon", "ch"), None),
        P(("member", "lat", "lon", "ch")),
        P(("member", "lat", "lon", "ch")),
        P(("member", "lat", "lon", "ch")),
        P(None, "ch", None),
        P(),
        P(),
    )
    out_specs = P(("member", "lat", "lon", "ch"), None)
    return jax.shard_map(
        per_device, mesh=mesh, in_specs=in_specs, out_specs=out_specs, check_vma=False
    )
```

time: 137 us -> 53.2 us (0.39)
  local copies, waits for them, and re-layouts: 42.2 us -> 2.7 us
  other arithmetic: 31.8 us -> 0 us
  matrix products: 18 us -> 0 us
  Pallas kernels: 0 us -> 15.2 us
  between operations: 13.5 us -> 0.15 us
  waiting for transfers between devices: 11.1 us -> 19 us
  starting transfers between devices: 19.2 us -> 16 us
    gather x5 -> x0, local copies, waits for them, and re-layouts: 19.4 us -> none  [the longest x2 14.7 us: per_device(): pre = grid_part[:, None, :] + mesh_part[spots] + biases[0]]
    scatter-add x2 -> x0, other arithmetic: 18.5 us -> none  [the longest x1 14.8 us: per_device(): jax.ops.segment_sum(notes.reshape(-1, width), spots, num_segments=mesh_dev)]
    dot_general x10 -> x0, matrix products: 18 us -> none  [project(): return jnp.dot(rows, matrix, preferred_element_type=jnp.float32)]
    ppermute x4 -> x11, waiting for transfers between devices: 2.72 us -> 19 us  [the longest x8 14.8 us: swap(): return lax.ppermute(value, axes, [(i, i ^ step) for i in range(count)])]
    pallas_call x0 -> x7, Pallas kernels: none -> 15.2 us  [call(): pl.pallas_call(kernel, out_shape=[jax.ShapeDtypeStruct(shape, kind) for s...]
    all_to_all x2 -> x0, starting transfers between devices: 13.1 us -> none  [the longest x1 7.25 us: per_device(): lax.all_to_all(sent[1], ('lat', 'lon'), split_axis=0, concat_axis=0, tile...]
    ppermute x4 -> x11, starting transfers between devices: 5.96 us -> 16 us  [the longest x8 10.8 us: swap(): return lax.ppermute(value, axes, [(i, i ^ step) for i in range(count)])]
    convert_element_type x4 -> x0, other arithmetic: 7.83 us -> none  [the longest x1 6.94 us: per_device(): hidden = jax.nn.silu(pre).astype(jnp.bfloat16)]
  transfers between devices with their start and end apart: 10 -> 11, of which waited for: 5 -> 5; matrix products, arithmetic and copies ran while one was open for 55% -> 0% of each run, Pallas kernels for 0% -> 16%
where the time goes in v1:
time: 53.2 us; the launch traced here: 53 us
  waiting for transfers between devices  19 us (36%)
  starting transfers between devices  16 us (30%)
  Pallas kernels  15.2 us (29%)
  local copies, waits for them, and re-layouts  2.7 us (5%)
    pallas_call x7, Pallas kernels, call(): pl.pallas_call(kernel, out_shape=[jax.ShapeDtypeStruct(shape, kind) for s...  15.2 us
    ppermute x8, waiting for transfers between devices, swap(): return lax.ppermute(value, axes, [(i, i ^ step) for i in range(count)])  14.8 us
    ppermute x8, starting transfers between devices, swap(): return lax.ppermute(value, axes, [(i, i ^ step) for i in range(count)])  10.8 us
    ppermute x3, starting transfers between devices, shift(): lax.ppermute(value, axis, [(i, (i + step) % count) for i in range(count)])  5.15 us
    ppermute x3, waiting for transfers between devices, shift(): lax.ppermute(value, axis, [(i, (i + step) % count) for i in range(count)])  4.22 us
    unnamed x22, local copies, waits for them, and re-layouts  2.7 us
  transfers between devices with their start and end apart: 11, of which 5 were waited for; matrix products, arithmetic and copies ran while one was open for 0% of the time, Pallas kernels for 16%

profile of v1, /device:TPU:0, one launch (start us, length us, event | category | flops | bytes accessed | tf_op | source)
XLA Modules:
  0.0 53.0 jit_solution(15178668481109838246)
XLA Ops:
  0.0 0.5 collective-permute-start
  0.5 1.3 %copy-done.8 = bf16[512,512]{1,0:T(8,128)(2,1)S(1)} copy-done((bf16[512,512]{1,0:T(8,128)(2,1)S(1)}, bf16[512,512]{1,0:T(8,128)(2,1)}, u32[]{:S(2)}) %copy-start.8) | copy-done | bytes 524312
  1.8 0.7 %copy-done.9 = s32[512,2]{0,1:T(2,128)S(1)} copy-done((s32[512,2]{0,1:T(2,128)S(1)}, s32[512,2]{0,1:T(2,128)}, u32[]{:S(2)}) %copy-start.9) | copy-done | bytes 4120
  2.5 0.7 %copy-done.10 = s32[512,1]{0,1:T(1,128)S(1)} copy-done((s32[512,1]{0,1:T(1,128)S(1)}, s32[512,1]{0,1:T(1,128)}, u32[]{:S(2)}) %copy-start.10) | copy-done | bytes 2072
  3.2 1.2 %shard_map.109 = (bf16[528,128]{1,0:T(8,128)(2,1)S(1)}, bf16[528,128]{1,0:T(8,128)(2,1)S(1)}, bf16[528,128]{1,0:T(8,128)(2,1)S(1)}, bf16[528,128]{1,0:T(8,128)(2...) custom-call(s32[1,512]{1,0:T(1,128)S(1)} %bitcast.11, ...), custom_call_target="tpu_custom_call" | custom-call | flops 1000000000 | bytes 2000000 | tf_op jit(solution)/shard_map/pallas_call | solution.py:204
  4.4 3.6 %collective-permute-start.1 = (bf16[528,128]{1,0:T(8,128)(2,1)S(1)}, bf16[528,128]{1,0:T(8,128)(2,1)S(1)}, u32[]{:S(2)}, u32[]{:S(2)}) collective-permute-start(bf16[528,128]{1,0:T(8,128)(2,1)S(1)} %get-tuple-element.24), channel_id=1, source_target_pairs={{0,8},{2,10},{4,12},{6,14},{8,0},{10,2},{12,4},{14,6},{1,9},{3,11}... | collective-permute-start | bytes 405512 | tf_op jit(solution)/shard_map/ppermute | solution.py:217
  7.9 1.3 %collective-permute-start.2 = (bf16[528,128]{1,0:T(8,128)(2,1)S(1)}, bf16[528,128]{1,0:T(8,128)(2,1)S(1)}, u32[]{:S(2)}, u32[]{:S(2)}) collective-permute-start(bf16[528,128]{1,0:T(8,128)(2,1)S(1)} %get-tuple-element.25), channel_id=1, source_target_pairs={{0,10},{2,8},{4,14},{6,12},{8,2},{10,0},{12,6},{14,4},{1,11},{3,9}... | collective-permute-start | bytes 405512 | tf_op jit(solution)/shard_map/ppermute | solution.py:217
  9.2 3.6 %collective-permute-start.3 = (bf16[528,128]{1,0:T(8,128)(2,1)S(1)}, bf16[528,128]{1,0:T(8,128)(2,1)S(1)}, u32[]{:S(2)}, u32[]{:S(2)}) collective-permute-start(bf16[528,128]{1,0:T(8,128)(2,1)S(1)} %get-tuple-element.26), channel_id=1, source_target_pairs={{0,12},{2,14},{4,8},{6,10},{8,4},{10,6},{12,0},{14,2},{1,13},{3,15... | collective-permute-start | bytes 405512 | tf_op jit(solution)/shard_map/ppermute | solution.py:217
  12.8 0.0 collective-permute-start.4
  12.8 0.0 collective-permute-done.other
  12.8 0.0 collective-permute-start.5
  12.8 1.5 %shard_map.110 = (f32[256,512]{1,0:T(8,128)S(1)}, bf16[256,512]{1,0:T(8,128)(2,1)S(1)}, bf16[512,512]{1,0:T(8,128)(2,1)S(1)}, bf16[512,512]{1,0:T(8,128)(2,1)S(1)}) custom-call(bf16[13,256,512]{2,1,0:T(8,128)(2,1)S(1)} %copy-done, bf16[13,256,512]{2,1,0:T(8,128)(2,1)S(1)} %collective-permute-done.other, bf16[256,512]{1,0:T(8,128)(2,1)S(1)} %copy-done.1, ...), custom_call_target="tpu_custom_call" | custom-call | flops 500000000 | bytes 3000000 | tf_op jit(solution)/shard_map/pallas_call | solution.py:204
  14.3 9.7 %collective-permute-done.1.rest_0_ = bf16[528,128]{1,0:T(8,128)(2,1)S(1)} collective-permute-done((bf16[528,128]{1,0:T(8,128)(2,1)S(1)}, bf16[528,128]{1,0:T(8,128)(2,1)S(1)}, u32[]{:S(2)}, u32[]{:S(2)}) %collective-permute-start.1) | collective-permute-done | bytes 135200 | tf_op jit(solution)/shard_map/ppermute | solution.py:217
  24.0 1.7 %collective-permute-start.6 = (bf16[528,128]{1,0:T(8,128)(2,1)S(1)}, bf16[528,128]{1,0:T(8,128)(2,1)S(1)}, u32[]{:S(2)}, u32[]{:S(2)}) collective-permute-start(bf16[528,128]{1,0:T(8,128)(2,1)S(1)} %get-tuple-element.29), channel_id=1, source_target_pairs={{0,6},{2,4},{4,2},{6,0},{8,14},{10,12},{12,10},{14,8},{1,7},{3,5},... | collective-permute-start | bytes 405512 | tf_op jit(solution)/shard_map/ppermute | solution.py:217
  25.7 2.5 %collective-permute-done.2.rest_1_ = bf16[528,128]{1,0:T(8,128)(2,1)S(1)} collective-permute-done((bf16[528,128]{1,0:T(8,128)(2,1)S(1)}, bf16[528,128]{1,0:T(8,128)(2,1)S(1)}, u32[]{:S(2)}, u32[]{:S(2)}) %collective-permute-start.2) | collective-permute-done | bytes 135200 | tf_op jit(solution)/shard_map/ppermute | solution.py:217
  28.1 0.2 collective-permute-start.7
  28.4 1.6 %shard_map.111.total = f32[256,512]{1,0:T(8,128)S(1)} custom-call(f32[256,512]{1,0:T(8,128)S(1)} %get-tuple-element.20.total, bf16[256,512]{1,0:T(8,128)(2,1)S(1)} %get-tuple-element.21.part, bf16[512,512]{1,0:T(8,128)(2,1)S(1)} %get-tuple-element.22.first, bf16[512,512]{1,0:T(8,128)(2,1)S(1)} %get-tuple-element.23.third, f32[4,512]{1,0:T(4,128)S(1)} %copy-done.3, ...), custom_call_target="tpu_custom_call" | custom-call | flops 800000000 | bytes 2000000 | tf_op jit(solution)/shard_map/pallas_call | solution.py:204
  30.0 0.0 collective-permute-done.3.rest_0_
  30.0 0.0 collective-permute-done.5.rest_2_
  30.0 2.4 %shard_map.112.total = f32[256,512]{1,0:T(8,128)S(1)} custom-call(f32[256,512]{1,0:T(8,128)S(1)} %shard_map.111.total, bf16[256,512]{1,0:T(8,128)(2,1)S(1)} %get-tuple-element.21.part, bf16[512,512]{1,0:T(8,128)(2,1)S(1)} %get-tuple-element.22.first, bf16[512,512]{1,0:T(8,128)(2,1)S(1)} %get-tuple-element.23.third, f32[4,512]{1,0:T(4,128)S(1)} %copy-done.3, ...), custom_call_target="tpu_custom_call" | custom-call | flops 1200000000 | bytes 2000000 | tf_op jit(solution)/shard_map/pallas_call | solution.py:204
  32.5 0.0 collective-permute-done.6.rest_0_
  32.5 2.6 %collective-permute-done.7.rest_1_ = bf16[528,128]{1,0:T(8,128)(2,1)S(1)} collective-permute-done((bf16[528,128]{1,0:T(8,128)(2,1)S(1)}, bf16[528,128]{1,0:T(8,128)(2,1)S(1)}, u32[]{:S(2)}, u32[]{:S(2)}) %collective-permute-start.7) | collective-permute-done | bytes 135200 | tf_op jit(solution)/shard_map/ppermute | solution.py:217
  35.2 0.0 copy-start.6
  35.2 3.0 %shard_map.113 = (bf16[256,512]{1,0:T(8,128)(2,1)S(1)}, bf16[64,512]{1,0:T(8,128)(2,1)S(1)}) custom-call(f32[256,512]{1,0:T(8,128)S(1)} %shard_map.112.total, bf16[256,512]{1,0:T(8,128)(2,1)S(1)} %get-tuple-element.21.part, bf16[512,512]{1,0:T(8,128)(2,1)S(1)} %get-tuple-element.22.first, bf16[512,512]{1,0:T(8,128)(2,1)S(1)} %get-tuple-element.23.third, ...), custom_call_target="tpu_custom_call" | custom-call | flops 1000000000 | bytes 3000000 | tf_op jit(solution)/shard_map/pallas_call | solution.py:204
  38.1 0.5 collective-permute-start.10
  38.6 4.7 %collective-permute-start.9 = (bf16[64,512]{1,0:T(8,128)(2,1)S(1)}, bf16[64,512]{1,0:T(8,128)(2,1)S(1)}, u32[]{:S(2)}, u32[]{:S(2)}) collective-permute-start(bf16[64,512]{1,0:T(8,128)(2,1)S(1)} %get-tuple-element.32), channel_id=1, source_target_pairs={{0,12},{4,0},{8,4},{12,8},{1,13},{5,1},{9,5},{13,9},{2,14},{6,2},{... | collective-permute-start | bytes 196616 | tf_op jit(solution)/shard_map/ppermute | solution.py:222
  43.3 0.0 collective-permute-start.8
  43.3 1.8 %shard_map.114.pre = f32[512,512]{1,0:T(8,128)S(1)} custom-call(bf16[256,512]{1,0:T(8,128)(2,1)S(1)} %get-tuple-element.31.mid_ref, bf16[512,512]{1,0:T(8,128)(2,1)S(1)} %copy-done.2, s32[1,512]{1,0:T(1,128)S(1)} %bitcast.5, s32[1,512]{1,0:T(1,128)S(1)} %bitcast.7, f32[4,512]{1,0:T(4,128)S(1)} %copy-done.3, bf16[13,256,512]{2,1,0:T(8,128)(2,1)S(1)} %copy-done, ...), custom_call_target="tpu_custom_call" | custom-call | flops 1000000000 | bytes 3000000 | tf_op jit(solution)/shard_map/pallas_call | solution.py:204
  45.1 0.0 collective-permute-done.10.rest_2_
  45.1 0.1 collective-permute-done.9.rest_1_
  45.2 4.2 %collective-permute-done.8.rest_0_ = bf16[64,512]{1,0:T(8,128)(2,1)S(1)} collective-permute-done((bf16[64,512]{1,0:T(8,128)(2,1)S(1)}, bf16[64,512]{1,0:T(8,128)(2,1)S(1)}, u32[]{:S(2)}, u32[]{:S(2)}) %collective-permute-start.8) | collective-permute-done | bytes 65568 | tf_op jit(solution)/shard_map/ppermute | solution.py:222
  49.3 3.7 %shard_map.115 = bf16[256,512]{1,0:T(8,128)(2,1)} custom-call(f32[512,512]{1,0:T(8,128)S(1)} %shard_map.114.pre, bf16[256,512]{1,0:T(8,128)(2,1)S(1)} %get-tuple-element.31.mid_ref, s32[1,512]{1,0:T(1,128)S(1)} %bitcast.6, s32[1,512]{1,0:T(1,128)S(1)} %bitcast.8, f32[4,512]{1,0:T(4,128)S(1)} %copy-done.3, f32[4,512]{1,0:T(4,128)S(1)} %copy-done.4, ...), custom_call_target="tpu_custom_call" | custom-call | flops 1000000000 | bytes 3000000 | tf_op jit(solution)/shard_map/pallas_call | solution.py:204
  (19 shorter events, 0.0 us)
Async XLA Ops:
  0.0 12.8 %copy-start = (bf16[13,256,512]{2,1,0:T(8,128)(2,1)S(1)}, bf16[13,256,512]{2,1,0:T(8,128)(2,1)}, u32[]{:S(2)}) copy-start(bf16[13,256,512]{2,1,0:T(8,128)(2,1)} %mine.7) | copy-start | bytes 10223620
  0.0 12.8 %copy-start.3 = (f32[4,512]{1,0:T(4,128)S(1)}, f32[4,512]{1,0:T(4,128)}, u32[]{:S(2)}) copy-start(f32[4,512]{1,0:T(4,128)} %biases.11) | copy-start | bytes 24580
  0.0 12.8 %copy-start.1 = (bf16[256,512]{1,0:T(8,128)(2,1)S(1)}, bf16[256,512]{1,0:T(8,128)(2,1)}, u32[]{:S(2)}) copy-start(bf16[256,512]{1,0:T(8,128)(2,1)} %mesh.3) | copy-start | bytes 786436
  0.0 12.8 %collective-permute-start = (bf16[13,256,512]{2,1,0:T(8,128)(2,1)}, bf16[13,256,512]{2,1,0:T(8,128)(2,1)S(1)}, u32[]{:S(2)}, u32[]{:S(2)}) collective-permute-start(bf16[13,256,512]{2,1,0:T(8,128)(2,1)} %mine.7), channel_id=1, source_target_pairs={{0,1},{1,0},{2,3},{3,2},{4,5},{5,4},{6,7},{7,6},{8,9},{9,8},{10,11... | collective-permute-start | bytes 10223624 | tf_op jit(solution)/shard_map/ppermute | solution.py:217
  0.5 1.3 %copy-start.8 = (bf16[512,512]{1,0:T(8,128)(2,1)S(1)}, bf16[512,512]{1,0:T(8,128)(2,1)}, u32[]{:S(2)}) copy-start(bf16[512,512]{1,0:T(8,128)(2,1)} %latent_ref.1) | copy-start | bytes 1572868
  1.8 0.7 %copy-start.9 = (s32[512,2]{0,1:T(2,128)S(1)}, s32[512,2]{0,1:T(2,128)}, u32[]{:S(2)}) copy-start(s32[512,2]{0,1:T(2,128)} %param.13) | copy-start | bytes 12292
  2.5 0.7 %copy-start.10 = (s32[512,1]{0,1:T(1,128)S(1)}, s32[512,1]{0,1:T(1,128)}, u32[]{:S(2)}) copy-start(s32[512,1]{0,1:T(1,128)} %param.12) | copy-start | bytes 6148
  4.4 19.7 %collective-permute-start.1 = (bf16[528,128]{1,0:T(8,128)(2,1)S(1)}, bf16[528,128]{1,0:T(8,128)(2,1)S(1)}, u32[]{:S(2)}, u32[]{:S(2)}) collective-permute-start(bf16[528,128]{1,0:T(8,128)(2,1)S(1)} %get-tuple-element.24), channel_id=1, source_target_pairs={{0,8},{2,10},{4,12},{6,14},{8,0},{10,2},{12,4},{14,6},{1,9},{3,11}... | collective-permute-start | bytes 405512 | tf_op jit(solution)/shard_map/ppermute | solution.py:217
  7.9 20.2 %collective-permute-start.2 = (bf16[528,128]{1,0:T(8,128)(2,1)S(1)}, bf16[528,128]{1,0:T(8,128)(2,1)S(1)}, u32[]{:S(2)}, u32[]{:S(2)}) collective-permute-start(bf16[528,128]{1,0:T(8,128)(2,1)S(1)} %get-tuple-element.25), channel_id=1, source_target_pairs={{0,10},{2,8},{4,14},{6,12},{8,2},{10,0},{12,6},{14,4},{1,11},{3,9}... | collective-permute-start | bytes 405512 | tf_op jit(solution)/shard_map/ppermute | solution.py:217
  9.2 20.8 %collective-permute-start.3 = (bf16[528,128]{1,0:T(8,128)(2,1)S(1)}, bf16[528,128]{1,0:T(8,128)(2,1)S(1)}, u32[]{:S(2)}, u32[]{:S(2)}) collective-permute-start(bf16[528,128]{1,0:T(8,128)(2,1)S(1)} %get-tuple-element.26), channel_id=1, source_target_pairs={{0,12},{2,14},{4,8},{6,10},{8,4},{10,6},{12,0},{14,2},{1,13},{3,15... | collective-permute-start | bytes 405512 | tf_op jit(solution)/shard_map/ppermute | solution.py:217
  12.8 17.2 %collective-permute-start.4 = (bf16[528,128]{1,0:T(8,128)(2,1)S(1)}, bf16[528,128]{1,0:T(8,128)(2,1)S(1)}, u32[]{:S(2)}, u32[]{:S(2)}) collective-permute-start(bf16[528,128]{1,0:T(8,128)(2,1)S(1)} %get-tuple-element.27), channel_id=1, source_target_pairs={{0,14},{2,12},{4,10},{6,8},{8,6},{10,4},{12,2},{14,0},{1,15},{3,13... | collective-permute-start | bytes 405512 | tf_op jit(solution)/shard_map/ppermute | solution.py:217
  12.8 17.2 %collective-permute-start.5 = (bf16[528,128]{1,0:T(8,128)(2,1)S(1)}, bf16[528,128]{1,0:T(8,128)(2,1)S(1)}, u32[]{:S(2)}, u32[]{:S(2)}) collective-permute-start(bf16[528,128]{1,0:T(8,128)(2,1)S(1)} %get-tuple-element.28), channel_id=1, source_target_pairs={{0,4},{2,6},{4,0},{6,2},{8,12},{10,14},{12,8},{14,10},{1,5},{3,7},... | collective-permute-start | bytes 405512 | tf_op jit(solution)/shard_map/ppermute | solution.py:217
  24.0 8.5 %collective-permute-start.6 = (bf16[528,128]{1,0:T(8,128)(2,1)S(1)}, bf16[528,128]{1,0:T(8,128)(2,1)S(1)}, u32[]{:S(2)}, u32[]{:S(2)}) collective-permute-start(bf16[528,128]{1,0:T(8,128)(2,1)S(1)} %get-tuple-element.29), channel_id=1, source_target_pairs={{0,6},{2,4},{4,2},{6,0},{8,14},{10,12},{12,10},{14,8},{1,7},{3,5},... | collective-permute-start | bytes 405512 | tf_op jit(solution)/shard_map/ppermute | solution.py:217
  28.1 7.0 %collective-permute-start.7 = (bf16[528,128]{1,0:T(8,128)(2,1)S(1)}, bf16[528,128]{1,0:T(8,128)(2,1)S(1)}, u32[]{:S(2)}, u32[]{:S(2)}) collective-permute-start(bf16[528,128]{1,0:T(8,128)(2,1)S(1)} %get-tuple-element.30), channel_id=1, source_target_pairs={{0,2},{2,0},{4,6},{6,4},{8,10},{10,8},{12,14},{14,12},{1,3},{3,1},... | collective-permute-start | bytes 405512 | tf_op jit(solution)/shard_map/ppermute | solution.py:217
  28.4 6.8 %copy-start.4 = (f32[4,512]{1,0:T(4,128)S(1)}, f32[4,512]{1,0:T(4,128)}, u32[]{:S(2)}) copy-start(f32[4,512]{1,0:T(4,128)} %gains.3) | copy-start | bytes 24580
  28.4 6.8 %copy-start.7 = (s32[64]{0:T(128)S(1)}, s32[64]{0:T(128)}, u32[]{:S(2)}) copy-start(s32[64]{0:T(128)} %param.18) | copy-start | bytes 772
  35.1 8.1 %copy-start.2 = (bf16[512,512]{1,0:T(8,128)(2,1)S(1)}, bf16[512,512]{1,0:T(8,128)(2,1)}, u32[]{:S(2)}) copy-start(bf16[512,512]{1,0:T(8,128)(2,1)} %edges.1) | copy-start | bytes 1572868
  35.1 8.1 %copy-start.5 = (s32[512]{0:T(512)S(1)}, s32[512]{0:T(512)}, u32[]{:S(2)}) copy-start(s32[512]{0:T(512)} %param.16) | copy-start | bytes 6148
  35.2 8.1 %copy-start.6 = (s32[512]{0:T(512)S(1)}, s32[512]{0:T(512)}, u32[]{:S(2)}) copy-start(s32[512]{0:T(512)} %param.17) | copy-start | bytes 6148
  38.1 7.0 %collective-permute-start.10 = (bf16[64,512]{1,0:T(8,128)(2,1)S(1)}, bf16[64,512]{1,0:T(8,128)(2,1)S(1)}, u32[]{:S(2)}, u32[]{:S(2)}) collective-permute-start(bf16[64,512]{1,0:T(8,128)(2,1)S(1)} %get-tuple-element.32), channel_id=1, source_target_pairs={{0,2},{2,0},{1,3},{3,1},{4,6},{6,4},{5,7},{7,5},{8,10},{10,8},{9,1... | collective-permute-start | bytes 196616 | tf_op jit(solution)/shard_map/ppermute | solution.py:222
  38.6 6.6 %collective-permute-start.9 = (bf16[64,512]{1,0:T(8,128)(2,1)S(1)}, bf16[64,512]{1,0:T(8,128)(2,1)S(1)}, u32[]{:S(2)}, u32[]{:S(2)}) collective-permute-start(bf16[64,512]{1,0:T(8,128)(2,1)S(1)} %get-tuple-element.32), channel_id=1, source_target_pairs={{0,12},{4,0},{8,4},{12,8},{1,13},{5,1},{9,5},{13,9},{2,14},{6,2},{... | collective-permute-start | bytes 196616 | tf_op jit(solution)/shard_map/ppermute | solution.py:222
  43.3 6.1 %collective-permute-start.8 = (bf16[64,512]{1,0:T(8,128)(2,1)S(1)}, bf16[64,512]{1,0:T(8,128)(2,1)S(1)}, u32[]{:S(2)}, u32[]{:S(2)}) collective-permute-start(bf16[64,512]{1,0:T(8,128)(2,1)S(1)} %get-tuple-element.32), channel_id=1, source_target_pairs={{0,4},{4,8},{8,12},{12,0},{1,5},{5,9},{9,13},{13,1},{2,6},{6,10},{... | collective-permute-start | bytes 196616 | tf_op jit(solution)/shard_map/ppermute | solution.py:222

commit v2 on v1

v2 whole, which is shorter than its diff:
```python
import functools

import jax
import jax.numpy as jnp
from jax import lax
from jax.experimental import pallas as pl
from jax.experimental.pallas import tpu as pltpu
from jax.sharding import PartitionSpec as P

EPSILON = 1e-05
LANES = 128
AIM_ROWS = 16
F32 = jnp.float32
BF16 = jnp.bfloat16
HBM = pl.BlockSpec(memory_space=pltpu.HBM)
VMEM = pl.BlockSpec(memory_space=pltpu.VMEM)
VMEM_LIMIT = 24 * 1024 * 1024


def mm(left, right):
    return jnp.dot(left, right, preferred_element_type=F32)


def mm_nt(left, right):
    return lax.dot_general(left, right, (((1,), (1,)), ((), ())), preferred_element_type=F32)


def silu(values):
    half = 0.5 * values
    return (half + half * jnp.tanh(half)).astype(BF16)


def normed(values):
    middle = jnp.mean(values, axis=-1, keepdims=True)
    centred = values - middle
    spread = jnp.mean(centred * centred, axis=-1, keepdims=True)
    return centred * lax.rsqrt(spread + EPSILON)


def as_bf16(mask):
    return jnp.where(mask, 1.0, 0.0).astype(BF16)


def down(row, count):
    return as_bf16(lax.broadcasted_iota(jnp.int32, (count, row.shape[1]), 0) == row)


def along(column, count):
    return as_bf16(lax.broadcasted_iota(jnp.int32, (column.shape[0], count), 1) == column)


def turned(row):
    wide = jnp.broadcast_to(row.astype(F32), (8, row.shape[1]))
    return jnp.transpose(wide)[:, :1].astype(jnp.int32)


def halves(rows):
    half = rows.shape[1] // 2
    low, high = rows[:, :half], rows[:, half:]
    first = lax.axis_index("ch") == 0
    return jnp.where(first, low, high), jnp.where(first, high, low)


def through(rows, maps, pick):
    here, there = halves(rows)
    return mm(here, maps[0][pick]) + mm(there, maps[1][pick])


def dispatch_kernel(owners, capacity, exchange, owner_in, target_in, latent_in, *rest):
    *outs, owner_ref, target_ref, latent_ref, sems = rest
    rows, width = latent_ref.shape
    pairs = ((owner_in, owner_ref), (target_in, target_ref), (latent_in, latent_ref))
    copies = [pltpu.make_async_copy(*pair, sems.at[i]) for i, pair in enumerate(pairs)]
    for copy in copies:
        copy.start()
    padded = max(16, owners)
    number = lax.broadcasted_iota(jnp.int32, (padded, rows), 0)
    before = as_bf16(
        lax.broadcasted_iota(jnp.int32, (rows, rows), 0)
        < lax.broadcasted_iota(jnp.int32, (rows, rows), 1)
    )
    copies[0].wait()
    named = number == owner_ref[...]
    rank = mm(as_bf16(named), before).astype(jnp.int32)
    place = jnp.sum(jnp.where(named, number * capacity + rank, 0), axis=0, keepdims=True)
    copies[1].wait()
    aims = jnp.concatenate(
        [
            (target_ref[...] + 1).astype(F32),
            jnp.zeros((AIM_ROWS - target_ref.shape[0], rows), F32),
        ],
        axis=0,
    ).astype(BF16)
    copies[2].wait()
    latent = latent_ref[...]
    me = lax.axis_index("lat") * lax.axis_size("lon") + lax.axis_index("lon")
    for q, out in enumerate(outs):
        base = (me ^ q) * capacity if exchange else q * LANES
        pick = as_bf16(lax.broadcasted_iota(jnp.int32, (LANES, rows), 0) + base == place)
        data = mm(pick, latent).astype(BF16)
        for j in range(width // LANES):
            out[j * LANES : (j + 1) * LANES, :] = data[:, j * LANES : (j + 1) * LANES]
        out[width : width + AIM_ROWS, :] = mm_nt(aims, pick).astype(BF16)


def encode(chunks, maps, mesh_part, bias):
    nodes, width = mesh_part.shape
    total = None
    for chunk in chunks:
        rows = jnp.concatenate(
            [chunk[j * LANES : (j + 1) * LANES, :] for j in range(width // LANES)], axis=1
        )
        aims = chunk[width : width + AIM_ROWS, :].astype(F32)
        columns = jnp.transpose(aims).astype(jnp.int32) - 1
        lines = aims.astype(jnp.int32) - 1
        part = through(rows, maps, 0) + bias
        hidden = jnp.concatenate(
            [silu(part + mm(along(columns[:, k : k + 1], nodes), mesh_part)) for k in range(2)],
            axis=0,
        )
        notes = normed(through(hidden, maps, 2)).astype(BF16)
        spread = jnp.concatenate([down(lines[k : k + 1, :], nodes) for k in range(2)], axis=1)
        partial = mm(spread, notes)
        total = partial if total is None else total + partial
    return total


def first_kernel(mine, other, mesh, chunk, biases, sum_out, part_out):
    maps = (mine, other)
    part = through(mesh[...], maps, 1).astype(BF16)
    part_out[...] = part
    sum_out[...] = encode([chunk], maps, part, biases[0:1, :])


def more_kernel(total, part, mine, other, biases, *rest):
    *chunks, out = rest
    out[...] = total[...] + encode(chunks, (mine, other), part[...], biases[0:1, :])


def node_kernel(total, part, mine, other, biases, gains, mesh, lend, *rest):
    *chunks, mid_out, lent_out = rest
    maps = (mine, other)
    sums = total[...] + encode(chunks, maps, part[...], biases[0:1, :])
    encoded = (sums * gains[0:1, :]).astype(BF16)
    latent = mesh[...]
    hidden = silu(through(latent, maps, 3) + through(encoded, maps, 4) + biases[1:2, :])
    mid = (
        latent.astype(F32) + normed(through(hidden, maps, 5)) * gains[1:2, :]
    ).astype(BF16)
    mid_out[...] = mid
    picks = along(turned(lend[...]), mid.shape[0])
    lent_out[...] = mm(picks, mid).astype(BF16)


def local_kernel(mid_ref, edges, sender, receiver, biases, mine, other, pre_out):
    maps = (mine, other)
    mid = mid_ref[...]
    nodes = mid.shape[0]
    at_sender = along(turned(sender[...]), nodes)
    at_receiver = along(turned(receiver[...]), nodes)
    pre = through(edges[...], maps, 6) + biases[2:3, :]
    pre = pre + mm(at_sender, through(mid, maps, 7).astype(BF16))
    pre_out[...] = pre + mm(at_receiver, through(mid, maps, 8).astype(BF16))


def process_kernel(pre, mid_ref, sender, receiver, biases, gains, mine, other, *rest):
    *lent, out = rest
    maps = (mine, other)
    mid = mid_ref[...]
    nodes = mid.shape[0]
    table = jnp.concatenate([ref[...] for ref in lent], axis=0)
    depth = lent[0].shape[0]
    entry = sender[...] - nodes
    if len(lent) == 3:
        entry = jnp.where(entry >= 3 * depth, entry - depth, entry)
    from_halo = along(turned(entry), len(lent) * depth)
    hidden = silu(pre[...] + mm(from_halo, through(table, maps, 7).astype(BF16)))
    notes = normed(through(hidden, maps, 9)).astype(BF16)
    sums = mm(down(receiver[...], nodes), notes)
    processed = (sums * gains[2:3, :]).astype(BF16)
    hidden = silu(through(mid, maps, 10) + through(processed, maps, 11) + biases[3:4, :])
    out[...] = (
        mid.astype(F32) + normed(through(hidden, maps, 12)) * gains[3:4, :]
    ).astype(BF16)


def call(kernel, outs, ins, specs, scratch=(), flops=0, moved=0):
    return pl.pallas_call(
        kernel,
        out_shape=[jax.ShapeDtypeStruct(shape, kind) for shape, kind in outs],
        in_specs=specs,
        out_specs=[VMEM] * len(outs),
        scratch_shapes=list(scratch),
        compiler_params=pltpu.CompilerParams(vmem_limit_bytes=VMEM_LIMIT),
        cost_estimate=pl.CostEstimate(flops=flops, bytes_accessed=moved, transcendentals=0),
    )(*ins)


def swap(value, axes, step):
    count = lax.axis_size(axes)
    return lax.ppermute(value, axes, [(i, i ^ step) for i in range(count)])


def shift(value, axis, step):
    count = lax.axis_size(axis)
    return lax.ppermute(value, axis, [(i, (i + step) % count) for i in range(count)])


def sent_whole(chunks, owners, capacity, width):
    count = len(chunks)
    stack = jnp.stack(chunks)
    rows = stack[:, :width].reshape(count, width // LANES, LANES, LANES)
    rows = rows.transpose(0, 2, 1, 3).reshape(owners, capacity, width)
    aims = stack[:, width:].transpose(0, 2, 1).reshape(owners, capacity, AIM_ROWS)
    rows, aims = (
        lax.all_to_all(part, ("lat", "lon"), split_axis=0, concat_axis=0, tiled=True)
        for part in (rows, aims)
    )
    rows = rows.reshape(count, LANES, width // LANES, LANES).transpose(0, 2, 1, 3)
    aims = aims.reshape(count, LANES, AIM_ROWS).transpose(0, 2, 1)
    stack = jnp.concatenate([rows.reshape(count, width, LANES), aims], axis=1)
    return [stack[i] for i in range(count)]


def per_device(
    grid_latent,
    grid_owner,
    grid_target,
    mesh_latent,
    edge_latent,
    mesh_sender,
    mesh_receiver,
    halo_rows,
    weights,
    biases,
    gains,
):
    rows_dev, width = grid_latent.shape
    nodes = mesh_latent.shape[0]
    edges = edge_latent.shape[0]
    lon_count = lax.axis_size("lon")
    owners = lax.axis_size("lat") * lon_count
    capacity = max(2, 2 * rows_dev // owners)
    exchange = capacity == LANES and owners <= 16 and owners & (owners - 1) == 0

    other = swap(weights, "ch", 1)

    count = owners * capacity // LANES
    chunk_shape = ((width + AIM_ROWS, LANES), BF16)
    chunks = call(
        functools.partial(dispatch_kernel, owners, capacity, exchange),
        [chunk_shape] * count,
        [
            pltpu.with_memory_space_constraint(value, pltpu.HBM)
            for value in (grid_owner.T, grid_target.T, grid_latent)
        ],
        [HBM] * 3,
        [
            pltpu.VMEM((1, rows_dev), jnp.int32),
            pltpu.VMEM((2, rows_dev), jnp.int32),
            pltpu.VMEM((rows_dev, width), BF16),
            pltpu.SemaphoreType.DMA((3,)),
        ],
        flops=10**9,
        moved=2 * 10**6,
    )
    if exchange:
        arrived = {0: chunks[0]}
        for step in [1, 4, 5, 6, 7, 2, 3] if owners == 8 else range(1, owners):
            arrived[step] = swap(chunks[step], ("lat", "lon"), step)
        groups = [[0], [1, 2], [4, 3, 5], [6, 7]] if owners == 8 else [[0], list(range(1, owners))]
    else:
        arrived = dict(enumerate(sent_whole(chunks, owners, capacity, width)))
        groups = [[0], list(range(1, count))]

    total, part = call(
        first_kernel,
        [((nodes, width), F32), ((nodes, width), BF16)],
        (weights, other, mesh_latent, arrived[0], biases),
        [VMEM] * 5,
        flops=5 * 10**8,
        moved=3 * 10**6,
    )
    for group in groups[1:-1]:
        (total,) = call(
            more_kernel,
            [((nodes, width), F32)],
            (total, part, weights, other, biases, *[arrived[i] for i in group]),
            [VMEM] * (5 + len(group)),
            flops=4 * 10**8 * len(group),
            moved=2 * 10**6,
        )
    mid, lent = call(
        node_kernel,
        [((nodes, width), BF16), ((halo_rows.shape[0], width), BF16)],
        (total, part, weights, other, biases, gains, mesh_latent)
        + (halo_rows.reshape(1, -1), *[arrived[i] for i in groups[-1]]),
        [VMEM] * (8 + len(groups[-1])),
        flops=10**9,
        moved=3 * 10**6,
    )
    halo = [shift(lent, "lat", 1), shift(lent, "lat", -1), shift(lent, "lon", 1)]
    if lon_count != 2:
        halo.append(shift(lent, "lon", -1))
    sender, receiver = mesh_sender.reshape(1, -1), mesh_receiver.reshape(1, -1)
    (pre,) = call(
        local_kernel,
        [((edges, width), F32)],
        (mid, edge_latent, sender, receiver, biases, weights, other),
        [VMEM] * 7,
        flops=10**9,
        moved=3 * 10**6,
    )
    (out,) = call(
        process_kernel,
        [((nodes, width), BF16)],
        (pre, mid, sender, receiver, biases, gains, weights, other, *halo),
        [VMEM] * (8 + len(halo)),
        flops=10**9,
        moved=3 * 10**6,
    )
    return out


def solution(mesh):
    in_specs = (
        P(("member", "lat", "lon", "ch"), None),
        P(("member", "lat", "lon", "ch"), None),
        P(("member", "lat", "lon", "ch"), None),
        P(("member", "lat", "lon", "ch"), None),
        P(("member", "lat", "lon", "ch"), None),
        P(("member", "lat", "lon", "ch")),
        P(("member", "lat", "lon", "ch")),
        P(("member", "lat", "lon", "ch")),
        P(None, "ch", None),
        P(),
        P(),
    )
    out_specs = P(("member", "lat", "lon", "ch"), None)
    return jax.shard_map(
        per_device, mesh=mesh, in_specs=in_specs, out_specs=out_specs, check_vma=False
    )
```

time: 53.2 us -> 47.1 us (0.89)
  waiting for transfers between devices: 19 us -> 13.6 us
  starting transfers between devices: 16 us -> 18.8 us
  local copies, waits for them, and re-layouts: 2.7 us -> 0.04 us
  Pallas kernels: 15.2 us -> 14.3 us
    ppermute x8, waiting for transfers between devices: 14.8 us -> 9.47 us  [swap(): return lax.ppermute(value, axes, [(i, i ^ step) for i in range(count)])]
    unnamed x22 -> x16, local copies, waits for them, and re-layouts: 2.7 us -> 0.04 us
    ppermute x8, starting transfers between devices: 10.8 us -> 13.4 us  [swap(): return lax.ppermute(value, axes, [(i, i ^ step) for i in range(count)])]
    pallas_call x7, Pallas kernels: 15.2 us -> 14.3 us  [call(): pl.pallas_call(kernel, out_shape=[jax.ShapeDtypeStruct(shape, kind) for s...]
  transfers between devices with their start and end apart: 11 -> 11, of which waited for: 5 -> 4; matrix products, arithmetic and copies ran while one was open for 0% -> 0% of each run, Pallas kernels for 16% -> 19%
where the time goes in v2:
time: 47.1 us; the launch traced here: 46.9 us
  starting transfers between devices  18.8 us (40%)
  Pallas kernels  14.3 us (30%)
  waiting for transfers between devices  13.6 us (29%)
    pallas_call x7, Pallas kernels, call(): pl.pallas_call(kernel, out_shape=[jax.ShapeDtypeStruct(shape, kind) for s...  14.3 us
    ppermute x8, starting transfers between devices, swap(): return lax.ppermute(value, axes, [(i, i ^ step) for i in range(count)])  13.4 us
    ppermute x8, waiting for transfers between devices, swap(): return lax.ppermute(value, axes, [(i, i ^ step) for i in range(count)])  9.47 us
    ppermute x3, starting transfers between devices, shift(): lax.ppermute(value, axis, [(i, (i + step) % count) for i in range(count)])  5.38 us
    ppermute x3, waiting for transfers between devices, shift(): lax.ppermute(value, axis, [(i, (i + step) % count) for i in range(count)])  4.13 us
  transfers between devices with their start and end apart: 11, of which 4 were waited for; matrix products, arithmetic and copies ran while one was open for 0% of the time, Pallas kernels for 19%

profile of v2, /device:TPU:0, one launch (start us, length us, event | category | flops | bytes accessed | tf_op | source)
XLA Modules:
  0.0 46.9 jit_solution(16835239758813914065)
XLA Ops:
  0.0 0.5 %collective-permute-start = (bf16[13,256,512]{2,1,0:T(8,128)(2,1)}, bf16[13,256,512]{2,1,0:T(8,128)(2,1)S(1)}, u32[]{:S(2)}, u32[]{:S(2)}) collective-permute-start(bf16[13,256,512]{2,1,0:T(8,128)(2,1)} %mine.11), channel_id=1, source_target_pairs={{0,1},{1,0},{2,3},{3,2},{4,5},{5,4},{6,7},{7,6},{8,9},{9,8},{10,11... | collective-permute-start | bytes 10223624 | tf_op jit(solution)/shard_map/ppermute | solution.py:201
  0.5 2.4 %shard_map.109 = (bf16[528,128]{1,0:T(8,128)(2,1)S(1)}, bf16[528,128]{1,0:T(8,128)(2,1)S(1)}, bf16[528,128]{1,0:T(8,128)(2,1)S(1)}, bf16[528,128]{1,0:T(8,128)(2...) custom-call(s32[1,512]{1,0:T(1,128)} %bitcast.11, ...), custom_call_target="tpu_custom_call" | custom-call | flops 1000000000 | bytes 2000000 | tf_op jit(solution)/shard_map/pallas_call | solution.py:188
  2.9 2.5 %collective-permute-start.1 = (bf16[528,128]{1,0:T(8,128)(2,1)S(1)}, bf16[528,128]{1,0:T(8,128)(2,1)S(1)}, u32[]{:S(2)}, u32[]{:S(2)}) collective-permute-start(bf16[528,128]{1,0:T(8,128)(2,1)S(1)} %get-tuple-element.20), channel_id=1, source_target_pairs={{0,2},{2,0},{4,6},{6,4},{8,10},{10,8},{12,14},{14,12},{1,3},{3,1},... | collective-permute-start | bytes 405512 | tf_op jit(solution)/shard_map/ppermute | solution.py:201
  5.4 1.6 %collective-permute-start.2 = (bf16[528,128]{1,0:T(8,128)(2,1)S(1)}, bf16[528,128]{1,0:T(8,128)(2,1)S(1)}, u32[]{:S(2)}, u32[]{:S(2)}) collective-permute-start(bf16[528,128]{1,0:T(8,128)(2,1)S(1)} %get-tuple-element.21), channel_id=1, source_target_pairs={{0,4},{2,6},{4,0},{6,2},{8,12},{10,14},{12,8},{14,10},{1,5},{3,7},... | collective-permute-start | bytes 405512 | tf_op jit(solution)/shard_map/ppermute | solution.py:201
  6.9 2.6 %collective-permute-start.3 = (bf16[528,128]{1,0:T(8,128)(2,1)S(1)}, bf16[528,128]{1,0:T(8,128)(2,1)S(1)}, u32[]{:S(2)}, u32[]{:S(2)}) collective-permute-start(bf16[528,128]{1,0:T(8,128)(2,1)S(1)} %get-tuple-element.22), channel_id=1, source_target_pairs={{0,8},{2,10},{4,12},{6,14},{8,0},{10,2},{12,4},{14,6},{1,9},{3,11}... | collective-permute-start | bytes 405512 | tf_op jit(solution)/shard_map/ppermute | solution.py:201
  9.5 0.4 collective-permute-start.4
  10.0 0.0 collective-permute-done.other
  10.0 1.3 %collective-permute-start.5 = (bf16[528,128]{1,0:T(8,128)(2,1)S(1)}, bf16[528,128]{1,0:T(8,128)(2,1)S(1)}, u32[]{:S(2)}, u32[]{:S(2)}) collective-permute-start(bf16[528,128]{1,0:T(8,128)(2,1)S(1)} %get-tuple-element.24), channel_id=1, source_target_pairs={{0,10},{2,8},{4,14},{6,12},{8,2},{10,0},{12,6},{14,4},{1,11},{3,9}... | collective-permute-start | bytes 405512 | tf_op jit(solution)/shard_map/ppermute | solution.py:201
  11.3 1.1 %shard_map.110 = (f32[256,512]{1,0:T(8,128)S(1)}, bf16[256,512]{1,0:T(8,128)(2,1)S(1)}) custom-call(bf16[13,256,512]{2,1,0:T(8,128)(2,1)S(1)} %copy-done, bf16[13,256,512]{2,1,0:T(8,128)(2,1)S(1)} %collective-permute-done.other, bf16[256,512]{1,0:T(8,128)(2,1)S(1)} %copy-done.1, bf16[528,128]{1,0:T(8,128)(2,1)S(1)} %get-tuple-element.17.chunk, ...), custom_call_target="tpu_custom_call" | custom-call | flops 500000000 | bytes 3000000 | tf_op jit(solution)/shard_map/pallas_call | solution.py:188
  12.4 0.0 collective-permute-done.1.rest_0_
  12.5 3.6 %collective-permute-start.6 = (bf16[528,128]{1,0:T(8,128)(2,1)S(1)}, bf16[528,128]{1,0:T(8,128)(2,1)S(1)}, u32[]{:S(2)}, u32[]{:S(2)}) collective-permute-start(bf16[528,128]{1,0:T(8,128)(2,1)S(1)} %get-tuple-element.25), channel_id=1, source_target_pairs={{0,12},{2,14},{4,8},{6,10},{8,4},{10,6},{12,0},{14,2},{1,13},{3,15... | collective-permute-start | bytes 405512 | tf_op jit(solution)/shard_map/ppermute | solution.py:201
  16.1 0.0 collective-permute-done.2.rest_1_
  16.1 0.9 %collective-permute-start.7 = (bf16[528,128]{1,0:T(8,128)(2,1)S(1)}, bf16[528,128]{1,0:T(8,128)(2,1)S(1)}, u32[]{:S(2)}, u32[]{:S(2)}) collective-permute-start(bf16[528,128]{1,0:T(8,128)(2,1)S(1)} %get-tuple-element.26), channel_id=1, source_target_pairs={{0,14},{2,12},{4,10},{6,8},{8,6},{10,4},{12,2},{14,0},{1,15},{3,13... | collective-permute-start | bytes 405512 | tf_op jit(solution)/shard_map/ppermute | solution.py:201
  17.0 1.6 %shard_map.111.total = f32[256,512]{1,0:T(8,128)S(1)} custom-call(f32[256,512]{1,0:T(8,128)S(1)} %get-tuple-element.18.total, bf16[256,512]{1,0:T(8,128)(2,1)S(1)} %get-tuple-element.19.part, bf16[13,256,512]{2,1,0:T(8,128)(2,1)S(1)} %copy-done, bf16[13,256,512]{2,1,0:T(8,128)(2,1)S(1)} %collective-permute-done.other, f32[4,512]{1,0:T(4,128)S(1)} %copy-done.3, ...), custom_call_target="tpu_custom_call" | custom-call | flops 800000000 | bytes 2000000 | tf_op jit(solution)/shard_map/pallas_call | solution.py:188
  18.6 0.0 copy-start.4
  18.6 0.0 copy-start.7
  18.6 0.9 %collective-permute-done.4.rest_1_ = bf16[528,128]{1,0:T(8,128)(2,1)S(1)} collective-permute-done((bf16[528,128]{1,0:T(8,128)(2,1)S(1)}, bf16[528,128]{1,0:T(8,128)(2,1)S(1)}, u32[]{:S(2)}, u32[]{:S(2)}) %collective-permute-start.4) | collective-permute-done | bytes 135200 | tf_op jit(solution)/shard_map/ppermute | solution.py:201
  19.5 8.6 %collective-permute-done.5.rest_2_ = bf16[528,128]{1,0:T(8,128)(2,1)S(1)} collective-permute-done((bf16[528,128]{1,0:T(8,128)(2,1)S(1)}, bf16[528,128]{1,0:T(8,128)(2,1)S(1)}, u32[]{:S(2)}, u32[]{:S(2)}) %collective-permute-start.5) | collective-permute-done | bytes 135200 | tf_op jit(solution)/shard_map/ppermute | solution.py:201
  28.1 2.4 %shard_map.112.total = f32[256,512]{1,0:T(8,128)S(1)} custom-call(f32[256,512]{1,0:T(8,128)S(1)} %shard_map.111.total, bf16[256,512]{1,0:T(8,128)(2,1)S(1)} %get-tuple-element.19.part, bf16[13,256,512]{2,1,0:T(8,128)(2,1)S(1)} %copy-done, bf16[13,256,512]{2,1,0:T(8,128)(2,1)S(1)} %collective-permute-done.other, f32[4,512]{1,0:T(4,128)S(1)} %copy-done.3, ...), custom_call_target="tpu_custom_call" | custom-call | flops 1200000000 | bytes 2000000 | tf_op jit(solution)/shard_map/pallas_call | solution.py:188
  30.5 0.0 collective-permute-done.7.rest_1_
  30.6 0.0 copy-start.2
  30.6 0.0 copy-start.5
  30.6 0.0 copy-start.6
  30.6 2.6 %shard_map.113 = (bf16[256,512]{1,0:T(8,128)(2,1)S(1)}, bf16[64,512]{1,0:T(8,128)(2,1)S(1)}) custom-call(f32[256,512]{1,0:T(8,128)S(1)} %shard_map.112.total, bf16[256,512]{1,0:T(8,128)(2,1)S(1)} %get-tuple-element.19.part, bf16[13,256,512]{2,1,0:T(8,128)(2,1)S(1)} %copy-done, bf16[13,256,512]{2,1,0:T(8,128)(2,1)S(1)} %collective-permute-done.other, ...), custom_call_target="tpu_custom_call" | custom-call | flops 1000000000 | bytes 3000000 | tf_op jit(solution)/shard_map/pallas_call | solution.py:188
  33.2 1.6 %collective-permute-start.10 = (bf16[64,512]{1,0:T(8,128)(2,1)S(1)}, bf16[64,512]{1,0:T(8,128)(2,1)S(1)}, u32[]{:S(2)}, u32[]{:S(2)}) collective-permute-start(bf16[64,512]{1,0:T(8,128)(2,1)S(1)} %get-tuple-element.28), channel_id=1, source_target_pairs={{0,2},{2,0},{1,3},{3,1},{4,6},{6,4},{5,7},{7,5},{8,10},{10,8},{9,1... | collective-permute-start | bytes 196616 | tf_op jit(solution)/shard_map/ppermute | solution.py:206
  34.8 3.2 %collective-permute-start.9 = (bf16[64,512]{1,0:T(8,128)(2,1)S(1)}, bf16[64,512]{1,0:T(8,128)(2,1)S(1)}, u32[]{:S(2)}, u32[]{:S(2)}) collective-permute-start(bf16[64,512]{1,0:T(8,128)(2,1)S(1)} %get-tuple-element.28), channel_id=1, source_target_pairs={{0,12},{4,0},{8,4},{12,8},{1,13},{5,1},{9,5},{13,9},{2,14},{6,2},{... | collective-permute-start | bytes 196616 | tf_op jit(solution)/shard_map/ppermute | solution.py:206
  38.0 0.6 %collective-permute-start.8 = (bf16[64,512]{1,0:T(8,128)(2,1)S(1)}, bf16[64,512]{1,0:T(8,128)(2,1)S(1)}, u32[]{:S(2)}, u32[]{:S(2)}) collective-permute-start(bf16[64,512]{1,0:T(8,128)(2,1)S(1)} %get-tuple-element.28), channel_id=1, source_target_pairs={{0,4},{4,8},{8,12},{12,0},{1,5},{5,9},{9,13},{13,1},{2,6},{6,10},{... | collective-permute-start | bytes 196616 | tf_op jit(solution)/shard_map/ppermute | solution.py:206
  38.6 1.3 %shard_map.114.pre = f32[512,512]{1,0:T(8,128)S(1)} custom-call(bf16[256,512]{1,0:T(8,128)(2,1)S(1)} %get-tuple-element.27.mid_ref, bf16[512,512]{1,0:T(8,128)(2,1)S(1)} %copy-done.2, s32[1,512]{1,0:T(1,128)S(1)} %bitcast.5, s32[1,512]{1,0:T(1,128)S(1)} %bitcast.7, f32[4,512]{1,0:T(4,128)S(1)} %copy-done.3, bf16[13,256,512]{2,1,0:T(8,128)(2,1)S(1)} %copy-done, ...), custom_call_target="tpu_custom_call" | custom-call | flops 1000000000 | bytes 3000000 | tf_op jit(solution)/shard_map/pallas_call | solution.py:188
  39.9 0.0 collective-permute-done.10.rest_2_
  39.9 0.9 %collective-permute-done.9.rest_1_ = bf16[64,512]{1,0:T(8,128)(2,1)S(1)} collective-permute-done((bf16[64,512]{1,0:T(8,128)(2,1)S(1)}, bf16[64,512]{1,0:T(8,128)(2,1)S(1)}, u32[]{:S(2)}, u32[]{:S(2)}) %collective-permute-start.9) | collective-permute-done | bytes 65568 | tf_op jit(solution)/shard_map/ppermute | solution.py:206
  40.8 3.2 %collective-permute-done.8.rest_0_ = bf16[64,512]{1,0:T(8,128)(2,1)S(1)} collective-permute-done((bf16[64,512]{1,0:T(8,128)(2,1)S(1)}, bf16[64,512]{1,0:T(8,128)(2,1)S(1)}, u32[]{:S(2)}, u32[]{:S(2)}) %collective-permute-start.8) | collective-permute-done | bytes 65568 | tf_op jit(solution)/shard_map/ppermute | solution.py:206
  44.0 2.9 %shard_map.115 = bf16[256,512]{1,0:T(8,128)(2,1)} custom-call(f32[512,512]{1,0:T(8,128)S(1)} %shard_map.114.pre, bf16[256,512]{1,0:T(8,128)(2,1)S(1)} %get-tuple-element.27.mid_ref, s32[1,512]{1,0:T(1,128)S(1)} %bitcast.6, s32[1,512]{1,0:T(1,128)S(1)} %bitcast.8, f32[4,512]{1,0:T(4,128)S(1)} %copy-done.3, f32[4,512]{1,0:T(4,128)S(1)} %copy-done.4, ...), custom_call_target="tpu_custom_call" | custom-call | flops 1000000000 | bytes 3000000 | tf_op jit(solution)/shard_map/pallas_call | solution.py:188
  (13 shorter events, 0.0 us)
Async XLA Ops:
  0.0 11.3 %copy-start = (bf16[13,256,512]{2,1,0:T(8,128)(2,1)S(1)}, bf16[13,256,512]{2,1,0:T(8,128)(2,1)}, u32[]{:S(2)}) copy-start(bf16[13,256,512]{2,1,0:T(8,128)(2,1)} %mine.11) | copy-start | bytes 10223620
  0.0 11.3 %copy-start.3 = (f32[4,512]{1,0:T(4,128)S(1)}, f32[4,512]{1,0:T(4,128)}, u32[]{:S(2)}) copy-start(f32[4,512]{1,0:T(4,128)} %biases.11) | copy-start | bytes 24580
  0.0 11.3 %copy-start.1 = (bf16[256,512]{1,0:T(8,128)(2,1)S(1)}, bf16[256,512]{1,0:T(8,128)(2,1)}, u32[]{:S(2)}) copy-start(bf16[256,512]{1,0:T(8,128)(2,1)} %mesh.3) | copy-start | bytes 786436
  0.0 10.0 %collective-permute-start = (bf16[13,256,512]{2,1,0:T(8,128)(2,1)}, bf16[13,256,512]{2,1,0:T(8,128)(2,1)S(1)}, u32[]{:S(2)}, u32[]{:S(2)}) collective-permute-start(bf16[13,256,512]{2,1,0:T(8,128)(2,1)} %mine.11), channel_id=1, source_target_pairs={{0,1},{1,0},{2,3},{3,2},{4,5},{5,4},{6,7},{7,6},{8,9},{9,8},{10,11... | collective-permute-start | bytes 10223624 | tf_op jit(solution)/shard_map/ppermute | solution.py:201
  2.9 9.5 %collective-permute-start.1 = (bf16[528,128]{1,0:T(8,128)(2,1)S(1)}, bf16[528,128]{1,0:T(8,128)(2,1)S(1)}, u32[]{:S(2)}, u32[]{:S(2)}) collective-permute-start(bf16[528,128]{1,0:T(8,128)(2,1)S(1)} %get-tuple-element.20), channel_id=1, source_target_pairs={{0,2},{2,0},{4,6},{6,4},{8,10},{10,8},{12,14},{14,12},{1,3},{3,1},... | collective-permute-start | bytes 405512 | tf_op jit(solution)/shard_map/ppermute | solution.py:201
  5.4 10.7 %collective-permute-start.2 = (bf16[528,128]{1,0:T(8,128)(2,1)S(1)}, bf16[528,128]{1,0:T(8,128)(2,1)S(1)}, u32[]{:S(2)}, u32[]{:S(2)}) collective-permute-start(bf16[528,128]{1,0:T(8,128)(2,1)S(1)} %get-tuple-element.21), channel_id=1, source_target_pairs={{0,4},{2,6},{4,0},{6,2},{8,12},{10,14},{12,8},{14,10},{1,5},{3,7},... | collective-permute-start | bytes 405512 | tf_op jit(solution)/shard_map/ppermute | solution.py:201
  6.9 11.7 %collective-permute-start.3 = (bf16[528,128]{1,0:T(8,128)(2,1)S(1)}, bf16[528,128]{1,0:T(8,128)(2,1)S(1)}, u32[]{:S(2)}, u32[]{:S(2)}) collective-permute-start(bf16[528,128]{1,0:T(8,128)(2,1)S(1)} %get-tuple-element.22), channel_id=1, source_target_pairs={{0,8},{2,10},{4,12},{6,14},{8,0},{10,2},{12,4},{14,6},{1,9},{3,11}... | collective-permute-start | bytes 405512 | tf_op jit(solution)/shard_map/ppermute | solution.py:201
  9.5 10.0 %collective-permute-start.4 = (bf16[528,128]{1,0:T(8,128)(2,1)S(1)}, bf16[528,128]{1,0:T(8,128)(2,1)S(1)}, u32[]{:S(2)}, u32[]{:S(2)}) collective-permute-start(bf16[528,128]{1,0:T(8,128)(2,1)S(1)} %get-tuple-element.23), channel_id=1, source_target_pairs={{0,6},{2,4},{4,2},{6,0},{8,14},{10,12},{12,10},{14,8},{1,7},{3,5},... | collective-permute-start | bytes 405512 | tf_op jit(solution)/shard_map/ppermute | solution.py:201
  10.0 18.1 %collective-permute-start.5 = (bf16[528,128]{1,0:T(8,128)(2,1)S(1)}, bf16[528,128]{1,0:T(8,128)(2,1)S(1)}, u32[]{:S(2)}, u32[]{:S(2)}) collective-permute-start(bf16[528,128]{1,0:T(8,128)(2,1)S(1)} %get-tuple-element.24), channel_id=1, source_target_pairs={{0,10},{2,8},{4,14},{6,12},{8,2},{10,0},{12,6},{14,4},{1,11},{3,9}... | collective-permute-start | bytes 405512 | tf_op jit(solution)/shard_map/ppermute | solution.py:201
  12.5 18.1 %collective-permute-start.6 = (bf16[528,128]{1,0:T(8,128)(2,1)S(1)}, bf16[528,128]{1,0:T(8,128)(2,1)S(1)}, u32[]{:S(2)}, u32[]{:S(2)}) collective-permute-start(bf16[528,128]{1,0:T(8,128)(2,1)S(1)} %get-tuple-element.25), channel_id=1, source_target_pairs={{0,12},{2,14},{4,8},{6,10},{8,4},{10,6},{12,0},{14,2},{1,13},{3,15... | collective-permute-start | bytes 405512 | tf_op jit(solution)/shard_map/ppermute | solution.py:201
  16.1 14.5 %collective-permute-start.7 = (bf16[528,128]{1,0:T(8,128)(2,1)S(1)}, bf16[528,128]{1,0:T(8,128)(2,1)S(1)}, u32[]{:S(2)}, u32[]{:S(2)}) collective-permute-start(bf16[528,128]{1,0:T(8,128)(2,1)S(1)} %get-tuple-element.26), channel_id=1, source_target_pairs={{0,14},{2,12},{4,10},{6,8},{8,6},{10,4},{12,2},{14,0},{1,15},{3,13... | collective-permute-start | bytes 405512 | tf_op jit(solution)/shard_map/ppermute | solution.py:201
  18.6 12.0 %copy-start.4 = (f32[4,512]{1,0:T(4,128)S(1)}, f32[4,512]{1,0:T(4,128)}, u32[]{:S(2)}) copy-start(f32[4,512]{1,0:T(4,128)} %gains.3) | copy-start | bytes 24580
  18.6 11.9 %copy-start.7 = (s32[64]{0:T(128)S(1)}, s32[64]{0:T(128)}, u32[]{:S(2)}) copy-start(s32[64]{0:T(128)} %param.18) | copy-start | bytes 772
  30.6 8.0 %copy-start.2 = (bf16[512,512]{1,0:T(8,128)(2,1)S(1)}, bf16[512,512]{1,0:T(8,128)(2,1)}, u32[]{:S(2)}) copy-start(bf16[512,512]{1,0:T(8,128)(2,1)} %edges.1) | copy-start | bytes 1572868
  30.6 8.0 %copy-start.5 = (s32[512]{0:T(512)S(1)}, s32[512]{0:T(512)}, u32[]{:S(2)}) copy-start(s32[512]{0:T(512)} %param.16) | copy-start | bytes 6148
  30.6 8.0 %copy-start.6 = (s32[512]{0:T(512)S(1)}, s32[512]{0:T(512)}, u32[]{:S(2)}) copy-start(s32[512]{0:T(512)} %param.17) | copy-start | bytes 6148
  33.2 6.7 %collective-permute-start.10 = (bf16[64,512]{1,0:T(8,128)(2,1)S(1)}, bf16[64,512]{1,0:T(8,128)(2,1)S(1)}, u32[]{:S(2)}, u32[]{:S(2)}) collective-permute-start(bf16[64,512]{1,0:T(8,128)(2,1)S(1)} %get-tuple-element.28), channel_id=1, source_target_pairs={{0,2},{2,0},{1,3},{3,1},{4,6},{6,4},{5,7},{7,5},{8,10},{10,8},{9,1... | collective-permute-start | bytes 196616 | tf_op jit(solution)/shard_map/ppermute | solution.py:206
  34.8 6.0 %collective-permute-start.9 = (bf16[64,512]{1,0:T(8,128)(2,1)S(1)}, bf16[64,512]{1,0:T(8,128)(2,1)S(1)}, u32[]{:S(2)}, u32[]{:S(2)}) collective-permute-start(bf16[64,512]{1,0:T(8,128)(2,1)S(1)} %get-tuple-element.28), channel_id=1, source_target_pairs={{0,12},{4,0},{8,4},{12,8},{1,13},{5,1},{9,5},{13,9},{2,14},{6,2},{... | collective-permute-start | bytes 196616 | tf_op jit(solution)/shard_map/ppermute | solution.py:206
  38.0 6.1 %collective-permute-start.8 = (bf16[64,512]{1,0:T(8,128)(2,1)S(1)}, bf16[64,512]{1,0:T(8,128)(2,1)S(1)}, u32[]{:S(2)}, u32[]{:S(2)}) collective-permute-start(bf16[64,512]{1,0:T(8,128)(2,1)S(1)} %get-tuple-element.28), channel_id=1, source_target_pairs={{0,4},{4,8},{8,12},{12,0},{1,5},{5,9},{9,13},{13,1},{2,6},{6,10},{... | collective-permute-start | bytes 196616 | tf_op jit(solution)/shard_map/ppermute | solution.py:206

commit v3 on v2

--- a/solution.py
+++ b/solution.py
@@ -66,15 +66,32 @@
     return mm(here, maps[0][pick]) + mm(there, maps[1][pick])
 
 
-def dispatch_kernel(owners, capacity, exchange, owner_in, target_in, latent_in, *rest):
-    *outs, owner_ref, target_ref, latent_ref, sems = rest
+def packed(place, aims, latent, base, out):
+    rows, width = latent.shape
+    pick = as_bf16(lax.broadcasted_iota(jnp.int32, (LANES, rows), 0) + base == place)
+    data = mm(pick, latent).astype(BF16)
+    for j in range(width // LANES):
+        out[j * LANES : (j + 1) * LANES, :] = data[:, j * LANES : (j + 1) * LANES]
+    out[width : width + AIM_ROWS, :] = mm_nt(aims, pick).astype(BF16)
+
+
+def base_of(step, capacity, exchange):
+    if not exchange:
+        return step * LANES
+    lats, lons = lax.axis_size("lat"), lax.axis_size("lon")
+    lat, lon = lax.axis_index("lat"), lax.axis_index("lon")
+    owner = lax.rem(lat + step // lons, lats) * lons + lax.rem(lon + step % lons, lons)
+    return owner * capacity
+
+
+def place_kernel(owners, capacity, exchange, step, owner_in, target_in, latent_in, *rest):
+    out, place_out, aims_out, owner_ref, target_ref, latent_ref, sems = rest
     rows, width = latent_ref.shape
     pairs = ((owner_in, owner_ref), (target_in, target_ref), (latent_in, latent_ref))
     copies = [pltpu.make_async_copy(*pair, sems.at[i]) for i, pair in enumerate(pairs)]
     for copy in copies:
         copy.start()
-    padded = max(16, owners)
-    number = lax.broadcasted_iota(jnp.int32, (padded, rows), 0)
+    number = lax.broadcasted_iota(jnp.int32, (max(16, owners), rows), 0)
     before = as_bf16(
         lax.broadcasted_iota(jnp.int32, (rows, rows), 0)
         < lax.broadcasted_iota(jnp.int32, (rows, rows), 1)
@@ -91,44 +108,49 @@
         ],
         axis=0,
     ).astype(BF16)
+    place_out[...] = place
+    aims_out[...] = aims
     copies[2].wait()
-    latent = latent_ref[...]
-    me = lax.axis_index("lat") * lax.axis_size("lon") + lax.axis_index("lon")
-    for q, out in enumerate(outs):
-        base = (me ^ q) * capacity if exchange else q * LANES
-        pick = as_bf16(lax.broadcasted_iota(jnp.int32, (LANES, rows), 0) + base == place)
-        data = mm(pick, latent).astype(BF16)
-        for j in range(width // LANES):
-            out[j * LANES : (j + 1) * LANES, :] = data[:, j * LANES : (j + 1) * LANES]
-        out[width : width + AIM_ROWS, :] = mm_nt(aims, pick).astype(BF16)
+    packed(place, aims, latent_ref[...], base_of(step, capacity, exchange), out)
+
+
+def dispatch_kernel(capacity, exchange, steps, place_ref, aims_ref, latent_ref, *outs):
+    place, aims, latent = place_ref[...], aims_ref[...], latent_ref[...]
+    for step, out in zip(steps, outs):
+        packed(place, aims, latent, base_of(step, capacity, exchange), out)
 
 
 def encode(chunks, maps, mesh_part, bias):
     nodes, width = mesh_part.shape
-    total = None
-    for chunk in chunks:
-        rows = jnp.concatenate(
-            [chunk[j * LANES : (j + 1) * LANES, :] for j in range(width // LANES)], axis=1
-        )
-        aims = chunk[width : width + AIM_ROWS, :].astype(F32)
-        columns = jnp.transpose(aims).astype(jnp.int32) - 1
-        lines = aims.astype(jnp.int32) - 1
-        part = through(rows, maps, 0) + bias
-        hidden = jnp.concatenate(
-            [silu(part + mm(along(columns[:, k : k + 1], nodes), mesh_part)) for k in range(2)],
-            axis=0,
-        )
-        notes = normed(through(hidden, maps, 2)).astype(BF16)
-        spread = jnp.concatenate([down(lines[k : k + 1, :], nodes) for k in range(2)], axis=1)
-        partial = mm(spread, notes)
-        total = partial if total is None else total + partial
-    return total
-
-
-def first_kernel(mine, other, mesh, chunk, biases, sum_out, part_out):
+    rows = jnp.concatenate(
+        [
+            jnp.concatenate(
+                [chunk[j * LANES : (j + 1) * LANES, :] for j in range(width // LANES)], axis=1
+            )
+            for chunk in chunks
+        ],
+        axis=0,
+    )
+    lines = [chunk[width : width + AIM_ROWS, :].astype(F32) for chunk in chunks]
+    columns = [jnp.transpose(line).astype(jnp.int32) - 1 for line in lines]
+    lines = [line.astype(jnp.int32) - 1 for line in lines]
+    part = through(rows, maps, 0) + bias
+    picks = jnp.concatenate(
+        [along(column[:, k : k + 1], nodes) for k in range(2) for column in columns], axis=0
+    )
+    spread = jnp.concatenate(
+        [down(line[k : k + 1, :], nodes) for k in range(2) for line in lines], axis=1
+    )
+    hidden = silu(jnp.concatenate([part, part], axis=0) + mm(picks, mesh_part))
+    return mm(spread, normed(through(hidden, maps, 2)).astype(BF16))
+
+
+def first_kernel(mine, other, mesh, chunk, biases, sum_out, part_out, ahead_out):
     maps = (mine, other)
-    part = through(mesh[...], maps, 1).astype(BF16)
+    latent = mesh[...]
+    part = through(latent, maps, 1).astype(BF16)
     part_out[...] = part
+    ahead_out[...] = through(latent, maps, 3) + biases[1:2, :]
     sum_out[...] = encode([chunk], maps, part, biases[0:1, :])
 
 
@@ -137,50 +159,52 @@
     out[...] = total[...] + encode(chunks, (mine, other), part[...], biases[0:1, :])
 
 
-def node_kernel(total, part, mine, other, biases, gains, mesh, lend, *rest):
+def node_kernel(total, part, ahead, mine, other, biases, gains, mesh, lend, *rest):
     *chunks, mid_out, lent_out = rest
     maps = (mine, other)
     sums = total[...] + encode(chunks, maps, part[...], biases[0:1, :])
     encoded = (sums * gains[0:1, :]).astype(BF16)
-    latent = mesh[...]
-    hidden = silu(through(latent, maps, 3) + through(encoded, maps, 4) + biases[1:2, :])
+    hidden = silu(ahead[...] + through(encoded, maps, 4))
     mid = (
-        latent.astype(F32) + normed(through(hidden, maps, 5)) * gains[1:2, :]
+        mesh[...].astype(F32) + normed(through(hidden, maps, 5)) * gains[1:2, :]
     ).astype(BF16)
     mid_out[...] = mid
     picks = along(turned(lend[...]), mid.shape[0])
     lent_out[...] = mm(picks, mid).astype(BF16)
 
 
-def local_kernel(mid_ref, edges, sender, receiver, biases, mine, other, pre_out):
+def local_kernel(pieces, depth, mid_ref, edges, sender, receiver, biases, mine, other, *outs):
+    pre_out, ahead_out, picks_out, spread_out = outs
     maps = (mine, other)
     mid = mid_ref[...]
     nodes = mid.shape[0]
-    at_sender = along(turned(sender[...]), nodes)
+    number = sender[...]
+    entry = number - nodes
+    if pieces == 3:
+        entry = jnp.where(entry >= 3 * depth, entry - depth, entry)
+    odd = lax.rem(lax.axis_index("lat"), 2) == 1
+    crossed = jnp.where(entry < depth, entry + depth, jnp.where(entry < 2 * depth, entry - depth, entry))
+    entry = jnp.where(odd & (entry >= 0), crossed, entry)
+    picks_out[...] = along(turned(entry), pieces * depth)
+    spread_out[...] = down(receiver[...], nodes)
+    at_sender = along(turned(number), nodes)
     at_receiver = along(turned(receiver[...]), nodes)
+    ahead_out[...] = through(mid, maps, 10) + biases[3:4, :]
     pre = through(edges[...], maps, 6) + biases[2:3, :]
     pre = pre + mm(at_sender, through(mid, maps, 7).astype(BF16))
     pre_out[...] = pre + mm(at_receiver, through(mid, maps, 8).astype(BF16))
 
 
-def process_kernel(pre, mid_ref, sender, receiver, biases, gains, mine, other, *rest):
+def process_kernel(pre, ahead, picks, spread, mid, gains, mine, other, *rest):
     *lent, out = rest
     maps = (mine, other)
-    mid = mid_ref[...]
-    nodes = mid.shape[0]
     table = jnp.concatenate([ref[...] for ref in lent], axis=0)
-    depth = lent[0].shape[0]
-    entry = sender[...] - nodes
-    if len(lent) == 3:
-        entry = jnp.where(entry >= 3 * depth, entry - depth, entry)
-    from_halo = along(turned(entry), len(lent) * depth)
-    hidden = silu(pre[...] + mm(from_halo, through(table, maps, 7).astype(BF16)))
+    hidden = silu(pre[...] + mm(picks[...], through(table, maps, 7).astype(BF16)))
     notes = normed(through(hidden, maps, 9)).astype(BF16)
-    sums = mm(down(receiver[...], nodes), notes)
-    processed = (sums * gains[2:3, :]).astype(BF16)
-    hidden = silu(through(mid, maps, 10) + through(processed, maps, 11) + biases[3:4, :])
+    processed = (mm(spread[...], notes) * gains[2:3, :]).astype(BF16)
+    hidden = silu(ahead[...] + through(processed, maps, 11))
     out[...] = (
-        mid.astype(F32) + normed(through(hidden, maps, 12)) * gains[3:4, :]
+        mid[...].astype(F32) + normed(through(hidden, maps, 12)) * gains[3:4, :]
     ).astype(BF16)
 
 
@@ -201,9 +225,27 @@
     return lax.ppermute(value, axes, [(i, i ^ step) for i in range(count)])
 
 
+def moved(value, step):
+    lats, lons = lax.axis_size("lat"), lax.axis_size("lon")
+    pairs = []
+    for i in range(lats * lons):
+        lat, lon = (i // lons + step // lons) % lats, (i % lons + step % lons) % lons
+        pairs.append((i, lat * lons + lon))
+    return lax.ppermute(value, ("lat", "lon"), pairs)
+
+
 def shift(value, axis, step):
     count = lax.axis_size(axis)
     return lax.ppermute(value, axis, [(i, (i + step) % count) for i in range(count)])
+
+
+def paired(value, axis, first):
+    count = lax.axis_size(axis)
+    pairs = []
+    for i in range(first, first + count, 2):
+        low, high = i % count, (i + 1) % count
+        pairs += [(low, high), (high, low)]
+    return lax.ppermute(value, axis, pairs)
 
 
 def sent_whole(chunks, owners, capacity, width):
@@ -241,15 +283,16 @@
     lon_count = lax.axis_size("lon")
     owners = lax.axis_size("lat") * lon_count
     capacity = max(2, 2 * rows_dev // owners)
-    exchange = capacity == LANES and owners <= 16 and owners & (owners - 1) == 0
+    exchange = capacity == LANES and owners <= 16
 
     other = swap(weights, "ch", 1)
 
     count = owners * capacity // LANES
     chunk_shape = ((width + AIM_ROWS, LANES), BF16)
-    chunks = call(
-        functools.partial(dispatch_kernel, owners, capacity, exchange),
-        [chunk_shape] * count,
+    order = [2, 6, 1, 7, 3, 4, 5] if owners == 8 else list(range(1, count))
+    lead, place, aims = call(
+        functools.partial(place_kernel, owners, capacity, exchange, order[0]),
+        [chunk_shape, ((1, rows_dev), jnp.int32), ((AIM_ROWS, rows_dev), BF16)],
         [
             pltpu.with_memory_space_constraint(value, pltpu.HBM)
             for value in (grid_owner.T, grid_target.T, grid_latent)
@@ -264,18 +307,29 @@
         flops=10**9,
         moved=2 * 10**6,
     )
+    others = [*order[1:], 0]
+    chunks = {order[0]: lead}
+    rest = call(
+        functools.partial(dispatch_kernel, capacity, exchange, others),
+        [chunk_shape] * len(others),
+        (place, aims, grid_latent),
+        [VMEM] * 3,
+        flops=10**9,
+        moved=2 * 10**6,
+    )
+    chunks.update(zip(others, rest))
     if exchange:
         arrived = {0: chunks[0]}
-        for step in [1, 4, 5, 6, 7, 2, 3] if owners == 8 else range(1, owners):
-            arrived[step] = swap(chunks[step], ("lat", "lon"), step)
-        groups = [[0], [1, 2], [4, 3, 5], [6, 7]] if owners == 8 else [[0], list(range(1, owners))]
+        for step in order:
+            arrived[step] = moved(chunks[step], step)
+        groups = [[0], order[:3], order[3:5], *[[step] for step in order[5:]]]
     else:
-        arrived = dict(enumerate(sent_whole(chunks, owners, capacity, width)))
+        arrived = dict(enumerate(sent_whole([chunks[i] for i in range(count)], owners, capacity, width)))
         groups = [[0], list(range(1, count))]
 
-    total, part = call(
+    total, part, ahead = call(
         first_kernel,
-        [((nodes, width), F32), ((nodes, width), BF16)],
+        [((nodes, width), F32), ((nodes, width), BF16), ((nodes, width), F32)],
         (weights, other, mesh_latent, arrived[0], biases),
         [VMEM] * 5,
         flops=5 * 10**8,
@@ -293,19 +347,25 @@
     mid, lent = call(
         node_kernel,
         [((nodes, width), BF16), ((halo_rows.shape[0], width), BF16)],
-        (total, part, weights, other, biases, gains, mesh_latent)
+        (total, part, ahead, weights, other, biases, gains, mesh_latent)
         + (halo_rows.reshape(1, -1), *[arrived[i] for i in groups[-1]]),
-        [VMEM] * (8 + len(groups[-1])),
+        [VMEM] * (9 + len(groups[-1])),
         flops=10**9,
         moved=3 * 10**6,
     )
-    halo = [shift(lent, "lat", 1), shift(lent, "lat", -1), shift(lent, "lon", 1)]
+    halo = [paired(lent, "lat", 1), paired(lent, "lat", 0), shift(lent, "lon", 1)]
     if lon_count != 2:
         halo.append(shift(lent, "lon", -1))
     sender, receiver = mesh_sender.reshape(1, -1), mesh_receiver.reshape(1, -1)
-    (pre,) = call(
-        local_kernel,
-        [((edges, width), F32)],
+    pieces, depth = len(halo), halo_rows.shape[0]
+    pre, ahead, picks, spread = call(
+        functools.partial(local_kernel, pieces, depth),
+        [
+            ((edges, width), F32),
+            ((nodes, width), F32),
+            ((edges, pieces * depth), BF16),
+            ((nodes, edges), BF16),
+        ],
         (mid, edge_latent, sender, receiver, biases, weights, other),
         [VMEM] * 7,
         flops=10**9,
@@ -314,8 +374,8 @@
     (out,) = call(
         process_kernel,
         [((nodes, width), BF16)],
-        (pre, mid, sender, receiver, biases, gains, weights, other, *halo),
-        [VMEM] * (8 + len(halo)),
+        (pre, ahead, picks, spread, mid, gains, weights, other, *halo),
+        [VMEM] * (8 + pieces),
         flops=10**9,
         moved=3 * 10**6,
     )

time: 47.1 us -> 43.8 us (0.930)
  starting transfers between devices: 18.8 us -> 14.8 us
  waiting for transfers between devices: 13.6 us -> 14.8 us
    ppermute x0 -> x9, waiting for transfers between devices: none -> 14.1 us  [the longest x7 11.7 us: moved(): return lax.ppermute(value, ('lat', 'lon'), pairs)]
    ppermute x0 -> x9, starting transfers between devices: none -> 13.7 us  [the longest x7 12.1 us: moved(): return lax.ppermute(value, ('lat', 'lon'), pairs)]
    ppermute x8 -> x1, starting transfers between devices: 13.4 us -> 0.45 us  [swap(): return lax.ppermute(value, axes, [(i, i ^ step) for i in range(count)])]
    ppermute x8 -> x1, waiting for transfers between devices: 9.47 us -> 0.01 us  [swap(): return lax.ppermute(value, axes, [(i, i ^ step) for i in range(count)])]
    ppermute x3 -> x1, starting transfers between devices: 5.38 us -> 0.6 us  [shift(): lax.ppermute(value, axis, [(i, (i + step) % count) for i in range(count)])]
    ppermute x3 -> x1, waiting for transfers between devices: 4.13 us -> 0.66 us  [shift(): lax.ppermute(value, axis, [(i, (i + step) % count) for i in range(count)])]
    pallas_call x7 -> x9, Pallas kernels: 14.3 us -> 13.9 us  [call(): pl.pallas_call(kernel, out_shape=[jax.ShapeDtypeStruct(shape, kind) for s...]
  transfers between devices with their start and end apart: 11 -> 11, of which waited for: 4 -> 6; matrix products, arithmetic and copies ran while one was open for 0% -> 0% of each run, Pallas kernels for 19% -> 21%
where the time goes in v3:
time: 43.8 us; the launch traced here: 43.6 us
  starting transfers between devices  14.8 us (34%)
  waiting for transfers between devices  14.8 us (34%)
  Pallas kernels  13.9 us (32%)
    pallas_call x9, Pallas kernels, call(): pl.pallas_call(kernel, out_shape=[jax.ShapeDtypeStruct(shape, kind) for s...  13.9 us
    ppermute x7, starting transfers between devices, moved(): return lax.ppermute(value, ('lat', 'lon'), pairs)  12.1 us
    ppermute x7, waiting for transfers between devices, moved(): return lax.ppermute(value, ('lat', 'lon'), pairs)  11.7 us
    ppermute x2, waiting for transfers between devices, paired(): return lax.ppermute(value, axis, pairs)  2.39 us
    ppermute x2, starting transfers between devices, paired(): return lax.ppermute(value, axis, pairs)  1.57 us
  transfers between devices with their start and end apart: 11, of which 6 were waited for; matrix products, arithmetic and copies ran while one was open for 0% of the time, Pallas kernels for 21%

profile of v3, /device:TPU:0, one launch (start us, length us, event | category | flops | bytes accessed | tf_op | source)
XLA Modules:
  0.0 43.6 jit_solution(15167019855351652237)
XLA Ops:
  0.0 0.5 %collective-permute-start = (bf16[13,256,512]{2,1,0:T(8,128)(2,1)}, bf16[13,256,512]{2,1,0:T(8,128)(2,1)S(1)}, u32[]{:S(2)}, u32[]{:S(2)}) collective-permute-start(bf16[13,256,512]{2,1,0:T(8,128)(2,1)} %mine.13), channel_id=1, source_target_pairs={{0,1},{1,0},{2,3},{3,2},{4,5},{5,4},{6,7},{7,6},{8,9},{9,8},{10,11... | collective-permute-start | bytes 10223624 | tf_op jit(solution)/shard_map/ppermute | solution.py:225
  0.5 1.5 %shard_map.109 = (bf16[528,128]{1,0:T(8,128)(2,1)S(1)}, s32[1,512]{1,0:T(1,128)S(1)}, bf16[16,512]{1,0:T(8,128)(2,1)S(1)}) custom-call(s32[1,512]{1,0:T(1,128)} %bitcast.9, s32[2,512]{1,0:T(2,128)} %bitcast.8, bf16[512,512]{1,0:T(8,128)(2,1)} %latent_ref.1), custom_call_target="tpu_custom_call" | custom-call | flops 1000000000 | bytes 2000000 | tf_op jit(solution)/shard_map/pallas_call | solution.py:212
  2.0 2.6 %collective-permute-start.1 = (bf16[528,128]{1,0:T(8,128)(2,1)S(1)}, bf16[528,128]{1,0:T(8,128)(2,1)S(1)}, u32[]{:S(2)}, u32[]{:S(2)}) collective-permute-start(bf16[528,128]{1,0:T(8,128)(2,1)S(1)} %get-tuple-element.29), channel_id=1, source_target_pairs={{0,4},{2,6},{4,8},{6,10},{8,12},{10,14},{12,0},{14,2},{1,5},{3,7},... | collective-permute-start | bytes 405512 | tf_op jit(solution)/shard_map/ppermute | solution.py:234
  4.6 0.9 %shard_map.110 = (bf16[528,128]{1,0:T(8,128)(2,1)S(1)}, bf16[528,128]{1,0:T(8,128)(2,1)S(1)}, bf16[528,128]{1,0:T(8,128)(2,1)S(1)}, bf16[528,128]{1,0:T(8,128)(2...) custom-call(s32[1,512]{1,0:T(1,128)S(1)} %get-tuple-element.24.place_ref, ...), custom_call_target="tpu_custom_call" | custom-call | flops 1000000000 | bytes 2000000 | tf_op jit(solution)/shard_map/pallas_call | solution.py:212
  5.5 2.1 %collective-permute-start.2 = (bf16[528,128]{1,0:T(8,128)(2,1)S(1)}, bf16[528,128]{1,0:T(8,128)(2,1)S(1)}, u32[]{:S(2)}, u32[]{:S(2)}) collective-permute-start(bf16[528,128]{1,0:T(8,128)(2,1)S(1)} %get-tuple-element.30), channel_id=1, source_target_pairs={{0,12},{2,14},{4,0},{6,2},{8,4},{10,6},{12,8},{14,10},{1,13},{3,15... | collective-permute-start | bytes 405512 | tf_op jit(solution)/shard_map/ppermute | solution.py:234
  7.6 1.7 %collective-permute-start.3 = (bf16[528,128]{1,0:T(8,128)(2,1)S(1)}, bf16[528,128]{1,0:T(8,128)(2,1)S(1)}, u32[]{:S(2)}, u32[]{:S(2)}) collective-permute-start(bf16[528,128]{1,0:T(8,128)(2,1)S(1)} %get-tuple-element.31), channel_id=1, source_target_pairs={{0,2},{2,0},{4,6},{6,4},{8,10},{10,8},{12,14},{14,12},{1,3},{3,1},... | collective-permute-start | bytes 405512 | tf_op jit(solution)/shard_map/ppermute | solution.py:234
  9.3 1.8 %collective-permute-start.4 = (bf16[528,128]{1,0:T(8,128)(2,1)S(1)}, bf16[528,128]{1,0:T(8,128)(2,1)S(1)}, u32[]{:S(2)}, u32[]{:S(2)}) collective-permute-start(bf16[528,128]{1,0:T(8,128)(2,1)S(1)} %get-tuple-element.32), channel_id=1, source_target_pairs={{0,14},{2,12},{4,2},{6,0},{8,6},{10,4},{12,10},{14,8},{1,15},{3,13... | collective-permute-start | bytes 405512 | tf_op jit(solution)/shard_map/ppermute | solution.py:234
  11.1 0.0 collective-permute-done.other
  11.1 1.2 %collective-permute-start.5 = (bf16[528,128]{1,0:T(8,128)(2,1)S(1)}, bf16[528,128]{1,0:T(8,128)(2,1)S(1)}, u32[]{:S(2)}, u32[]{:S(2)}) collective-permute-start(bf16[528,128]{1,0:T(8,128)(2,1)S(1)} %get-tuple-element.33), channel_id=1, source_target_pairs={{0,6},{2,4},{4,10},{6,8},{8,14},{10,12},{12,2},{14,0},{1,7},{3,5},... | collective-permute-start | bytes 405512 | tf_op jit(solution)/shard_map/ppermute | solution.py:234
  12.3 1.2 %shard_map.111 = (f32[256,512]{1,0:T(8,128)S(1)}, bf16[256,512]{1,0:T(8,128)(2,1)S(1)}, f32[256,512]{1,0:T(8,128)S(1)}) custom-call(bf16[13,256,512]{2,1,0:T(8,128)(2,1)S(1)} %copy-done, bf16[13,256,512]{2,1,0:T(8,128)(2,1)S(1)} %collective-permute-done.other, bf16[256,512]{1,0:T(8,128)(2,1)S(1)} %copy-done.1, bf16[528,128]{1,0:T(8,128)(2,1)S(1)} %get-tuple-element.26.chunk, ...), custom_call_target="tpu_custom_call" | custom-call | flops 500000000 | bytes 3000000 | tf_op jit(solution)/shard_map/pallas_call | solution.py:212
  13.5 0.9 %collective-permute-start.6 = (bf16[528,128]{1,0:T(8,128)(2,1)S(1)}, bf16[528,128]{1,0:T(8,128)(2,1)S(1)}, u32[]{:S(2)}, u32[]{:S(2)}) collective-permute-start(bf16[528,128]{1,0:T(8,128)(2,1)S(1)} %get-tuple-element.34), channel_id=1, source_target_pairs={{0,8},{2,10},{4,12},{6,14},{8,0},{10,2},{12,4},{14,6},{1,9},{3,11}... | collective-permute-start | bytes 405512 | tf_op jit(solution)/shard_map/ppermute | solution.py:234
  14.3 0.0 collective-permute-done.2.rest_1_
  14.3 1.9 %collective-permute-start.7 = (bf16[528,128]{1,0:T(8,128)(2,1)S(1)}, bf16[528,128]{1,0:T(8,128)(2,1)S(1)}, u32[]{:S(2)}, u32[]{:S(2)}) collective-permute-start(bf16[528,128]{1,0:T(8,128)(2,1)S(1)} %get-tuple-element.36), channel_id=1, source_target_pairs={{0,10},{2,8},{4,14},{6,12},{8,2},{10,0},{12,6},{14,4},{1,11},{3,9}... | collective-permute-start | bytes 405512 | tf_op jit(solution)/shard_map/ppermute | solution.py:234
  16.3 0.0 collective-permute-done.3.rest_2_
  16.3 1.8 %shard_map.112.total = f32[256,512]{1,0:T(8,128)S(1)} custom-call(f32[256,512]{1,0:T(8,128)S(1)} %get-tuple-element.27.total, bf16[256,512]{1,0:T(8,128)(2,1)S(1)} %get-tuple-element.28.part, bf16[13,256,512]{2,1,0:T(8,128)(2,1)S(1)} %copy-done, bf16[13,256,512]{2,1,0:T(8,128)(2,1)S(1)} %collective-permute-done.other, f32[4,512]{1,0:T(4,128)S(1)} %copy-done.3, ...), custom_call_target="tpu_custom_call" | custom-call | flops 1200000000 | bytes 2000000 | tf_op jit(solution)/shard_map/pallas_call | solution.py:212
  18.0 0.0 collective-permute-done.4.rest_0_
  18.1 2.9 %collective-permute-done.5.rest_1_ = bf16[528,128]{1,0:T(8,128)(2,1)S(1)} collective-permute-done((bf16[528,128]{1,0:T(8,128)(2,1)S(1)}, bf16[528,128]{1,0:T(8,128)(2,1)S(1)}, u32[]{:S(2)}, u32[]{:S(2)}) %collective-permute-start.5) | collective-permute-done | bytes 135200 | tf_op jit(solution)/shard_map/ppermute | solution.py:234
  21.0 1.4 %shard_map.113.total = f32[256,512]{1,0:T(8,128)S(1)} custom-call(f32[256,512]{1,0:T(8,128)S(1)} %shard_map.112.total, bf16[256,512]{1,0:T(8,128)(2,1)S(1)} %get-tuple-element.28.part, bf16[13,256,512]{2,1,0:T(8,128)(2,1)S(1)} %copy-done, bf16[13,256,512]{2,1,0:T(8,128)(2,1)S(1)} %collective-permute-done.other, f32[4,512]{1,0:T(4,128)S(1)} %copy-done.3, ...), custom_call_target="tpu_custom_call" | custom-call | flops 800000000 | bytes 2000000 | tf_op jit(solution)/shard_map/pallas_call | solution.py:212
  22.3 0.0 copy-start.4
  22.3 0.0 copy-start.7
  22.4 6.1 %collective-permute-done.6.rest_0_ = bf16[528,128]{1,0:T(8,128)(2,1)S(1)} collective-permute-done((bf16[528,128]{1,0:T(8,128)(2,1)S(1)}, bf16[528,128]{1,0:T(8,128)(2,1)S(1)}, u32[]{:S(2)}, u32[]{:S(2)}) %collective-permute-start.6) | collective-permute-done | bytes 135200 | tf_op jit(solution)/shard_map/ppermute | solution.py:234
  28.4 1.0 %shard_map.114.total = f32[256,512]{1,0:T(8,128)S(1)} custom-call(f32[256,512]{1,0:T(8,128)S(1)} %shard_map.113.total, bf16[256,512]{1,0:T(8,128)(2,1)S(1)} %get-tuple-element.28.part, bf16[13,256,512]{2,1,0:T(8,128)(2,1)S(1)} %copy-done, bf16[13,256,512]{2,1,0:T(8,128)(2,1)S(1)} %collective-permute-done.other, f32[4,512]{1,0:T(4,128)S(1)} %copy-done.3, ...), custom_call_target="tpu_custom_call" | custom-call | flops 400000000 | bytes 2000000 | tf_op jit(solution)/shard_map/pallas_call | solution.py:212
  29.5 2.7 %collective-permute-done.7.rest_0_ = bf16[528,128]{1,0:T(8,128)(2,1)S(1)} collective-permute-done((bf16[528,128]{1,0:T(8,128)(2,1)S(1)}, bf16[528,128]{1,0:T(8,128)(2,1)S(1)}, u32[]{:S(2)}, u32[]{:S(2)}) %collective-permute-start.7) | collective-permute-done | bytes 135200 | tf_op jit(solution)/shard_map/ppermute | solution.py:234
  32.2 0.0 copy-start.6
  32.2 1.9 %shard_map.115 = (bf16[256,512]{1,0:T(8,128)(2,1)S(1)}, bf16[64,512]{1,0:T(8,128)(2,1)S(1)}) custom-call(f32[256,512]{1,0:T(8,128)S(1)} %shard_map.114.total, bf16[256,512]{1,0:T(8,128)(2,1)S(1)} %get-tuple-element.28.part, f32[256,512]{1,0:T(8,128)S(1)} %get-tuple-element.35.ahead, bf16[13,256,512]{2,1,0:T(8,128)(2,1)S(1)} %copy-done, ...), custom_call_target="tpu_custom_call" | custom-call | flops 1000000000 | bytes 3000000 | tf_op jit(solution)/shard_map/pallas_call | solution.py:212
  34.1 0.6 %collective-permute-start.10 = (bf16[64,512]{1,0:T(8,128)(2,1)S(1)}, bf16[64,512]{1,0:T(8,128)(2,1)S(1)}, u32[]{:S(2)}, u32[]{:S(2)}) collective-permute-start(bf16[64,512]{1,0:T(8,128)(2,1)S(1)} %get-tuple-element.42), channel_id=1, source_target_pairs={{0,2},{2,0},{1,3},{3,1},{4,6},{6,4},{5,7},{7,5},{8,10},{10,8},{9,1... | collective-permute-start | bytes 196616 | tf_op jit(solution)/shard_map/ppermute | solution.py:239
  34.7 1.6 %collective-permute-start.8 = (bf16[64,512]{1,0:T(8,128)(2,1)S(1)}, bf16[64,512]{1,0:T(8,128)(2,1)S(1)}, u32[]{:S(2)}, u32[]{:S(2)}) collective-permute-start(bf16[64,512]{1,0:T(8,128)(2,1)S(1)} %get-tuple-element.42), channel_id=1, source_target_pairs={{4,8},{8,4},{12,0},{0,12},{5,9},{9,5},{13,1},{1,13},{6,10},{10,6},... | collective-permute-start | bytes 196616 | tf_op jit(solution)/shard_map/ppermute | solution.py:248
  36.3 1.5 %shard_map.116 = (f32[512,512]{1,0:T(8,128)S(1)}, f32[256,512]{1,0:T(8,128)S(1)}, bf16[512,192]{1,0:T(8,128)(2,1)S(1)}, bf16[256,512]{1,0:T(8,128)(2,1)S(1)}) custom-call(bf16[256,512]{1,0:T(8,128)(2,1)S(1)} %get-tuple-element.37.mid_ref.mid, bf16[512,512]{1,0:T(8,128)(2,1)S(1)} %copy-done.2, s32[1,512]{1,0:T(1,128)S(1)} %bitcast.5, s32[1,512]{1,0:T(1,128)S(1)} %bitcast.6, ...), custom_call_target="tpu_custom_call" | custom-call | flops 1000000000 | bytes 3000000 | tf_op jit(solution)/shard_map/pallas_call | solution.py:212
  37.8 0.7 %collective-permute-done.10.rest_2_ = bf16[64,512]{1,0:T(8,128)(2,1)S(1)} collective-permute-done((bf16[64,512]{1,0:T(8,128)(2,1)S(1)}, bf16[64,512]{1,0:T(8,128)(2,1)S(1)}, u32[]{:S(2)}, u32[]{:S(2)}) %collective-permute-start.10) | collective-permute-done | bytes 65568 | tf_op jit(solution)/shard_map/ppermute | solution.py:239
  38.5 0.6 %collective-permute-done.9.rest_1_ = bf16[64,512]{1,0:T(8,128)(2,1)S(1)} collective-permute-done((bf16[64,512]{1,0:T(8,128)(2,1)S(1)}, bf16[64,512]{1,0:T(8,128)(2,1)S(1)}, u32[]{:S(2)}, u32[]{:S(2)}) %collective-permute-start.9) | collective-permute-done | bytes 65568 | tf_op jit(solution)/shard_map/ppermute | solution.py:248
  39.1 1.8 %collective-permute-done.8.rest_0_ = bf16[64,512]{1,0:T(8,128)(2,1)S(1)} collective-permute-done((bf16[64,512]{1,0:T(8,128)(2,1)S(1)}, bf16[64,512]{1,0:T(8,128)(2,1)S(1)}, u32[]{:S(2)}, u32[]{:S(2)}) %collective-permute-start.8) | collective-permute-done | bytes 65568 | tf_op jit(solution)/shard_map/ppermute | solution.py:248
  40.9 2.8 %shard_map.117 = bf16[256,512]{1,0:T(8,128)(2,1)} custom-call(f32[512,512]{1,0:T(8,128)S(1)} %get-tuple-element.38.pre, f32[256,512]{1,0:T(8,128)S(1)} %get-tuple-element.39.ahead, bf16[512,192]{1,0:T(8,128)(2,1)S(1)} %get-tuple-element.40.picks, bf16[256,512]{1,0:T(8,128)(2,1)S(1)} %get-tuple-element.41.spread, ...), custom_call_target="tpu_custom_call" | custom-call | flops 1000000000 | bytes 3000000 | tf_op jit(solution)/shard_map/pallas_call | solution.py:212
  (17 shorter events, 0.0 us)
Async XLA Ops:
  0.0 4.6 %copy-start.8 = (bf16[512,512]{1,0:T(8,128)(2,1)S(1)}, bf16[512,512]{1,0:T(8,128)(2,1)}, u32[]{:S(2)}) copy-start(bf16[512,512]{1,0:T(8,128)(2,1)} %latent_ref.1) | copy-start | bytes 1572868
  0.0 11.1 %collective-permute-start = (bf16[13,256,512]{2,1,0:T(8,128)(2,1)}, bf16[13,256,512]{2,1,0:T(8,128)(2,1)S(1)}, u32[]{:S(2)}, u32[]{:S(2)}) collective-permute-start(bf16[13,256,512]{2,1,0:T(8,128)(2,1)} %mine.13), channel_id=1, source_target_pairs={{0,1},{1,0},{2,3},{3,2},{4,5},{5,4},{6,7},{7,6},{8,9},{9,8},{10,11... | collective-permute-start | bytes 10223624 | tf_op jit(solution)/shard_map/ppermute | solution.py:225
  0.5 11.8 %copy-start = (bf16[13,256,512]{2,1,0:T(8,128)(2,1)S(1)}, bf16[13,256,512]{2,1,0:T(8,128)(2,1)}, u32[]{:S(2)}) copy-start(bf16[13,256,512]{2,1,0:T(8,128)(2,1)} %mine.13) | copy-start | bytes 10223620
  0.5 11.8 %copy-start.1 = (bf16[256,512]{1,0:T(8,128)(2,1)S(1)}, bf16[256,512]{1,0:T(8,128)(2,1)}, u32[]{:S(2)}) copy-start(bf16[256,512]{1,0:T(8,128)(2,1)} %mesh.3) | copy-start | bytes 786436
  0.5 11.8 %copy-start.3 = (f32[4,512]{1,0:T(4,128)S(1)}, f32[4,512]{1,0:T(4,128)}, u32[]{:S(2)}) copy-start(f32[4,512]{1,0:T(4,128)} %biases.11) | copy-start | bytes 24580
  2.0 11.5 %collective-permute-start.1 = (bf16[528,128]{1,0:T(8,128)(2,1)S(1)}, bf16[528,128]{1,0:T(8,128)(2,1)S(1)}, u32[]{:S(2)}, u32[]{:S(2)}) collective-permute-start(bf16[528,128]{1,0:T(8,128)(2,1)S(1)} %get-tuple-element.29), channel_id=1, source_target_pairs={{0,4},{2,6},{4,8},{6,10},{8,12},{10,14},{12,0},{14,2},{1,5},{3,7},... | collective-permute-start | bytes 405512 | tf_op jit(solution)/shard_map/ppermute | solution.py:234
  5.5 8.8 %collective-permute-start.2 = (bf16[528,128]{1,0:T(8,128)(2,1)S(1)}, bf16[528,128]{1,0:T(8,128)(2,1)S(1)}, u32[]{:S(2)}, u32[]{:S(2)}) collective-permute-start(bf16[528,128]{1,0:T(8,128)(2,1)S(1)} %get-tuple-element.30), channel_id=1, source_target_pairs={{0,12},{2,14},{4,0},{6,2},{8,4},{10,6},{12,8},{14,10},{1,13},{3,15... | collective-permute-start | bytes 405512 | tf_op jit(solution)/shard_map/ppermute | solution.py:234
  7.6 8.6 %collective-permute-start.3 = (bf16[528,128]{1,0:T(8,128)(2,1)S(1)}, bf16[528,128]{1,0:T(8,128)(2,1)S(1)}, u32[]{:S(2)}, u32[]{:S(2)}) collective-permute-start(bf16[528,128]{1,0:T(8,128)(2,1)S(1)} %get-tuple-element.31), channel_id=1, source_target_pairs={{0,2},{2,0},{4,6},{6,4},{8,10},{10,8},{12,14},{14,12},{1,3},{3,1},... | collective-permute-start | bytes 405512 | tf_op jit(solution)/shard_map/ppermute | solution.py:234
  9.3 8.7 %collective-permute-start.4 = (bf16[528,128]{1,0:T(8,128)(2,1)S(1)}, bf16[528,128]{1,0:T(8,128)(2,1)S(1)}, u32[]{:S(2)}, u32[]{:S(2)}) collective-permute-start(bf16[528,128]{1,0:T(8,128)(2,1)S(1)} %get-tuple-element.32), channel_id=1, source_target_pairs={{0,14},{2,12},{4,2},{6,0},{8,6},{10,4},{12,10},{14,8},{1,15},{3,13... | collective-permute-start | bytes 405512 | tf_op jit(solution)/shard_map/ppermute | solution.py:234
  11.1 9.9 %collective-permute-start.5 = (bf16[528,128]{1,0:T(8,128)(2,1)S(1)}, bf16[528,128]{1,0:T(8,128)(2,1)S(1)}, u32[]{:S(2)}, u32[]{:S(2)}) collective-permute-start(bf16[528,128]{1,0:T(8,128)(2,1)S(1)} %get-tuple-element.33), channel_id=1, source_target_pairs={{0,6},{2,4},{4,10},{6,8},{8,14},{10,12},{12,2},{14,0},{1,7},{3,5},... | collective-permute-start | bytes 405512 | tf_op jit(solution)/shard_map/ppermute | solution.py:234
  13.5 15.0 %collective-permute-start.6 = (bf16[528,128]{1,0:T(8,128)(2,1)S(1)}, bf16[528,128]{1,0:T(8,128)(2,1)S(1)}, u32[]{:S(2)}, u32[]{:S(2)}) collective-permute-start(bf16[528,128]{1,0:T(8,128)(2,1)S(1)} %get-tuple-element.34), channel_id=1, source_target_pairs={{0,8},{2,10},{4,12},{6,14},{8,0},{10,2},{12,4},{14,6},{1,9},{3,11}... | collective-permute-start | bytes 405512 | tf_op jit(solution)/shard_map/ppermute | solution.py:234
  14.3 17.9 %collective-permute-start.7 = (bf16[528,128]{1,0:T(8,128)(2,1)S(1)}, bf16[528,128]{1,0:T(8,128)(2,1)S(1)}, u32[]{:S(2)}, u32[]{:S(2)}) collective-permute-start(bf16[528,128]{1,0:T(8,128)(2,1)S(1)} %get-tuple-element.36), channel_id=1, source_target_pairs={{0,10},{2,8},{4,14},{6,12},{8,2},{10,0},{12,6},{14,4},{1,11},{3,9}... | collective-permute-start | bytes 405512 | tf_op jit(solution)/shard_map/ppermute | solution.py:234
  22.3 9.9 %copy-start.4 = (f32[4,512]{1,0:T(4,128)S(1)}, f32[4,512]{1,0:T(4,128)}, u32[]{:S(2)}) copy-start(f32[4,512]{1,0:T(4,128)} %gains.3) | copy-start | bytes 24580
  22.3 9.9 %copy-start.7 = (s32[64]{0:T(128)S(1)}, s32[64]{0:T(128)}, u32[]{:S(2)}) copy-start(s32[64]{0:T(128)} %param.18) | copy-start | bytes 772
  32.2 4.1 %copy-start.2 = (bf16[512,512]{1,0:T(8,128)(2,1)S(1)}, bf16[512,512]{1,0:T(8,128)(2,1)}, u32[]{:S(2)}) copy-start(bf16[512,512]{1,0:T(8,128)(2,1)} %edges.1) | copy-start | bytes 1572868
  32.2 4.1 %copy-start.5 = (s32[512]{0:T(512)S(1)}, s32[512]{0:T(512)}, u32[]{:S(2)}) copy-start(s32[512]{0:T(512)} %param.16) | copy-start | bytes 6148
  32.2 4.1 %copy-start.6 = (s32[512]{0:T(512)S(1)}, s32[512]{0:T(512)}, u32[]{:S(2)}) copy-start(s32[512]{0:T(512)} %param.17) | copy-start | bytes 6148
  34.1 4.3 %collective-permute-start.10 = (bf16[64,512]{1,0:T(8,128)(2,1)S(1)}, bf16[64,512]{1,0:T(8,128)(2,1)S(1)}, u32[]{:S(2)}, u32[]{:S(2)}) collective-permute-start(bf16[64,512]{1,0:T(8,128)(2,1)S(1)} %get-tuple-element.42), channel_id=1, source_target_pairs={{0,2},{2,0},{1,3},{3,1},{4,6},{6,4},{5,7},{7,5},{8,10},{10,8},{9,1... | collective-permute-start | bytes 196616 | tf_op jit(solution)/shard_map/ppermute | solution.py:239
  34.7 4.3 %collective-permute-start.9 = (bf16[64,512]{1,0:T(8,128)(2,1)S(1)}, bf16[64,512]{1,0:T(8,128)(2,1)S(1)}, u32[]{:S(2)}, u32[]{:S(2)}) collective-permute-start(bf16[64,512]{1,0:T(8,128)(2,1)S(1)} %get-tuple-element.42), channel_id=1, source_target_pairs={{0,4},{4,0},{8,12},{12,8},{1,5},{5,1},{9,13},{13,9},{2,6},{6,2},{1... | collective-permute-start | bytes 196616 | tf_op jit(solution)/shard_map/ppermute | solution.py:248
  34.7 6.1 %collective-permute-start.8 = (bf16[64,512]{1,0:T(8,128)(2,1)S(1)}, bf16[64,512]{1,0:T(8,128)(2,1)S(1)}, u32[]{:S(2)}, u32[]{:S(2)}) collective-permute-start(bf16[64,512]{1,0:T(8,128)(2,1)S(1)} %get-tuple-element.42), channel_id=1, source_target_pairs={{4,8},{8,4},{12,0},{0,12},{5,9},{9,5},{13,1},{1,13},{6,10},{10,6},... | collective-permute-start | bytes 196616 | tf_op jit(solution)/shard_map/ppermute | solution.py:248

commit v4 on v3

--- a/solution.py
+++ b/solution.py
@@ -9,7 +9,7 @@
 
 EPSILON = 1e-05
 LANES = 128
-AIM_ROWS = 16
+AIM_ROWS = 8
 F32 = jnp.float32
 BF16 = jnp.bfloat16
 HBM = pl.BlockSpec(memory_space=pltpu.HBM)
@@ -145,13 +145,17 @@
     return mm(spread, normed(through(hidden, maps, 2)).astype(BF16))
 
 
-def first_kernel(mine, other, mesh, chunk, biases, sum_out, part_out, ahead_out):
+def first_kernel(mine, other, mesh, lend, biases, *rest):
+    *chunks, sum_out, part_out, ahead_out, lent_ahead_out, lent_latent_out = rest
     maps = (mine, other)
     latent = mesh[...]
     part = through(latent, maps, 1).astype(BF16)
     part_out[...] = part
     ahead_out[...] = through(latent, maps, 3) + biases[1:2, :]
-    sum_out[...] = encode([chunk], maps, part, biases[0:1, :])
+    lent = mm(along(turned(lend[...]), latent.shape[0]), latent).astype(BF16)
+    lent_latent_out[...] = lent
+    lent_ahead_out[...] = through(lent, maps, 3) + biases[1:2, :]
+    sum_out[...] = encode(chunks, maps, part, biases[0:1, :])
 
 
 def more_kernel(total, part, mine, other, biases, *rest):
@@ -160,23 +164,27 @@
 
 
 def node_kernel(total, part, ahead, mine, other, biases, gains, mesh, lend, *rest):
-    *chunks, mid_out, lent_out = rest
+    *chunks, sums_out, lent_out = rest
     maps = (mine, other)
     sums = total[...] + encode(chunks, maps, part[...], biases[0:1, :])
-    encoded = (sums * gains[0:1, :]).astype(BF16)
-    hidden = silu(ahead[...] + through(encoded, maps, 4))
-    mid = (
-        mesh[...].astype(F32) + normed(through(hidden, maps, 5)) * gains[1:2, :]
-    ).astype(BF16)
+    sums = (sums * gains[0:1, :]).astype(BF16)
+    sums_out[...] = sums
+    picks = along(turned(lend[...]), sums.shape[0])
+    lent = mm(picks, sums).astype(BF16)
+    lent_out[...] = updated(ahead[...], lent, mesh[...], maps, gains)
+
+
+def updated(ahead, sums, latent, maps, gains):
+    hidden = silu(ahead + through(sums, maps, 4))
+    change = normed(through(hidden, maps, 5)) * gains[1:2, :]
+    return (latent.astype(F32) + change).astype(BF16)
+
+
+def local_kernel(pieces, depth, sums, node_ahead, mesh, edges, sender, receiver, *rest):
+    biases, gains, mine, other, mid_out, pre_out, ahead_out, picks_out, spread_out = rest
+    maps = (mine, other)
+    mid = updated(node_ahead[...], sums[...], mesh[...], maps, gains)
     mid_out[...] = mid
-    picks = along(turned(lend[...]), mid.shape[0])
-    lent_out[...] = mm(picks, mid).astype(BF16)
-
-
-def local_kernel(pieces, depth, mid_ref, edges, sender, receiver, biases, mine, other, *outs):
-    pre_out, ahead_out, picks_out, spread_out = outs
-    maps = (mine, other)
-    mid = mid_ref[...]
     nodes = mid.shape[0]
     number = sender[...]
     entry = number - nodes
@@ -197,6 +205,7 @@
 
 def process_kernel(pre, ahead, picks, spread, mid, gains, mine, other, *rest):
     *lent, out = rest
+    lent = [lent[1], lent[0], *lent[2:]]
     maps = (mine, other)
     table = jnp.concatenate([ref[...] for ref in lent], axis=0)
     hidden = silu(pre[...] + mm(picks[...], through(table, maps, 7).astype(BF16)))
@@ -289,7 +298,7 @@
 
     count = owners * capacity // LANES
     chunk_shape = ((width + AIM_ROWS, LANES), BF16)
-    order = [2, 6, 1, 7, 3, 4, 5] if owners == 8 else list(range(1, count))
+    order = [4, 2, 6, 1, 7, 3, 5] if owners == 8 else list(range(1, count))
     lead, place, aims = call(
         functools.partial(place_kernel, owners, capacity, exchange, order[0]),
         [chunk_shape, ((1, rows_dev), jnp.int32), ((AIM_ROWS, rows_dev), BF16)],
@@ -322,16 +331,19 @@
         arrived = {0: chunks[0]}
         for step in order:
             arrived[step] = moved(chunks[step], step)
-        groups = [[0], order[:3], order[3:5], *[[step] for step in order[5:]]]
+        groups = [[0, order[0]], order[1:3], order[3:5], *[[step] for step in order[5:]]]
     else:
         arrived = dict(enumerate(sent_whole([chunks[i] for i in range(count)], owners, capacity, width)))
         groups = [[0], list(range(1, count))]
 
-    total, part, ahead = call(
+    depth = halo_rows.shape[0]
+    lend = halo_rows.reshape(1, -1)
+    total, part, node_ahead, lent_ahead, lent_latent = call(
         first_kernel,
-        [((nodes, width), F32), ((nodes, width), BF16), ((nodes, width), F32)],
-        (weights, other, mesh_latent, arrived[0], biases),
-        [VMEM] * 5,
+        [((nodes, width), F32), ((nodes, width), BF16), ((nodes, width), F32)]
+        + [((depth, width), F32), ((depth, width), BF16)],
+        (weights, other, mesh_latent, lend, biases, *[arrived[i] for i in groups[0]]),
+        [VMEM] * (5 + len(groups[0])),
         flops=5 * 10**8,
         moved=3 * 10**6,
     )
@@ -344,11 +356,11 @@
             flops=4 * 10**8 * len(group),
             moved=2 * 10**6,
         )
-    mid, lent = call(
+    sums, lent = call(
         node_kernel,
-        [((nodes, width), BF16), ((halo_rows.shape[0], width), BF16)],
-        (total, part, ahead, weights, other, biases, gains, mesh_latent)
-        + (halo_rows.reshape(1, -1), *[arrived[i] for i in groups[-1]]),
+        [((nodes, width), BF16), ((depth, width), BF16)],
+        (total, part, lent_ahead, weights, other, biases, gains, lent_latent)
+        + (lend, *[arrived[i] for i in groups[-1]]),
         [VMEM] * (9 + len(groups[-1])),
         flops=10**9,
         moved=3 * 10**6,
@@ -357,24 +369,26 @@
     if lon_count != 2:
         halo.append(shift(lent, "lon", -1))
     sender, receiver = mesh_sender.reshape(1, -1), mesh_receiver.reshape(1, -1)
-    pieces, depth = len(halo), halo_rows.shape[0]
-    pre, ahead, picks, spread = call(
+    pieces = len(halo)
+    mid, pre, ahead, picks, spread = call(
         functools.partial(local_kernel, pieces, depth),
         [
+            ((nodes, width), BF16),
             ((edges, width), F32),
             ((nodes, width), F32),
             ((edges, pieces * depth), BF16),
             ((nodes, edges), BF16),
         ],
-        (mid, edge_latent, sender, receiver, biases, weights, other),
-        [VMEM] * 7,
+        (sums, node_ahead, mesh_latent, edge_latent, sender, receiver)
+        + (biases, gains, weights, other),
+        [VMEM] * 10,
         flops=10**9,
         moved=3 * 10**6,
     )
     (out,) = call(
         process_kernel,
         [((nodes, width), BF16)],
-        (pre, ahead, picks, spread, mid, gains, weights, other, *halo),
+        (pre, ahead, picks, spread, mid, gains, weights, other, halo[1], halo[0], *halo[2:]),
         [VMEM] * (8 + pieces),
         flops=10**9,
         moved=3 * 10**6,

time: 43.8 us -> 42.9 us (0.979)
  waiting for transfers between devices: 14.8 us -> 7.51 us
  starting transfers between devices: 14.8 us -> 20.4 us
  Pallas kernels: 13.9 us -> 14.8 us
    ppermute x7, waiting for transfers between devices: 11.7 us -> 6.43 us  [moved(): return lax.ppermute(value, ('lat', 'lon'), pairs)]
    ppermute x7, starting transfers between devices: 12.1 us -> 16.2 us  [moved(): return lax.ppermute(value, ('lat', 'lon'), pairs)]
    ppermute x2, starting transfers between devices: 1.57 us -> 3.05 us  [paired(): return lax.ppermute(value, axis, pairs)]
    ppermute x2, waiting for transfers between devices: 2.39 us -> 1.07 us  [paired(): return lax.ppermute(value, axis, pairs)]
    pallas_call x9, Pallas kernels: 13.9 us -> 14.8 us  [call(): pl.pallas_call(kernel, out_shape=[jax.ShapeDtypeStruct(shape, kind) for s...]
    ppermute x1, waiting for transfers between devices: 0.66 us -> 0.01 us  [shift(): lax.ppermute(value, axis, [(i, (i + step) % count) for i in range(count)])]
  transfers between devices with their start and end apart: 11 -> 11, of which waited for: 6 -> 3; matrix products, arithmetic and copies ran while one was open for 0% -> 0% of each run, Pallas kernels for 21% -> 24%
where the time goes in v4:
time: 42.9 us; the launch traced here: 42.8 us
  starting transfers between devices  20.4 us (48%)
  Pallas kernels  14.8 us (34%)
  waiting for transfers between devices  7.51 us (18%)
    ppermute x7, starting transfers between devices, moved(): return lax.ppermute(value, ('lat', 'lon'), pairs)  16.2 us
    pallas_call x9, Pallas kernels, call(): pl.pallas_call(kernel, out_shape=[jax.ShapeDtypeStruct(shape, kind) for s...  14.8 us
    ppermute x7, waiting for transfers between devices, moved(): return lax.ppermute(value, ('lat', 'lon'), pairs)  6.43 us
    ppermute x2, starting transfers between devices, paired(): return lax.ppermute(value, axis, pairs)  3.05 us
    ppermute x2, waiting for transfers between devices, paired(): return lax.ppermute(value, axis, pairs)  1.07 us
  transfers between devices with their start and end apart: 11, of which 3 were waited for; matrix products, arithmetic and copies ran while one was open for 0% of the time, Pallas kernels for 24%

profile of v4, /device:TPU:0, one launch (start us, length us, event | category | flops | bytes accessed | tf_op | source)
XLA Modules:
  0.0 42.8 jit_solution(4533239485520364162)
XLA Ops:
  0.0 0.5 %collective-permute-start = (bf16[13,256,512]{2,1,0:T(8,128)(2,1)}, bf16[13,256,512]{2,1,0:T(8,128)(2,1)S(1)}, u32[]{:S(2)}, u32[]{:S(2)}) collective-permute-start(bf16[13,256,512]{2,1,0:T(8,128)(2,1)} %mine.11), channel_id=1, source_target_pairs={{0,1},{1,0},{2,3},{3,2},{4,5},{5,4},{6,7},{7,6},{8,9},{9,8},{10,11... | collective-permute-start | bytes 10223624 | tf_op jit(solution)/shard_map/ppermute | solution.py:234
  0.5 1.5 %shard_map.109 = (bf16[520,128]{1,0:T(8,128)(2,1)S(1)}, s32[1,512]{1,0:T(1,128)S(1)}, bf16[8,512]{1,0:T(8,128)(2,1)S(1)}) custom-call(s32[1,512]{1,0:T(1,128)} %bitcast.10, s32[2,512]{1,0:T(2,128)} %bitcast.9, bf16[512,512]{1,0:T(8,128)(2,1)} %latent_ref.1), custom_call_target="tpu_custom_call" | custom-call | flops 1000000000 | bytes 2000000 | tf_op jit(solution)/shard_map/pallas_call | solution.py:221
  2.0 3.7 %collective-permute-start.1 = (bf16[520,128]{1,0:T(8,128)(2,1)S(1)}, bf16[520,128]{1,0:T(8,128)(2,1)S(1)}, u32[]{:S(2)}, u32[]{:S(2)}) collective-permute-start(bf16[520,128]{1,0:T(8,128)(2,1)S(1)} %get-tuple-element.30), channel_id=1, source_target_pairs={{0,8},{2,10},{4,12},{6,14},{8,0},{10,2},{12,4},{14,6},{1,9},{3,11}... | collective-permute-start | bytes 399368 | tf_op jit(solution)/shard_map/ppermute | solution.py:243
  5.7 0.9 %shard_map.110 = (bf16[520,128]{1,0:T(8,128)(2,1)S(1)}, bf16[520,128]{1,0:T(8,128)(2,1)S(1)}, bf16[520,128]{1,0:T(8,128)(2,1)S(1)}, bf16[520,128]{1,0:T(8,128)(2...) custom-call(s32[1,512]{1,0:T(1,128)S(1)} %get-tuple-element.27.place_ref, ...), custom_call_target="tpu_custom_call" | custom-call | flops 1000000000 | bytes 2000000 | tf_op jit(solution)/shard_map/pallas_call | solution.py:221
  6.6 1.6 %collective-permute-start.2 = (bf16[520,128]{1,0:T(8,128)(2,1)S(1)}, bf16[520,128]{1,0:T(8,128)(2,1)S(1)}, u32[]{:S(2)}, u32[]{:S(2)}) collective-permute-start(bf16[520,128]{1,0:T(8,128)(2,1)S(1)} %get-tuple-element.33), channel_id=1, source_target_pairs={{0,4},{2,6},{4,8},{6,10},{8,12},{10,14},{12,0},{14,2},{1,5},{3,7},... | collective-permute-start | bytes 399368 | tf_op jit(solution)/shard_map/ppermute | solution.py:243
  8.2 2.3 %collective-permute-start.3 = (bf16[520,128]{1,0:T(8,128)(2,1)S(1)}, bf16[520,128]{1,0:T(8,128)(2,1)S(1)}, u32[]{:S(2)}, u32[]{:S(2)}) collective-permute-start(bf16[520,128]{1,0:T(8,128)(2,1)S(1)} %get-tuple-element.34), channel_id=1, source_target_pairs={{0,12},{2,14},{4,0},{6,2},{8,4},{10,6},{12,8},{14,10},{1,13},{3,15... | collective-permute-start | bytes 399368 | tf_op jit(solution)/shard_map/ppermute | solution.py:243
  10.5 1.5 %collective-permute-start.4 = (bf16[520,128]{1,0:T(8,128)(2,1)S(1)}, bf16[520,128]{1,0:T(8,128)(2,1)S(1)}, u32[]{:S(2)}, u32[]{:S(2)}) collective-permute-start(bf16[520,128]{1,0:T(8,128)(2,1)S(1)} %get-tuple-element.35), channel_id=1, source_target_pairs={{0,2},{2,0},{4,6},{6,4},{8,10},{10,8},{12,14},{14,12},{1,3},{3,1},... | collective-permute-start | bytes 399368 | tf_op jit(solution)/shard_map/ppermute | solution.py:243
  12.0 3.9 %collective-permute-done.1.rest_1_ = bf16[520,128]{1,0:T(8,128)(2,1)S(1)} collective-permute-done((bf16[520,128]{1,0:T(8,128)(2,1)S(1)}, bf16[520,128]{1,0:T(8,128)(2,1)S(1)}, u32[]{:S(2)}, u32[]{:S(2)}) %collective-permute-start.1) | collective-permute-done | bytes 133152 | tf_op jit(solution)/shard_map/ppermute | solution.py:243
  15.8 1.9 %collective-permute-start.5 = (bf16[520,128]{1,0:T(8,128)(2,1)S(1)}, bf16[520,128]{1,0:T(8,128)(2,1)S(1)}, u32[]{:S(2)}, u32[]{:S(2)}) collective-permute-start(bf16[520,128]{1,0:T(8,128)(2,1)S(1)} %get-tuple-element.36), channel_id=1, source_target_pairs={{0,14},{2,12},{4,2},{6,0},{8,6},{10,4},{12,10},{14,8},{1,15},{3,13... | collective-permute-start | bytes 399368 | tf_op jit(solution)/shard_map/ppermute | solution.py:243
  17.7 0.0 collective-permute-done.other.rest_3_
  17.7 1.0 %collective-permute-start.6 = (bf16[520,128]{1,0:T(8,128)(2,1)S(1)}, bf16[520,128]{1,0:T(8,128)(2,1)S(1)}, u32[]{:S(2)}, u32[]{:S(2)}) collective-permute-start(bf16[520,128]{1,0:T(8,128)(2,1)S(1)} %get-tuple-element.37), channel_id=1, source_target_pairs={{0,6},{2,4},{4,10},{6,8},{8,14},{10,12},{12,2},{14,0},{1,7},{3,5},... | collective-permute-start | bytes 399368 | tf_op jit(solution)/shard_map/ppermute | solution.py:243
  18.8 1.8 %shard_map.111 = (f32[256,512]{1,0:T(8,128)S(1)}, bf16[256,512]{1,0:T(8,128)(2,1)S(1)}, f32[256,512]{1,0:T(8,128)S(1)}, f32[64,512]{1,0:T(8,128)S(1)}, bf16[64,512]{1,0:T(8,128)(2,1)S(1)}) custom-call(bf16[13,256,512]{2,1,0:T(8,128)(2,1)S(1)} %copy-done, bf16[13,256,512]{2,1,0:T(8,128)(2,1)S(1)} %collective-permute-done.other.rest_3_, ...), custom_call_target="tpu_custom_call" | custom-call | flops 500000000 | bytes 3000000 | tf_op jit(solution)/shard_map/pallas_call | solution.py:221
  20.6 0.0 collective-permute-done.2.rest_0_
  20.6 4.2 %collective-permute-start.7 = (bf16[520,128]{1,0:T(8,128)(2,1)S(1)}, bf16[520,128]{1,0:T(8,128)(2,1)S(1)}, u32[]{:S(2)}, u32[]{:S(2)}) collective-permute-start(bf16[520,128]{1,0:T(8,128)(2,1)S(1)} %get-tuple-element.40), channel_id=1, source_target_pairs={{0,10},{2,8},{4,14},{6,12},{8,2},{10,0},{12,6},{14,4},{1,11},{3,9}... | collective-permute-start | bytes 399368 | tf_op jit(solution)/shard_map/ppermute | solution.py:243
  24.8 0.0 collective-permute-done.3.rest_1_
  24.8 1.4 %shard_map.112.total = f32[256,512]{1,0:T(8,128)S(1)} custom-call(f32[256,512]{1,0:T(8,128)S(1)} %get-tuple-element.31.total, bf16[256,512]{1,0:T(8,128)(2,1)S(1)} %get-tuple-element.32.part, bf16[13,256,512]{2,1,0:T(8,128)(2,1)S(1)} %copy-done, bf16[13,256,512]{2,1,0:T(8,128)(2,1)S(1)} %collective-permute-done.other.rest_3_, f32[4,512]{1,0:T(4,128)S(1)} %copy-done.3, ...), custom_call_target="tpu_custom_call" | custom-call | flops 800000000 | bytes 2000000 | tf_op jit(solution)/shard_map/pallas_call | solution.py:221
  26.2 0.0 collective-permute-done.4.rest_0_
  26.2 0.0 collective-permute-done.5.rest_1_
  26.3 1.4 %shard_map.113.total = f32[256,512]{1,0:T(8,128)S(1)} custom-call(f32[256,512]{1,0:T(8,128)S(1)} %shard_map.112.total, bf16[256,512]{1,0:T(8,128)(2,1)S(1)} %get-tuple-element.32.part, bf16[13,256,512]{2,1,0:T(8,128)(2,1)S(1)} %copy-done, bf16[13,256,512]{2,1,0:T(8,128)(2,1)S(1)} %collective-permute-done.other.rest_3_, f32[4,512]{1,0:T(4,128)S(1)} %copy-done.3, ...), custom_call_target="tpu_custom_call" | custom-call | flops 800000000 | bytes 2000000 | tf_op jit(solution)/shard_map/pallas_call | solution.py:221
  27.6 0.0 copy-start.4
  27.7 0.0 collective-permute-done.6.rest_0_
  27.7 1.0 %shard_map.114.total = f32[256,512]{1,0:T(8,128)S(1)} custom-call(f32[256,512]{1,0:T(8,128)S(1)} %shard_map.113.total, bf16[256,512]{1,0:T(8,128)(2,1)S(1)} %get-tuple-element.32.part, bf16[13,256,512]{2,1,0:T(8,128)(2,1)S(1)} %copy-done, bf16[13,256,512]{2,1,0:T(8,128)(2,1)S(1)} %collective-permute-done.other.rest_3_, f32[4,512]{1,0:T(4,128)S(1)} %copy-done.3, ...), custom_call_target="tpu_custom_call" | custom-call | flops 400000000 | bytes 2000000 | tf_op jit(solution)/shard_map/pallas_call | solution.py:221
  28.7 2.5 %collective-permute-done.7.rest_0_ = bf16[520,128]{1,0:T(8,128)(2,1)S(1)} collective-permute-done((bf16[520,128]{1,0:T(8,128)(2,1)S(1)}, bf16[520,128]{1,0:T(8,128)(2,1)S(1)}, u32[]{:S(2)}, u32[]{:S(2)}) %collective-permute-start.7) | collective-permute-done | bytes 133152 | tf_op jit(solution)/shard_map/ppermute | solution.py:243
  31.3 1.7 %shard_map.115 = (bf16[256,512]{1,0:T(8,128)(2,1)S(1)}, bf16[64,512]{1,0:T(8,128)(2,1)S(1)}) custom-call(f32[256,512]{1,0:T(8,128)S(1)} %shard_map.114.total, bf16[256,512]{1,0:T(8,128)(2,1)S(1)} %get-tuple-element.32.part, f32[64,512]{1,0:T(8,128)S(1)} %get-tuple-element.38.ahead, bf16[13,256,512]{2,1,0:T(8,128)(2,1)S(1)} %copy-done, ...), custom_call_target="tpu_custom_call" | custom-call | flops 1000000000 | bytes 3000000 | tf_op jit(solution)/shard_map/pallas_call | solution.py:221
  33.0 0.7 %collective-permute-start.10 = (bf16[64,512]{1,0:T(8,128)(2,1)S(1)}, bf16[64,512]{1,0:T(8,128)(2,1)S(1)}, u32[]{:S(2)}, u32[]{:S(2)}) collective-permute-start(bf16[64,512]{1,0:T(8,128)(2,1)S(1)} %get-tuple-element.48), channel_id=1, source_target_pairs={{0,2},{2,0},{1,3},{3,1},{4,6},{6,4},{5,7},{7,5},{8,10},{10,8},{9,1... | collective-permute-start | bytes 196616 | tf_op jit(solution)/shard_map/ppermute | solution.py:248
  33.6 0.3 collective-permute-start.8
  33.9 2.8 %collective-permute-start.9 = (bf16[64,512]{1,0:T(8,128)(2,1)S(1)}, bf16[64,512]{1,0:T(8,128)(2,1)S(1)}, u32[]{:S(2)}, u32[]{:S(2)}) collective-permute-start(bf16[64,512]{1,0:T(8,128)(2,1)S(1)} %get-tuple-element.48), channel_id=1, source_target_pairs={{4,8},{8,4},{12,0},{0,12},{5,9},{9,5},{13,1},{1,13},{6,10},{10,6},... | collective-permute-start | bytes 196616 | tf_op jit(solution)/shard_map/ppermute | solution.py:257
  36.7 2.3 %shard_map.116 = (bf16[256,512]{1,0:T(8,128)(2,1)S(1)}, f32[512,512]{1,0:T(8,128)S(1)}, f32[256,512]{1,0:T(8,128)S(1)}, bf16[512,192]{1,0:T(8,128)(2,1)S(1)}, bf16[256,512]{1,0:T(8,128)(2,1)S(1)}) custom-call(bf16[256,512]{1,0:T(8,128)(2,1)S(1)} %get-tuple-element.41.sums, f32[256,512]{1,0:T(8,128)S(1)} %get-tuple-element.42.node_ahead, ...), custom_call_target="tpu_custom_call" | custom-call | flops 1000000000 | bytes 3000000 | tf_op jit(solution)/shard_map/pallas_call | solution.py:221
  38.9 0.0 collective-permute-done.10.rest_2_
  38.9 0.0 collective-permute-done.8.rest_0_
  39.0 1.1 %collective-permute-done.9.rest_1_ = bf16[64,512]{1,0:T(8,128)(2,1)S(1)} collective-permute-done((bf16[64,512]{1,0:T(8,128)(2,1)S(1)}, bf16[64,512]{1,0:T(8,128)(2,1)S(1)}, u32[]{:S(2)}, u32[]{:S(2)}) %collective-permute-start.9) | collective-permute-done | bytes 65568 | tf_op jit(solution)/shard_map/ppermute | solution.py:257
  40.0 2.8 %shard_map.117 = bf16[256,512]{1,0:T(8,128)(2,1)} custom-call(f32[512,512]{1,0:T(8,128)S(1)} %get-tuple-element.43.pre, f32[256,512]{1,0:T(8,128)S(1)} %get-tuple-element.44.ahead, bf16[512,192]{1,0:T(8,128)(2,1)S(1)} %get-tuple-element.45.picks, bf16[256,512]{1,0:T(8,128)(2,1)S(1)} %get-tuple-element.46.spread, bf16[256,512]{1,0:T(8,128)(2,1)S(1)} %get-tuple-element.47.mid, ...), custom_call_target="tpu_custom_call" | custom-call | flops 1000000000 | bytes 3000000 | tf_op jit(solution)/shard_map/pallas_call | solution.py:221
  (17 shorter events, 0.0 us)
Async XLA Ops:
  0.0 5.7 %copy-start.8 = (bf16[512,512]{1,0:T(8,128)(2,1)S(1)}, bf16[512,512]{1,0:T(8,128)(2,1)}, u32[]{:S(2)}) copy-start(bf16[512,512]{1,0:T(8,128)(2,1)} %latent_ref.1) | copy-start | bytes 1572868
  0.0 17.7 %collective-permute-start = (bf16[13,256,512]{2,1,0:T(8,128)(2,1)}, bf16[13,256,512]{2,1,0:T(8,128)(2,1)S(1)}, u32[]{:S(2)}, u32[]{:S(2)}) collective-permute-start(bf16[13,256,512]{2,1,0:T(8,128)(2,1)} %mine.11), channel_id=1, source_target_pairs={{0,1},{1,0},{2,3},{3,2},{4,5},{5,4},{6,7},{7,6},{8,9},{9,8},{10,11... | collective-permute-start | bytes 10223624 | tf_op jit(solution)/shard_map/ppermute | solution.py:234
  0.5 18.3 %copy-start = (bf16[13,256,512]{2,1,0:T(8,128)(2,1)S(1)}, bf16[13,256,512]{2,1,0:T(8,128)(2,1)}, u32[]{:S(2)}) copy-start(bf16[13,256,512]{2,1,0:T(8,128)(2,1)} %mine.11) | copy-start | bytes 10223620
  0.5 18.3 %copy-start.1 = (bf16[256,512]{1,0:T(8,128)(2,1)S(1)}, bf16[256,512]{1,0:T(8,128)(2,1)}, u32[]{:S(2)}) copy-start(bf16[256,512]{1,0:T(8,128)(2,1)} %mesh.3) | copy-start | bytes 786436
  0.5 18.3 %copy-start.3 = (f32[4,512]{1,0:T(4,128)S(1)}, f32[4,512]{1,0:T(4,128)}, u32[]{:S(2)}) copy-start(f32[4,512]{1,0:T(4,128)} %rest_0_.1) | copy-start | bytes 24580
  0.5 18.3 %copy-start.5 = (s32[64]{0:T(128)S(1)}, s32[64]{0:T(128)}, u32[]{:S(2)}) copy-start(s32[64]{0:T(128)} %param.18) | copy-start | bytes 772
  2.0 13.8 %collective-permute-start.1 = (bf16[520,128]{1,0:T(8,128)(2,1)S(1)}, bf16[520,128]{1,0:T(8,128)(2,1)S(1)}, u32[]{:S(2)}, u32[]{:S(2)}) collective-permute-start(bf16[520,128]{1,0:T(8,128)(2,1)S(1)} %get-tuple-element.30), channel_id=1, source_target_pairs={{0,8},{2,10},{4,12},{6,14},{8,0},{10,2},{12,4},{14,6},{1,9},{3,11}... | collective-permute-start | bytes 399368 | tf_op jit(solution)/shard_map/ppermute | solution.py:243
  6.6 14.0 %collective-permute-start.2 = (bf16[520,128]{1,0:T(8,128)(2,1)S(1)}, bf16[520,128]{1,0:T(8,128)(2,1)S(1)}, u32[]{:S(2)}, u32[]{:S(2)}) collective-permute-start(bf16[520,128]{1,0:T(8,128)(2,1)S(1)} %get-tuple-element.33), channel_id=1, source_target_pairs={{0,4},{2,6},{4,8},{6,10},{8,12},{10,14},{12,0},{14,2},{1,5},{3,7},... | collective-permute-start | bytes 399368 | tf_op jit(solution)/shard_map/ppermute | solution.py:243
  8.2 16.6 %collective-permute-start.3 = (bf16[520,128]{1,0:T(8,128)(2,1)S(1)}, bf16[520,128]{1,0:T(8,128)(2,1)S(1)}, u32[]{:S(2)}, u32[]{:S(2)}) collective-permute-start(bf16[520,128]{1,0:T(8,128)(2,1)S(1)} %get-tuple-element.34), channel_id=1, source_target_pairs={{0,12},{2,14},{4,0},{6,2},{8,4},{10,6},{12,8},{14,10},{1,13},{3,15... | collective-permute-start | bytes 399368 | tf_op jit(solution)/shard_map/ppermute | solution.py:243
  10.5 15.8 %collective-permute-start.4 = (bf16[520,128]{1,0:T(8,128)(2,1)S(1)}, bf16[520,128]{1,0:T(8,128)(2,1)S(1)}, u32[]{:S(2)}, u32[]{:S(2)}) collective-permute-start(bf16[520,128]{1,0:T(8,128)(2,1)S(1)} %get-tuple-element.35), channel_id=1, source_target_pairs={{0,2},{2,0},{4,6},{6,4},{8,10},{10,8},{12,14},{14,12},{1,3},{3,1},... | collective-permute-start | bytes 399368 | tf_op jit(solution)/shard_map/ppermute | solution.py:243
  15.8 10.4 %collective-permute-start.5 = (bf16[520,128]{1,0:T(8,128)(2,1)S(1)}, bf16[520,128]{1,0:T(8,128)(2,1)S(1)}, u32[]{:S(2)}, u32[]{:S(2)}) collective-permute-start(bf16[520,128]{1,0:T(8,128)(2,1)S(1)} %get-tuple-element.36), channel_id=1, source_target_pairs={{0,14},{2,12},{4,2},{6,0},{8,6},{10,4},{12,10},{14,8},{1,15},{3,13... | collective-permute-start | bytes 399368 | tf_op jit(solution)/shard_map/ppermute | solution.py:243
  17.7 9.9 %collective-permute-start.6 = (bf16[520,128]{1,0:T(8,128)(2,1)S(1)}, bf16[520,128]{1,0:T(8,128)(2,1)S(1)}, u32[]{:S(2)}, u32[]{:S(2)}) collective-permute-start(bf16[520,128]{1,0:T(8,128)(2,1)S(1)} %get-tuple-element.37), channel_id=1, source_target_pairs={{0,6},{2,4},{4,10},{6,8},{8,14},{10,12},{12,2},{14,0},{1,7},{3,5},... | collective-permute-start | bytes 399368 | tf_op jit(solution)/shard_map/ppermute | solution.py:243
  20.6 10.6 %collective-permute-start.7 = (bf16[520,128]{1,0:T(8,128)(2,1)S(1)}, bf16[520,128]{1,0:T(8,128)(2,1)S(1)}, u32[]{:S(2)}, u32[]{:S(2)}) collective-permute-start(bf16[520,128]{1,0:T(8,128)(2,1)S(1)} %get-tuple-element.40), channel_id=1, source_target_pairs={{0,10},{2,8},{4,14},{6,12},{8,2},{10,0},{12,6},{14,4},{1,11},{3,9}... | collective-permute-start | bytes 399368 | tf_op jit(solution)/shard_map/ppermute | solution.py:243
  27.6 3.6 %copy-start.4 = (f32[4,512]{1,0:T(4,128)S(1)}, f32[4,512]{1,0:T(4,128)}, u32[]{:S(2)}) copy-start(f32[4,512]{1,0:T(4,128)} %gains.3) | copy-start | bytes 24580
  31.2 5.4 %copy-start.2 = (bf16[512,512]{1,0:T(8,128)(2,1)S(1)}, bf16[512,512]{1,0:T(8,128)(2,1)}, u32[]{:S(2)}) copy-start(bf16[512,512]{1,0:T(8,128)(2,1)} %edges.1) | copy-start | bytes 1572868
  31.2 5.4 %copy-start.6 = (s32[512]{0:T(512)S(1)}, s32[512]{0:T(512)}, u32[]{:S(2)}) copy-start(s32[512]{0:T(512)} %param.16) | copy-start | bytes 6148
  31.2 5.4 %copy-start.7 = (s32[512]{0:T(512)S(1)}, s32[512]{0:T(512)}, u32[]{:S(2)}) copy-start(s32[512]{0:T(512)} %param.17) | copy-start | bytes 6148
  33.0 6.0 %collective-permute-start.10 = (bf16[64,512]{1,0:T(8,128)(2,1)S(1)}, bf16[64,512]{1,0:T(8,128)(2,1)S(1)}, u32[]{:S(2)}, u32[]{:S(2)}) collective-permute-start(bf16[64,512]{1,0:T(8,128)(2,1)S(1)} %get-tuple-element.48), channel_id=1, source_target_pairs={{0,2},{2,0},{1,3},{3,1},{4,6},{6,4},{5,7},{7,5},{8,10},{10,8},{9,1... | collective-permute-start | bytes 196616 | tf_op jit(solution)/shard_map/ppermute | solution.py:248
  33.6 5.3 %collective-permute-start.8 = (bf16[64,512]{1,0:T(8,128)(2,1)S(1)}, bf16[64,512]{1,0:T(8,128)(2,1)S(1)}, u32[]{:S(2)}, u32[]{:S(2)}) collective-permute-start(bf16[64,512]{1,0:T(8,128)(2,1)S(1)} %get-tuple-element.48), channel_id=1, source_target_pairs={{0,4},{4,0},{8,12},{12,8},{1,5},{5,1},{9,13},{13,9},{2,6},{6,2},{1... | collective-permute-start | bytes 196616 | tf_op jit(solution)/shard_map/ppermute | solution.py:257
  33.9 6.1 %collective-permute-start.9 = (bf16[64,512]{1,0:T(8,128)(2,1)S(1)}, bf16[64,512]{1,0:T(8,128)(2,1)S(1)}, u32[]{:S(2)}, u32[]{:S(2)}) collective-permute-start(bf16[64,512]{1,0:T(8,128)(2,1)S(1)} %get-tuple-element.48), channel_id=1, source_target_pairs={{4,8},{8,4},{12,0},{0,12},{5,9},{9,5},{13,1},{1,13},{6,10},{10,6},... | collective-permute-start | bytes 196616 | tf_op jit(solution)/shard_map/ppermute | solution.py:257

commit v5 on v4

--- a/solution.py
+++ b/solution.py
@@ -13,6 +13,7 @@
 F32 = jnp.float32
 BF16 = jnp.bfloat16
 HBM = pl.BlockSpec(memory_space=pltpu.HBM)
+ANY = pl.BlockSpec(memory_space=pl.ANY)
 VMEM = pl.BlockSpec(memory_space=pltpu.VMEM)
 VMEM_LIMIT = 24 * 1024 * 1024
 
@@ -114,13 +115,14 @@
     packed(place, aims, latent_ref[...], base_of(step, capacity, exchange), out)
 
 
-def dispatch_kernel(capacity, exchange, steps, place_ref, aims_ref, latent_ref, *outs):
+def dispatch_kernel(capacity, exchange, steps, place_ref, aims_ref, latent_ref, after, *outs):
+    del after
     place, aims, latent = place_ref[...], aims_ref[...], latent_ref[...]
     for step, out in zip(steps, outs):
         packed(place, aims, latent, base_of(step, capacity, exchange), out)
 
 
-def encode(chunks, maps, mesh_part, bias):
+def messages(chunks, maps, mesh_part, bias):
     nodes, width = mesh_part.shape
     rows = jnp.concatenate(
         [
@@ -142,7 +144,19 @@
         [down(line[k : k + 1, :], nodes) for k in range(2) for line in lines], axis=1
     )
     hidden = silu(jnp.concatenate([part, part], axis=0) + mm(picks, mesh_part))
-    return mm(spread, normed(through(hidden, maps, 2)).astype(BF16))
+    return spread, normed(through(hidden, maps, 2)).astype(BF16)
+
+
+def encode(chunks, maps, mesh_part, bias):
+    return mm(*messages(chunks, maps, mesh_part, bias))
+
+
+def rows_of(picks, values):
+    parts = []
+    for _ in range(3):
+        parts.append(values.astype(BF16))
+        values = values - parts[-1].astype(F32)
+    return sum(mm(picks, part) for part in parts)
 
 
 def first_kernel(mine, other, mesh, lend, biases, *rest):
@@ -163,15 +177,23 @@
     out[...] = total[...] + encode(chunks, (mine, other), part[...], biases[0:1, :])
 
 
-def node_kernel(total, part, ahead, mine, other, biases, gains, mesh, lend, *rest):
-    *chunks, sums_out, lent_out = rest
+def last_kernel(total, part, mine, other, biases, lend, *rest):
+    *chunks, out, lent_out = rest
+    sums = total[...] + encode(chunks, (mine, other), part[...], biases[0:1, :])
+    out[...] = sums
+    lent_out[...] = rows_of(along(turned(lend[...]), sums.shape[0]), sums)
+
+
+def node_kernel(lent_total, part, ahead, mine, other, biases, gains, latent, lend, *rest):
+    *chunks, spread_out, notes_out, lent_out = rest
     maps = (mine, other)
-    sums = total[...] + encode(chunks, maps, part[...], biases[0:1, :])
-    sums = (sums * gains[0:1, :]).astype(BF16)
-    sums_out[...] = sums
-    picks = along(turned(lend[...]), sums.shape[0])
-    lent = mm(picks, sums).astype(BF16)
-    lent_out[...] = updated(ahead[...], lent, mesh[...], maps, gains)
+    spread, notes = messages(chunks, maps, part[...], biases[0:1, :])
+    spread_out[...] = spread
+    notes_out[...] = notes
+    lent_spread = mm(along(turned(lend[...]), spread.shape[0]), spread).astype(BF16)
+    sums = ((lent_total[...] + mm(lent_spread, notes)) * gains[0:1, :]).astype(BF16)
+    mid = updated(ahead[...], sums, latent[...], maps, gains)
+    lent_out[...] = through(mid, maps, 7).astype(BF16)
 
 
 def updated(ahead, sums, latent, maps, gains):
@@ -180,10 +202,11 @@
     return (latent.astype(F32) + change).astype(BF16)
 
 
-def local_kernel(pieces, depth, sums, node_ahead, mesh, edges, sender, receiver, *rest):
+def local_kernel(pieces, depth, total, spread, notes, node_ahead, mesh, edges, sender, receiver, *rest):
     biases, gains, mine, other, mid_out, pre_out, ahead_out, picks_out, spread_out = rest
     maps = (mine, other)
-    mid = updated(node_ahead[...], sums[...], mesh[...], maps, gains)
+    sums = ((total[...] + mm(spread[...], notes[...])) * gains[0:1, :]).astype(BF16)
+    mid = updated(node_ahead[...], sums, mesh[...], maps, gains)
     mid_out[...] = mid
     nodes = mid.shape[0]
     number = sender[...]
@@ -208,7 +231,7 @@
     lent = [lent[1], lent[0], *lent[2:]]
     maps = (mine, other)
     table = jnp.concatenate([ref[...] for ref in lent], axis=0)
-    hidden = silu(pre[...] + mm(picks[...], through(table, maps, 7).astype(BF16)))
+    hidden = silu(pre[...] + mm(picks[...], table))
     notes = normed(through(hidden, maps, 9)).astype(BF16)
     processed = (mm(spread[...], notes) * gains[2:3, :]).astype(BF16)
     hidden = silu(ahead[...] + through(processed, maps, 11))
@@ -316,25 +339,26 @@
         flops=10**9,
         moved=2 * 10**6,
     )
-    others = [*order[1:], 0]
     chunks = {order[0]: lead}
-    rest = call(
-        functools.partial(dispatch_kernel, capacity, exchange, others),
-        [chunk_shape] * len(others),
-        (place, aims, grid_latent),
-        [VMEM] * 3,
-        flops=10**9,
-        moved=2 * 10**6,
-    )
-    chunks.update(zip(others, rest))
+    early, late = order[1:4], [*order[4:], 0]
+    for steps, after in ((early, aims), (late, other)):
+        made = call(
+            functools.partial(dispatch_kernel, capacity, exchange, steps),
+            [chunk_shape] * len(steps),
+            (place, aims, grid_latent, after),
+            [VMEM] * 3 + [ANY],
+            flops=10**9,
+            moved=2 * 10**6,
+        )
+        chunks.update(zip(steps, made))
     if exchange:
         arrived = {0: chunks[0]}
         for step in order:
             arrived[step] = moved(chunks[step], step)
-        groups = [[0, order[0]], order[1:3], order[3:5], *[[step] for step in order[5:]]]
+        groups = [[0, 4], [2, 6], [1, 7], [3], [5]]
     else:
         arrived = dict(enumerate(sent_whole([chunks[i] for i in range(count)], owners, capacity, width)))
-        groups = [[0], list(range(1, count))]
+        groups = [[0], [1], list(range(2, count))]
 
     depth = halo_rows.shape[0]
     lend = halo_rows.reshape(1, -1)
@@ -347,7 +371,7 @@
         flops=5 * 10**8,
         moved=3 * 10**6,
     )
-    for group in groups[1:-1]:
+    for group in groups[1:-2]:
         (total,) = call(
             more_kernel,
             [((nodes, width), F32)],
@@ -356,10 +380,19 @@
             flops=4 * 10**8 * len(group),
             moved=2 * 10**6,
         )
-    sums, lent = call(
+    total, lent_total = call(
+        last_kernel,
+        [((nodes, width), F32), ((depth, width), F32)],
+        (total, part, weights, other, biases, lend, *[arrived[i] for i in groups[-2]]),
+        [VMEM] * (6 + len(groups[-2])),
+        flops=10**9,
+        moved=2 * 10**6,
+    )
+    last_edges = 2 * LANES * len(groups[-1])
+    spread, notes, lent = call(
         node_kernel,
-        [((nodes, width), BF16), ((depth, width), BF16)],
-        (total, part, lent_ahead, weights, other, biases, gains, lent_latent)
+        [((nodes, last_edges), BF16), ((last_edges, width), BF16), ((depth, width), BF16)],
+        (lent_total, part, lent_ahead, weights, other, biases, gains, lent_latent)
         + (lend, *[arrived[i] for i in groups[-1]]),
         [VMEM] * (9 + len(groups[-1])),
         flops=10**9,
@@ -379,9 +412,9 @@
             ((edges, pieces * depth), BF16),
             ((nodes, edges), BF16),
         ],
-        (sums, node_ahead, mesh_latent, edge_latent, sender, receiver)
+        (total, spread, notes, node_ahead, mesh_latent, edge_latent, sender, receiver)
         + (biases, gains, weights, other),
-        [VMEM] * 10,
+        [VMEM] * 12,
         flops=10**9,
         moved=3 * 10**6,
     )

time: 42.9 us -> 42.6 us (level)
  waiting for transfers between devices: 7.51 us -> 6.4 us
  starting transfers between devices: 20.4 us -> 21 us
    ppermute x7, waiting for transfers between devices: 6.43 us -> 5.31 us  [moved(): return lax.ppermute(value, ('lat', 'lon'), pairs)]
    ppermute x7, starting transfers between devices: 16.2 us -> 17.1 us  [moved(): return lax.ppermute(value, ('lat', 'lon'), pairs)]
    pallas_call x9 -> x10, Pallas kernels: 14.8 us -> 14.9 us  [call(): pl.pallas_call(kernel, out_shape=[jax.ShapeDtypeStruct(shape, kind) for s...]
  transfers between devices with their start and end apart: 11 -> 11, of which waited for: 3 -> 3; matrix products, arithmetic and copies ran while one was open for 0% -> 0% of each run, Pallas kernels for 24% -> 25%
where the time goes in v5:
time: 42.6 us; the launch traced here: 42.5 us
  starting transfers between devices  21 us (49%)
  Pallas kernels  14.9 us (35%)
  waiting for transfers between devices  6.4 us (15%)
    ppermute x7, starting transfers between devices, moved(): return lax.ppermute(value, ('lat', 'lon'), pairs)  17.1 us
    pallas_call x10, Pallas kernels, call(): pl.pallas_call(kernel, out_shape=[jax.ShapeDtypeStruct(shape, kind) for s...  14.9 us
    ppermute x7, waiting for transfers between devices, moved(): return lax.ppermute(value, ('lat', 'lon'), pairs)  5.31 us
    ppermute x2, starting transfers between devices, paired(): return lax.ppermute(value, axis, pairs)  2.83 us
    ppermute x2, waiting for transfers between devices, paired(): return lax.ppermute(value, axis, pairs)  1.09 us
  transfers between devices with their start and end apart: 11, of which 3 were waited for; matrix products, arithmetic and copies ran while one was open for 0% of the time, Pallas kernels for 25%

profile of v5, /device:TPU:0, one launch (start us, length us, event | category | flops | bytes accessed | tf_op | source)
XLA Modules:
  0.0 42.5 jit_solution(3406636309313681331)
XLA Ops:
  0.0 0.5 %collective-permute-start = (bf16[13,256,512]{2,1,0:T(8,128)(2,1)}, bf16[13,256,512]{2,1,0:T(8,128)(2,1)S(1)}, u32[]{:S(2)}, u32[]{:S(2)}) collective-permute-start(bf16[13,256,512]{2,1,0:T(8,128)(2,1)} %mine.11), channel_id=1, source_target_pairs={{0,1},{1,0},{2,3},{3,2},{4,5},{5,4},{6,7},{7,6},{8,9},{9,8},{10,11... | collective-permute-start | bytes 10223624 | tf_op jit(solution)/shard_map/ppermute | solution.py:257
  0.5 1.4 %shard_map.109 = (bf16[520,128]{1,0:T(8,128)(2,1)S(1)}, s32[1,512]{1,0:T(1,128)S(1)}, bf16[8,512]{1,0:T(8,128)(2,1)S(1)}) custom-call(s32[1,512]{1,0:T(1,128)} %bitcast.11, s32[2,512]{1,0:T(2,128)} %bitcast.10, bf16[512,512]{1,0:T(8,128)(2,1)} %latent_ref.3), custom_call_target="tpu_custom_call" | custom-call | flops 1000000000 | bytes 2000000 | tf_op jit(solution)/shard_map/pallas_call | solution.py:244
  1.8 3.7 %collective-permute-start.1 = (bf16[520,128]{1,0:T(8,128)(2,1)S(1)}, bf16[520,128]{1,0:T(8,128)(2,1)S(1)}, u32[]{:S(2)}, u32[]{:S(2)}) collective-permute-start(bf16[520,128]{1,0:T(8,128)(2,1)S(1)} %get-tuple-element.33), channel_id=1, source_target_pairs={{0,8},{2,10},{4,12},{6,14},{8,0},{10,2},{12,4},{14,6},{1,9},{3,11}... | collective-permute-start | bytes 399368 | tf_op jit(solution)/shard_map/ppermute | solution.py:266
  5.6 0.0 copy-start.6
  5.6 0.5 %shard_map.112 = (bf16[520,128]{1,0:T(8,128)(2,1)S(1)}, bf16[520,128]{1,0:T(8,128)(2,1)S(1)}, bf16[520,128]{1,0:T(8,128)(2,1)S(1)}) custom-call(s32[1,512]{1,0:T(1,128)S(1)} %get-tuple-element.30.place_ref, bf16[8,512]{1,0:T(8,128)(2,1)S(1)} %get-tuple-element.31.aims_ref.after, bf16[512,512]{1,0:T(8,128)(2,1)S(1)} %copy-done.2, ...), custom_call_target="tpu_custom_call" | custom-call | flops 1000000000 | bytes 2000000 | tf_op jit(solution)/shard_map/pallas_call | solution.py:244
  6.0 1.6 %collective-permute-start.2 = (bf16[520,128]{1,0:T(8,128)(2,1)S(1)}, bf16[520,128]{1,0:T(8,128)(2,1)S(1)}, u32[]{:S(2)}, u32[]{:S(2)}) collective-permute-start(bf16[520,128]{1,0:T(8,128)(2,1)S(1)} %get-tuple-element.36), channel_id=1, source_target_pairs={{0,4},{2,6},{4,8},{6,10},{8,12},{10,14},{12,0},{14,2},{1,5},{3,7},... | collective-permute-start | bytes 399368 | tf_op jit(solution)/shard_map/ppermute | solution.py:266
  7.7 2.2 %collective-permute-start.3 = (bf16[520,128]{1,0:T(8,128)(2,1)S(1)}, bf16[520,128]{1,0:T(8,128)(2,1)S(1)}, u32[]{:S(2)}, u32[]{:S(2)}) collective-permute-start(bf16[520,128]{1,0:T(8,128)(2,1)S(1)} %get-tuple-element.37), channel_id=1, source_target_pairs={{0,12},{2,14},{4,0},{6,2},{8,4},{10,6},{12,8},{14,10},{1,13},{3,15... | collective-permute-start | bytes 399368 | tf_op jit(solution)/shard_map/ppermute | solution.py:266
  9.9 1.5 %collective-permute-start.4 = (bf16[520,128]{1,0:T(8,128)(2,1)S(1)}, bf16[520,128]{1,0:T(8,128)(2,1)S(1)}, u32[]{:S(2)}, u32[]{:S(2)}) collective-permute-start(bf16[520,128]{1,0:T(8,128)(2,1)S(1)} %get-tuple-element.38), channel_id=1, source_target_pairs={{0,2},{2,0},{4,6},{6,4},{8,10},{10,8},{12,14},{14,12},{1,3},{3,1},... | collective-permute-start | bytes 399368 | tf_op jit(solution)/shard_map/ppermute | solution.py:266
  11.4 0.0 collective-permute-done.after.other.rest_3_
  11.4 0.6 %shard_map.110 = (bf16[520,128]{1,0:T(8,128)(2,1)S(1)}, bf16[520,128]{1,0:T(8,128)(2,1)S(1)}, bf16[520,128]{1,0:T(8,128)(2,1)S(1)}, bf16[520,128]{1,0:T(8,128)(2,1)S(1)}) custom-call(s32[1,512]{1,0:T(1,128)S(1)} %get-tuple-element.30.place_ref, bf16[8,512]{1,0:T(8,128)(2,1)S(1)} %get-tuple-element.31.aims_ref.after, bf16[512,512]{1,0:T(8,128)(2,1)S(1)} %copy-done.2, ...), custom_call_target="tpu_custom_call" | custom-call | flops 1000000000 | bytes 2000000 | tf_op jit(solution)/shard_map/pallas_call | solution.py:244
  12.0 0.9 %collective-permute-start.5 = (bf16[520,128]{1,0:T(8,128)(2,1)S(1)}, bf16[520,128]{1,0:T(8,128)(2,1)S(1)}, u32[]{:S(2)}, u32[]{:S(2)}) collective-permute-start(bf16[520,128]{1,0:T(8,128)(2,1)S(1)} %get-tuple-element.39), channel_id=1, source_target_pairs={{0,14},{2,12},{4,2},{6,0},{8,6},{10,4},{12,10},{14,8},{1,15},{3,13... | collective-permute-start | bytes 399368 | tf_op jit(solution)/shard_map/ppermute | solution.py:266
  12.9 2.8 %collective-permute-done.1.rest_1_ = bf16[520,128]{1,0:T(8,128)(2,1)S(1)} collective-permute-done((bf16[520,128]{1,0:T(8,128)(2,1)S(1)}, bf16[520,128]{1,0:T(8,128)(2,1)S(1)}, u32[]{:S(2)}, u32[]{:S(2)}) %collective-permute-start.1) | collective-permute-done | bytes 133152 | tf_op jit(solution)/shard_map/ppermute | solution.py:266
  15.7 0.0 collective-permute-start.6
  15.7 1.8 %shard_map.111 = (f32[256,512]{1,0:T(8,128)S(1)}, bf16[256,512]{1,0:T(8,128)(2,1)S(1)}, f32[256,512]{1,0:T(8,128)S(1)}, f32[64,512]{1,0:T(8,128)S(1)}, bf16[64,512]{1,0:T(8,128)(2,1)S(1)}) custom-call(bf16[13,256,512]{2,1,0:T(8,128)(2,1)S(1)} %copy-done, bf16[13,256,512]{2,1,0:T(8,128)(2,1)S(1)} %collective-permute-done.after.other.rest_3_, ...), custom_call_target="tpu_custom_call" | custom-call | flops 500000000 | bytes 3000000 | tf_op jit(solution)/shard_map/pallas_call | solution.py:244
  17.6 0.0 collective-permute-done.2.rest_0_
  17.6 7.1 %collective-permute-start.7 = (bf16[520,128]{1,0:T(8,128)(2,1)S(1)}, bf16[520,128]{1,0:T(8,128)(2,1)S(1)}, u32[]{:S(2)}, u32[]{:S(2)}) collective-permute-start(bf16[520,128]{1,0:T(8,128)(2,1)S(1)} %get-tuple-element.45), channel_id=1, source_target_pairs={{0,10},{2,8},{4,14},{6,12},{8,2},{10,0},{12,6},{14,4},{1,11},{3,9}... | collective-permute-start | bytes 399368 | tf_op jit(solution)/shard_map/ppermute | solution.py:266
  24.7 0.0 collective-permute-done.3.rest_1_
  24.7 1.4 %shard_map.113.total = f32[256,512]{1,0:T(8,128)S(1)} custom-call(f32[256,512]{1,0:T(8,128)S(1)} %get-tuple-element.34.total, bf16[256,512]{1,0:T(8,128)(2,1)S(1)} %get-tuple-element.35.part, bf16[13,256,512]{2,1,0:T(8,128)(2,1)S(1)} %copy-done, bf16[13,256,512]{2,1,0:T(8,128)(2,1)S(1)} %collective-permute-done.after.other.rest_3_, f32[4,512]{1,0:T(4,128)S(1)} %copy-done.4, ...), custom_call_target="tpu_custom_call" | custom-call | flops 800000000 | bytes 2000000 | tf_op jit(solution)/shard_map/pallas_call | solution.py:244
  26.1 0.0 collective-permute-done.4.rest_0_
  26.1 0.0 collective-permute-done.5.rest_1_
  26.1 1.4 %shard_map.114.total = f32[256,512]{1,0:T(8,128)S(1)} custom-call(f32[256,512]{1,0:T(8,128)S(1)} %shard_map.113.total, bf16[256,512]{1,0:T(8,128)(2,1)S(1)} %get-tuple-element.35.part, bf16[13,256,512]{2,1,0:T(8,128)(2,1)S(1)} %copy-done, bf16[13,256,512]{2,1,0:T(8,128)(2,1)S(1)} %collective-permute-done.after.other.rest_3_, f32[4,512]{1,0:T(4,128)S(1)} %copy-done.4, ...), custom_call_target="tpu_custom_call" | custom-call | flops 800000000 | bytes 2000000 | tf_op jit(solution)/shard_map/pallas_call | solution.py:244
  27.5 0.0 copy-start.5
  27.5 1.3 %shard_map.115 = (f32[256,512]{1,0:T(8,128)S(1)}, f32[64,512]{1,0:T(8,128)S(1)}) custom-call(f32[256,512]{1,0:T(8,128)S(1)} %shard_map.114.total, bf16[256,512]{1,0:T(8,128)(2,1)S(1)} %get-tuple-element.35.part, bf16[13,256,512]{2,1,0:T(8,128)(2,1)S(1)} %copy-done, bf16[13,256,512]{2,1,0:T(8,128)(2,1)S(1)} %collective-permute-done.after.other.rest_3_, ...), custom_call_target="tpu_custom_call" | custom-call | flops 1000000000 | bytes 2000000 | tf_op jit(solution)/shard_map/pallas_call | solution.py:244
  28.8 2.5 %collective-permute-done.7.rest_0_ = bf16[520,128]{1,0:T(8,128)(2,1)S(1)} collective-permute-done((bf16[520,128]{1,0:T(8,128)(2,1)S(1)}, bf16[520,128]{1,0:T(8,128)(2,1)S(1)}, u32[]{:S(2)}, u32[]{:S(2)}) %collective-permute-start.7) | collective-permute-done | bytes 133152 | tf_op jit(solution)/shard_map/ppermute | solution.py:266
  31.3 1.7 %shard_map.116 = (bf16[256,256]{1,0:T(8,128)(2,1)S(1)}, bf16[256,512]{1,0:T(8,128)(2,1)S(1)}, bf16[64,512]{1,0:T(8,128)(2,1)S(1)}) custom-call(f32[64,512]{1,0:T(8,128)S(1)} %get-tuple-element.42.lent_total, bf16[256,512]{1,0:T(8,128)(2,1)S(1)} %get-tuple-element.35.part, f32[64,512]{1,0:T(8,128)S(1)} %get-tuple-element.43.ahead, ...), custom_call_target="tpu_custom_call" | custom-call | flops 1000000000 | bytes 3000000 | tf_op jit(solution)/shard_map/pallas_call | solution.py:244
  33.0 0.6 %collective-permute-start.10 = (bf16[64,512]{1,0:T(8,128)(2,1)S(1)}, bf16[64,512]{1,0:T(8,128)(2,1)S(1)}, u32[]{:S(2)}, u32[]{:S(2)}) collective-permute-start(bf16[64,512]{1,0:T(8,128)(2,1)S(1)} %get-tuple-element.54), channel_id=1, source_target_pairs={{0,2},{2,0},{1,3},{3,1},{4,6},{6,4},{5,7},{7,5},{8,10},{10,8},{9,1... | collective-permute-start | bytes 196616 | tf_op jit(solution)/shard_map/ppermute | solution.py:271
  33.6 0.1 collective-permute-start.8
  33.7 2.8 %collective-permute-start.9 = (bf16[64,512]{1,0:T(8,128)(2,1)S(1)}, bf16[64,512]{1,0:T(8,128)(2,1)S(1)}, u32[]{:S(2)}, u32[]{:S(2)}) collective-permute-start(bf16[64,512]{1,0:T(8,128)(2,1)S(1)} %get-tuple-element.54), channel_id=1, source_target_pairs={{4,8},{8,4},{12,0},{0,12},{5,9},{9,5},{13,1},{1,13},{6,10},{10,6},... | collective-permute-start | bytes 196616 | tf_op jit(solution)/shard_map/ppermute | solution.py:280
  36.4 2.4 %shard_map.117 = (bf16[256,512]{1,0:T(8,128)(2,1)S(1)}, f32[512,512]{1,0:T(8,128)S(1)}, f32[256,512]{1,0:T(8,128)S(1)}, bf16[512,192]{1,0:T(8,128)(2,1)S(1)}, bf16[256,512]{1,0:T(8,128)(2,1)S(1)}) custom-call(f32[256,512]{1,0:T(8,128)S(1)} %get-tuple-element.41.total, bf16[256,256]{1,0:T(8,128)(2,1)S(1)} %get-tuple-element.46.spread, ...), custom_call_target="tpu_custom_call" | custom-call | flops 1000000000 | bytes 3000000 | tf_op jit(solution)/shard_map/pallas_call | solution.py:244
  38.8 0.0 collective-permute-done.8.rest_0_
  38.9 1.1 %collective-permute-done.9.rest_1_ = bf16[64,512]{1,0:T(8,128)(2,1)S(1)} collective-permute-done((bf16[64,512]{1,0:T(8,128)(2,1)S(1)}, bf16[64,512]{1,0:T(8,128)(2,1)S(1)}, u32[]{:S(2)}, u32[]{:S(2)}) %collective-permute-start.9) | collective-permute-done | bytes 65568 | tf_op jit(solution)/shard_map/ppermute | solution.py:280
  39.9 2.5 %shard_map.118 = bf16[256,512]{1,0:T(8,128)(2,1)} custom-call(f32[512,512]{1,0:T(8,128)S(1)} %get-tuple-element.49.pre, f32[256,512]{1,0:T(8,128)S(1)} %get-tuple-element.50.ahead, bf16[512,192]{1,0:T(8,128)(2,1)S(1)} %get-tuple-element.51.picks, bf16[256,512]{1,0:T(8,128)(2,1)S(1)} %get-tuple-element.52.spread, bf16[256,512]{1,0:T(8,128)(2,1)S(1)} %get-tuple-element.53.mid, ...), custom_call_target="tpu_custom_call" | custom-call | flops 1000000000 | bytes 3000000 | tf_op jit(solution)/shard_map/pallas_call | solution.py:244
  (18 shorter events, 0.0 us)
Async XLA Ops:
  0.0 5.6 %copy-start.2 = (bf16[512,512]{1,0:T(8,128)(2,1)S(1)}, bf16[512,512]{1,0:T(8,128)(2,1)}, u32[]{:S(2)}) copy-start(bf16[512,512]{1,0:T(8,128)(2,1)} %latent_ref.3) | copy-start | bytes 1572868
  0.0 11.4 %collective-permute-start = (bf16[13,256,512]{2,1,0:T(8,128)(2,1)}, bf16[13,256,512]{2,1,0:T(8,128)(2,1)S(1)}, u32[]{:S(2)}, u32[]{:S(2)}) collective-permute-start(bf16[13,256,512]{2,1,0:T(8,128)(2,1)} %mine.11), channel_id=1, source_target_pairs={{0,1},{1,0},{2,3},{3,2},{4,5},{5,4},{6,7},{7,6},{8,9},{9,8},{10,11... | collective-permute-start | bytes 10223624 | tf_op jit(solution)/shard_map/ppermute | solution.py:257
  1.8 13.9 %collective-permute-start.1 = (bf16[520,128]{1,0:T(8,128)(2,1)S(1)}, bf16[520,128]{1,0:T(8,128)(2,1)S(1)}, u32[]{:S(2)}, u32[]{:S(2)}) collective-permute-start(bf16[520,128]{1,0:T(8,128)(2,1)S(1)} %get-tuple-element.33), channel_id=1, source_target_pairs={{0,8},{2,10},{4,12},{6,14},{8,0},{10,2},{12,4},{14,6},{1,9},{3,11}... | collective-permute-start | bytes 399368 | tf_op jit(solution)/shard_map/ppermute | solution.py:266
  5.6 10.1 %copy-start = (bf16[13,256,512]{2,1,0:T(8,128)(2,1)S(1)}, bf16[13,256,512]{2,1,0:T(8,128)(2,1)}, u32[]{:S(2)}) copy-start(bf16[13,256,512]{2,1,0:T(8,128)(2,1)} %mine.11) | copy-start | bytes 10223620
  5.6 10.1 %copy-start.1 = (bf16[256,512]{1,0:T(8,128)(2,1)S(1)}, bf16[256,512]{1,0:T(8,128)(2,1)}, u32[]{:S(2)}) copy-start(bf16[256,512]{1,0:T(8,128)(2,1)} %mesh.3) | copy-start | bytes 786436
  5.6 10.1 %copy-start.4 = (f32[4,512]{1,0:T(4,128)S(1)}, f32[4,512]{1,0:T(4,128)}, u32[]{:S(2)}) copy-start(f32[4,512]{1,0:T(4,128)} %rest_0_.1) | copy-start | bytes 24580
  5.6 10.2 %copy-start.6 = (s32[64]{0:T(128)S(1)}, s32[64]{0:T(128)}, u32[]{:S(2)}) copy-start(s32[64]{0:T(128)} %param.18) | copy-start | bytes 772
  6.0 11.5 %collective-permute-start.2 = (bf16[520,128]{1,0:T(8,128)(2,1)S(1)}, bf16[520,128]{1,0:T(8,128)(2,1)S(1)}, u32[]{:S(2)}, u32[]{:S(2)}) collective-permute-start(bf16[520,128]{1,0:T(8,128)(2,1)S(1)} %get-tuple-element.36), channel_id=1, source_target_pairs={{0,4},{2,6},{4,8},{6,10},{8,12},{10,14},{12,0},{14,2},{1,5},{3,7},... | collective-permute-start | bytes 399368 | tf_op jit(solution)/shard_map/ppermute | solution.py:266
  7.7 17.1 %collective-permute-start.3 = (bf16[520,128]{1,0:T(8,128)(2,1)S(1)}, bf16[520,128]{1,0:T(8,128)(2,1)S(1)}, u32[]{:S(2)}, u32[]{:S(2)}) collective-permute-start(bf16[520,128]{1,0:T(8,128)(2,1)S(1)} %get-tuple-element.37), channel_id=1, source_target_pairs={{0,12},{2,14},{4,0},{6,2},{8,4},{10,6},{12,8},{14,10},{1,13},{3,15... | collective-permute-start | bytes 399368 | tf_op jit(solution)/shard_map/ppermute | solution.py:266
  9.9 16.2 %collective-permute-start.4 = (bf16[520,128]{1,0:T(8,128)(2,1)S(1)}, bf16[520,128]{1,0:T(8,128)(2,1)S(1)}, u32[]{:S(2)}, u32[]{:S(2)}) collective-permute-start(bf16[520,128]{1,0:T(8,128)(2,1)S(1)} %get-tuple-element.38), channel_id=1, source_target_pairs={{0,2},{2,0},{4,6},{6,4},{8,10},{10,8},{12,14},{14,12},{1,3},{3,1},... | collective-permute-start | bytes 399368 | tf_op jit(solution)/shard_map/ppermute | solution.py:266
  12.0 14.1 %collective-permute-start.5 = (bf16[520,128]{1,0:T(8,128)(2,1)S(1)}, bf16[520,128]{1,0:T(8,128)(2,1)S(1)}, u32[]{:S(2)}, u32[]{:S(2)}) collective-permute-start(bf16[520,128]{1,0:T(8,128)(2,1)S(1)} %get-tuple-element.39), channel_id=1, source_target_pairs={{0,14},{2,12},{4,2},{6,0},{8,6},{10,4},{12,10},{14,8},{1,15},{3,13... | collective-permute-start | bytes 399368 | tf_op jit(solution)/shard_map/ppermute | solution.py:266
  15.7 11.8 %collective-permute-start.6 = (bf16[520,128]{1,0:T(8,128)(2,1)S(1)}, bf16[520,128]{1,0:T(8,128)(2,1)S(1)}, u32[]{:S(2)}, u32[]{:S(2)}) collective-permute-start(bf16[520,128]{1,0:T(8,128)(2,1)S(1)} %get-tuple-element.40), channel_id=1, source_target_pairs={{0,6},{2,4},{4,10},{6,8},{8,14},{10,12},{12,2},{14,0},{1,7},{3,5},... | collective-permute-start | bytes 399368 | tf_op jit(solution)/shard_map/ppermute | solution.py:266
  17.6 13.7 %collective-permute-start.7 = (bf16[520,128]{1,0:T(8,128)(2,1)S(1)}, bf16[520,128]{1,0:T(8,128)(2,1)S(1)}, u32[]{:S(2)}, u32[]{:S(2)}) collective-permute-start(bf16[520,128]{1,0:T(8,128)(2,1)S(1)} %get-tuple-element.45), channel_id=1, source_target_pairs={{0,10},{2,8},{4,14},{6,12},{8,2},{10,0},{12,6},{14,4},{1,11},{3,9}... | collective-permute-start | bytes 399368 | tf_op jit(solution)/shard_map/ppermute | solution.py:266
  27.5 3.8 %copy-start.5 = (f32[4,512]{1,0:T(4,128)S(1)}, f32[4,512]{1,0:T(4,128)}, u32[]{:S(2)}) copy-start(f32[4,512]{1,0:T(4,128)} %gains.3) | copy-start | bytes 24580
  31.3 5.1 %copy-start.3 = (bf16[512,512]{1,0:T(8,128)(2,1)S(1)}, bf16[512,512]{1,0:T(8,128)(2,1)}, u32[]{:S(2)}) copy-start(bf16[512,512]{1,0:T(8,128)(2,1)} %edges.1) | copy-start | bytes 1572868
  31.3 5.1 %copy-start.7 = (s32[512]{0:T(512)S(1)}, s32[512]{0:T(512)}, u32[]{:S(2)}) copy-start(s32[512]{0:T(512)} %param.16) | copy-start | bytes 6148
  31.3 5.1 %copy-start.8 = (s32[512]{0:T(512)S(1)}, s32[512]{0:T(512)}, u32[]{:S(2)}) copy-start(s32[512]{0:T(512)} %param.17) | copy-start | bytes 6148
  33.0 5.8 %collective-permute-start.10 = (bf16[64,512]{1,0:T(8,128)(2,1)S(1)}, bf16[64,512]{1,0:T(8,128)(2,1)S(1)}, u32[]{:S(2)}, u32[]{:S(2)}) collective-permute-start(bf16[64,512]{1,0:T(8,128)(2,1)S(1)} %get-tuple-element.54), channel_id=1, source_target_pairs={{0,2},{2,0},{1,3},{3,1},{4,6},{6,4},{5,7},{7,5},{8,10},{10,8},{9,1... | collective-permute-start | bytes 196616 | tf_op jit(solution)/shard_map/ppermute | solution.py:271
  33.6 5.2 %collective-permute-start.8 = (bf16[64,512]{1,0:T(8,128)(2,1)S(1)}, bf16[64,512]{1,0:T(8,128)(2,1)S(1)}, u32[]{:S(2)}, u32[]{:S(2)}) collective-permute-start(bf16[64,512]{1,0:T(8,128)(2,1)S(1)} %get-tuple-element.54), channel_id=1, source_target_pairs={{0,4},{4,0},{8,12},{12,8},{1,5},{5,1},{9,13},{13,9},{2,6},{6,2},{1... | collective-permute-start | bytes 196616 | tf_op jit(solution)/shard_map/ppermute | solution.py:280
  33.7 6.3 %collective-permute-start.9 = (bf16[64,512]{1,0:T(8,128)(2,1)S(1)}, bf16[64,512]{1,0:T(8,128)(2,1)S(1)}, u32[]{:S(2)}, u32[]{:S(2)}) collective-permute-start(bf16[64,512]{1,0:T(8,128)(2,1)S(1)} %get-tuple-element.54), channel_id=1, source_target_pairs={{4,8},{8,4},{12,0},{0,12},{5,9},{9,5},{13,1},{1,13},{6,10},{10,6},... | collective-permute-start | bytes 196616 | tf_op jit(solution)/shard_map/ppermute | solution.py:280

commit v6 on v5

--- a/solution.py
+++ b/solution.py
@@ -9,7 +9,7 @@
 
 EPSILON = 1e-05
 LANES = 128
-AIM_ROWS = 8
+AIM_ROWS = 16
 F32 = jnp.float32
 BF16 = jnp.bfloat16
 HBM = pl.BlockSpec(memory_space=pltpu.HBM)
@@ -159,8 +159,29 @@
     return sum(mm(picks, part) for part in parts)
 
 
-def first_kernel(mine, other, mesh, lend, biases, *rest):
-    *chunks, sum_out, part_out, ahead_out, lent_ahead_out, lent_latent_out = rest
+def edge_ends(pieces, depth, nodes, sender, receiver):
+    entry = sender - nodes
+    if pieces == 3:
+        entry = jnp.where(entry >= 3 * depth, entry - depth, entry)
+    odd = lax.rem(lax.axis_index("lat"), 2) == 1
+    crossed = jnp.where(entry < 2 * depth, entry - depth, entry)
+    crossed = jnp.where(entry < depth, entry + depth, crossed)
+    entry = jnp.where(odd & (entry >= 0), crossed, entry)
+    return (
+        along(turned(entry), pieces * depth),
+        along(turned(sender), nodes),
+        along(turned(receiver), nodes),
+        down(receiver, nodes),
+    )
+
+
+def first_kernel(pieces, mine, other, mesh, lend, biases, edges, sender, receiver, *rest):
+    chunks, outs = rest[:-10], rest[-10:]
+    sum_out, part_out, ahead_out, lent_ahead_out, lent_latent_out = outs[:5]
+    outs[5][...] = through(edges[...], (mine, other), 6) + biases[2:3, :]
+    ends = edge_ends(pieces, lend.shape[1], mesh.shape[0], sender[...], receiver[...])
+    for out, value in zip(outs[6:], ends):
+        out[...] = value
     maps = (mine, other)
     latent = mesh[...]
     part = through(latent, maps, 1).astype(BF16)
@@ -202,33 +223,19 @@
     return (latent.astype(F32) + change).astype(BF16)
 
 
-def local_kernel(pieces, depth, total, spread, notes, node_ahead, mesh, edges, sender, receiver, *rest):
-    biases, gains, mine, other, mid_out, pre_out, ahead_out, picks_out, spread_out = rest
+def local_kernel(total, spread, notes, node_ahead, mesh, biases, gains, mine, other, *rest):
+    pre, at_sender, at_receiver, mid_out, pre_out, ahead_out = rest
     maps = (mine, other)
     sums = ((total[...] + mm(spread[...], notes[...])) * gains[0:1, :]).astype(BF16)
     mid = updated(node_ahead[...], sums, mesh[...], maps, gains)
     mid_out[...] = mid
-    nodes = mid.shape[0]
-    number = sender[...]
-    entry = number - nodes
-    if pieces == 3:
-        entry = jnp.where(entry >= 3 * depth, entry - depth, entry)
-    odd = lax.rem(lax.axis_index("lat"), 2) == 1
-    crossed = jnp.where(entry < depth, entry + depth, jnp.where(entry < 2 * depth, entry - depth, entry))
-    entry = jnp.where(odd & (entry >= 0), crossed, entry)
-    picks_out[...] = along(turned(entry), pieces * depth)
-    spread_out[...] = down(receiver[...], nodes)
-    at_sender = along(turned(number), nodes)
-    at_receiver = along(turned(receiver[...]), nodes)
     ahead_out[...] = through(mid, maps, 10) + biases[3:4, :]
-    pre = through(edges[...], maps, 6) + biases[2:3, :]
-    pre = pre + mm(at_sender, through(mid, maps, 7).astype(BF16))
-    pre_out[...] = pre + mm(at_receiver, through(mid, maps, 8).astype(BF16))
+    sent = pre[...] + mm(at_sender[...], through(mid, maps, 7).astype(BF16))
+    pre_out[...] = sent + mm(at_receiver[...], through(mid, maps, 8).astype(BF16))
 
 
 def process_kernel(pre, ahead, picks, spread, mid, gains, mine, other, *rest):
     *lent, out = rest
-    lent = [lent[1], lent[0], *lent[2:]]
     maps = (mine, other)
     table = jnp.concatenate([ref[...] for ref in lent], axis=0)
     hidden = silu(pre[...] + mm(picks[...], table))
@@ -315,13 +322,13 @@
     lon_count = lax.axis_size("lon")
     owners = lax.axis_size("lat") * lon_count
     capacity = max(2, 2 * rows_dev // owners)
-    exchange = capacity == LANES and owners <= 16
+    exchange = capacity == LANES and owners == 8
 
     other = swap(weights, "ch", 1)
 
     count = owners * capacity // LANES
     chunk_shape = ((width + AIM_ROWS, LANES), BF16)
-    order = [4, 2, 6, 1, 7, 3, 5] if owners == 8 else list(range(1, count))
+    order = [4, 2, 6, 7, 3, 1, 5] if exchange else list(range(1, count))
     lead, place, aims = call(
         functools.partial(place_kernel, owners, capacity, exchange, order[0]),
         [chunk_shape, ((1, rows_dev), jnp.int32), ((AIM_ROWS, rows_dev), BF16)],
@@ -355,19 +362,24 @@
         arrived = {0: chunks[0]}
         for step in order:
             arrived[step] = moved(chunks[step], step)
-        groups = [[0, 4], [2, 6], [1, 7], [3], [5]]
+        groups = [[0, 4], [2, 6], [7, 3], [1], [5]]
     else:
         arrived = dict(enumerate(sent_whole([chunks[i] for i in range(count)], owners, capacity, width)))
         groups = [[0], [1], list(range(2, count))]
 
     depth = halo_rows.shape[0]
     lend = halo_rows.reshape(1, -1)
-    total, part, node_ahead, lent_ahead, lent_latent = call(
-        first_kernel,
+    pieces = 3 if lon_count == 2 else 4
+    sender, receiver = mesh_sender.reshape(1, -1), mesh_receiver.reshape(1, -1)
+    total, part, node_ahead, lent_ahead, lent_latent, pre, *ends = call(
+        functools.partial(first_kernel, pieces),
         [((nodes, width), F32), ((nodes, width), BF16), ((nodes, width), F32)]
-        + [((depth, width), F32), ((depth, width), BF16)],
-        (weights, other, mesh_latent, lend, biases, *[arrived[i] for i in groups[0]]),
-        [VMEM] * (5 + len(groups[0])),
+        + [((depth, width), F32), ((depth, width), BF16), ((edges, width), F32)]
+        + [((edges, pieces * depth), BF16), ((edges, nodes), BF16)]
+        + [((edges, nodes), BF16), ((nodes, edges), BF16)],
+        (weights, other, mesh_latent, lend, biases, edge_latent, sender, receiver)
+        + tuple(arrived[i] for i in groups[0]),
+        [VMEM] * (8 + len(groups[0])),
         flops=5 * 10**8,
         moved=3 * 10**6,
     )
@@ -401,19 +413,12 @@
     halo = [paired(lent, "lat", 1), paired(lent, "lat", 0), shift(lent, "lon", 1)]
     if lon_count != 2:
         halo.append(shift(lent, "lon", -1))
-    sender, receiver = mesh_sender.reshape(1, -1), mesh_receiver.reshape(1, -1)
-    pieces = len(halo)
-    mid, pre, ahead, picks, spread = call(
-        functools.partial(local_kernel, pieces, depth),
-        [
-            ((nodes, width), BF16),
-            ((edges, width), F32),
-            ((nodes, width), F32),
-            ((edges, pieces * depth), BF16),
-            ((nodes, edges), BF16),
-        ],
-        (total, spread, notes, node_ahead, mesh_latent, edge_latent, sender, receiver)
-        + (biases, gains, weights, other),
+    picks, at_sender, at_receiver, edge_spread = ends
+    mid, pre, ahead = call(
+        local_kernel,
+        [((nodes, width), BF16), ((edges, width), F32), ((nodes, width), F32)],
+        (total, spread, notes, node_ahead, mesh_latent, biases, gains, weights, other)
+        + (pre, at_sender, at_receiver),
         [VMEM] * 12,
         flops=10**9,
         moved=3 * 10**6,
@@ -421,7 +426,7 @@
     (out,) = call(
         process_kernel,
         [((nodes, width), BF16)],
-        (pre, ahead, picks, spread, mid, gains, weights, other, halo[1], halo[0], *halo[2:]),
+        (pre, ahead, picks, edge_spread, mid, gains, weights, other, *halo),
         [VMEM] * (8 + pieces),
         flops=10**9,
         moved=3 * 10**6,

time: 42.6 us -> 42.9 us (level)
  starting transfers between devices: 21 us -> 21.5 us
where the time goes in v6:
time: 42.9 us; the launch traced here: 42.8 us
  starting transfers between devices  21.5 us (50%)
  Pallas kernels  14.9 us (35%)
  waiting for transfers between devices  6.17 us (14%)
    ppermute x7, starting transfers between devices, moved(): return lax.ppermute(value, ('lat', 'lon'), pairs)  17.4 us
    pallas_call x10, Pallas kernels, call(): pl.pallas_call(kernel, out_shape=[jax.ShapeDtypeStruct(shape, kind) for s...  14.9 us
    ppermute x7, waiting for transfers between devices, moved(): return lax.ppermute(value, ('lat', 'lon'), pairs)  4.9 us
    ppermute x2, starting transfers between devices, paired(): return lax.ppermute(value, axis, pairs)  3.08 us
    ppermute x2, waiting for transfers between devices, paired(): return lax.ppermute(value, axis, pairs)  1.27 us
  transfers between devices with their start and end apart: 11, of which 3 were waited for; matrix products, arithmetic and copies ran while one was open for 0% of the time, Pallas kernels for 25%

profile of v6, /device:TPU:0, one launch (start us, length us, event | category | flops | bytes accessed | tf_op | source)
XLA Modules:
  0.0 42.8 jit_solution(15206129296994609150)
XLA Ops:
  0.0 0.5 %collective-permute-start = (bf16[13,256,512]{2,1,0:T(8,128)(2,1)}, bf16[13,256,512]{2,1,0:T(8,128)(2,1)S(1)}, u32[]{:S(2)}, u32[]{:S(2)}) collective-permute-start(bf16[13,256,512]{2,1,0:T(8,128)(2,1)} %mine.13), channel_id=1, source_target_pairs={{0,1},{1,0},{2,3},{3,2},{4,5},{5,4},{6,7},{7,6},{8,9},{9,8},{10,11... | collective-permute-start | bytes 10223624 | tf_op jit(solution)/shard_map/ppermute | solution.py:264
  0.5 1.4 %shard_map.109 = (bf16[528,128]{1,0:T(8,128)(2,1)S(1)}, s32[1,512]{1,0:T(1,128)S(1)}, bf16[16,512]{1,0:T(8,128)(2,1)S(1)}) custom-call(s32[1,512]{1,0:T(1,128)} %bitcast.11, s32[2,512]{1,0:T(2,128)} %bitcast.10, bf16[512,512]{1,0:T(8,128)(2,1)} %latent_ref.3), custom_call_target="tpu_custom_call" | custom-call | flops 1000000000 | bytes 2000000 | tf_op jit(solution)/shard_map/pallas_call | solution.py:251
  1.8 3.7 %collective-permute-start.1 = (bf16[528,128]{1,0:T(8,128)(2,1)S(1)}, bf16[528,128]{1,0:T(8,128)(2,1)S(1)}, u32[]{:S(2)}, u32[]{:S(2)}) collective-permute-start(bf16[528,128]{1,0:T(8,128)(2,1)S(1)} %get-tuple-element.36), channel_id=1, source_target_pairs={{0,8},{2,10},{4,12},{6,14},{8,0},{10,2},{12,4},{14,6},{1,9},{3,11}... | collective-permute-start | bytes 405512 | tf_op jit(solution)/shard_map/ppermute | solution.py:273
  5.6 0.0 copy-start.4
  5.6 0.0 copy-start.6
  5.6 0.0 copy-start.7
  5.6 0.0 copy-start.8
  5.6 0.5 %shard_map.112 = (bf16[528,128]{1,0:T(8,128)(2,1)S(1)}, bf16[528,128]{1,0:T(8,128)(2,1)S(1)}, bf16[528,128]{1,0:T(8,128)(2,1)S(1)}) custom-call(s32[1,512]{1,0:T(1,128)S(1)} %get-tuple-element.33.place_ref, bf16[16,512]{1,0:T(8,128)(2,1)S(1)} %get-tuple-element.34.aims_ref.after, bf16[512,512]{1,0:T(8,128)(2,1)S(1)} %copy-done.2, ...), custom_call_target="tpu_custom_call" | custom-call | flops 1000000000 | bytes 2000000 | tf_op jit(solution)/shard_map/pallas_call | solution.py:251
  6.1 1.6 %collective-permute-start.2 = (bf16[528,128]{1,0:T(8,128)(2,1)S(1)}, bf16[528,128]{1,0:T(8,128)(2,1)S(1)}, u32[]{:S(2)}, u32[]{:S(2)}) collective-permute-start(bf16[528,128]{1,0:T(8,128)(2,1)S(1)} %get-tuple-element.39), channel_id=1, source_target_pairs={{0,4},{2,6},{4,8},{6,10},{8,12},{10,14},{12,0},{14,2},{1,5},{3,7},... | collective-permute-start | bytes 405512 | tf_op jit(solution)/shard_map/ppermute | solution.py:273
  7.7 2.2 %collective-permute-start.3 = (bf16[528,128]{1,0:T(8,128)(2,1)S(1)}, bf16[528,128]{1,0:T(8,128)(2,1)S(1)}, u32[]{:S(2)}, u32[]{:S(2)}) collective-permute-start(bf16[528,128]{1,0:T(8,128)(2,1)S(1)} %get-tuple-element.40), channel_id=1, source_target_pairs={{0,12},{2,14},{4,0},{6,2},{8,4},{10,6},{12,8},{14,10},{1,13},{3,15... | collective-permute-start | bytes 405512 | tf_op jit(solution)/shard_map/ppermute | solution.py:273
  9.9 0.9 %collective-permute-start.4 = (bf16[528,128]{1,0:T(8,128)(2,1)S(1)}, bf16[528,128]{1,0:T(8,128)(2,1)S(1)}, u32[]{:S(2)}, u32[]{:S(2)}) collective-permute-start(bf16[528,128]{1,0:T(8,128)(2,1)S(1)} %get-tuple-element.41), channel_id=1, source_target_pairs={{0,14},{2,12},{4,2},{6,0},{8,6},{10,4},{12,10},{14,8},{1,15},{3,13... | collective-permute-start | bytes 405512 | tf_op jit(solution)/shard_map/ppermute | solution.py:273
  10.9 0.0 collective-permute-done.after.other
  10.9 0.6 %shard_map.110 = (bf16[528,128]{1,0:T(8,128)(2,1)S(1)}, bf16[528,128]{1,0:T(8,128)(2,1)S(1)}, bf16[528,128]{1,0:T(8,128)(2,1)S(1)}, bf16[528,128]{1,0:T(8,128)(2,1)S(1)}) custom-call(s32[1,512]{1,0:T(1,128)S(1)} %get-tuple-element.33.place_ref, bf16[16,512]{1,0:T(8,128)(2,1)S(1)} %get-tuple-element.34.aims_ref.after, bf16[512,512]{1,0:T(8,128)(2,1)S(1)} %copy-done.2, ...), custom_call_target="tpu_custom_call" | custom-call | flops 1000000000 | bytes 2000000 | tf_op jit(solution)/shard_map/pallas_call | solution.py:251
  11.5 2.0 %collective-permute-start.5 = (bf16[528,128]{1,0:T(8,128)(2,1)S(1)}, bf16[528,128]{1,0:T(8,128)(2,1)S(1)}, u32[]{:S(2)}, u32[]{:S(2)}) collective-permute-start(bf16[528,128]{1,0:T(8,128)(2,1)S(1)} %get-tuple-element.42), channel_id=1, source_target_pairs={{0,6},{2,4},{4,10},{6,8},{8,14},{10,12},{12,2},{14,0},{1,7},{3,5},... | collective-permute-start | bytes 405512 | tf_op jit(solution)/shard_map/ppermute | solution.py:273
  13.5 2.3 %collective-permute-done.1.rest_1_ = bf16[528,128]{1,0:T(8,128)(2,1)S(1)} collective-permute-done((bf16[528,128]{1,0:T(8,128)(2,1)S(1)}, bf16[528,128]{1,0:T(8,128)(2,1)S(1)}, u32[]{:S(2)}, u32[]{:S(2)}) %collective-permute-start.1) | collective-permute-done | bytes 135200 | tf_op jit(solution)/shard_map/ppermute | solution.py:273
  15.8 1.7 %collective-permute-start.6 = (bf16[528,128]{1,0:T(8,128)(2,1)S(1)}, bf16[528,128]{1,0:T(8,128)(2,1)S(1)}, u32[]{:S(2)}, u32[]{:S(2)}) collective-permute-start(bf16[528,128]{1,0:T(8,128)(2,1)S(1)} %get-tuple-element.43), channel_id=1, source_target_pairs={{0,2},{2,0},{4,6},{6,4},{8,10},{10,8},{12,14},{14,12},{1,3},{3,1},... | collective-permute-start | bytes 405512 | tf_op jit(solution)/shard_map/ppermute | solution.py:273
  17.6 2.3 %shard_map.111 = (f32[256,512]{1,0:T(8,128)S(1)}, bf16[256,512]{1,0:T(8,128)(2,1)S(1)}, f32[256,512]{1,0:T(8,128)S(1)}, f32[64,512]{1,0:T(8,128)S(1)}, bf16[64,5...) custom-call(bf16[13,256,512]{2,1,0:T(8,128)(2,1)S(1)} %copy-done, ...), custom_call_target="tpu_custom_call" | custom-call | flops 500000000 | bytes 3000000 | tf_op jit(solution)/shard_map/pallas_call | solution.py:251
  19.9 0.0 collective-permute-done.2.rest_0_
  19.9 5.1 %collective-permute-start.7 = (bf16[528,128]{1,0:T(8,128)(2,1)S(1)}, bf16[528,128]{1,0:T(8,128)(2,1)S(1)}, u32[]{:S(2)}, u32[]{:S(2)}) collective-permute-start(bf16[528,128]{1,0:T(8,128)(2,1)S(1)} %get-tuple-element.48), channel_id=1, source_target_pairs={{0,10},{2,8},{4,14},{6,12},{8,2},{10,0},{12,6},{14,4},{1,11},{3,9}... | collective-permute-start | bytes 405512 | tf_op jit(solution)/shard_map/ppermute | solution.py:273
  25.0 0.0 collective-permute-done.3.rest_1_
  25.0 1.4 %shard_map.113.total = f32[256,512]{1,0:T(8,128)S(1)} custom-call(f32[256,512]{1,0:T(8,128)S(1)} %get-tuple-element.37.total, bf16[256,512]{1,0:T(8,128)(2,1)S(1)} %get-tuple-element.38.part, bf16[13,256,512]{2,1,0:T(8,128)(2,1)S(1)} %copy-done, bf16[13,256,512]{2,1,0:T(8,128)(2,1)S(1)} %collective-permute-done.after.other, f32[4,512]{1,0:T(4,128)S(1)} %copy-done.4, ...), custom_call_target="tpu_custom_call" | custom-call | flops 800000000 | bytes 2000000 | tf_op jit(solution)/shard_map/pallas_call | solution.py:251
  26.4 1.4 %shard_map.114.total = f32[256,512]{1,0:T(8,128)S(1)} custom-call(f32[256,512]{1,0:T(8,128)S(1)} %shard_map.113.total, bf16[256,512]{1,0:T(8,128)(2,1)S(1)} %get-tuple-element.38.part, bf16[13,256,512]{2,1,0:T(8,128)(2,1)S(1)} %copy-done, bf16[13,256,512]{2,1,0:T(8,128)(2,1)S(1)} %collective-permute-done.after.other, f32[4,512]{1,0:T(4,128)S(1)} %copy-done.4, ...), custom_call_target="tpu_custom_call" | custom-call | flops 800000000 | bytes 2000000 | tf_op jit(solution)/shard_map/pallas_call | solution.py:251
  27.8 0.0 copy-start.5
  27.8 1.3 %shard_map.115 = (f32[256,512]{1,0:T(8,128)S(1)}, f32[64,512]{1,0:T(8,128)S(1)}) custom-call(f32[256,512]{1,0:T(8,128)S(1)} %shard_map.114.total, bf16[256,512]{1,0:T(8,128)(2,1)S(1)} %get-tuple-element.38.part, bf16[13,256,512]{2,1,0:T(8,128)(2,1)S(1)} %copy-done, bf16[13,256,512]{2,1,0:T(8,128)(2,1)S(1)} %collective-permute-done.after.other, ...), custom_call_target="tpu_custom_call" | custom-call | flops 1000000000 | bytes 2000000 | tf_op jit(solution)/shard_map/pallas_call | solution.py:251
  29.1 2.6 %collective-permute-done.7.rest_0_ = bf16[528,128]{1,0:T(8,128)(2,1)S(1)} collective-permute-done((bf16[528,128]{1,0:T(8,128)(2,1)S(1)}, bf16[528,128]{1,0:T(8,128)(2,1)S(1)}, u32[]{:S(2)}, u32[]{:S(2)}) %collective-permute-start.7) | collective-permute-done | bytes 135200 | tf_op jit(solution)/shard_map/ppermute | solution.py:273
  31.7 1.7 %shard_map.116 = (bf16[256,256]{1,0:T(8,128)(2,1)S(1)}, bf16[256,512]{1,0:T(8,128)(2,1)S(1)}, bf16[64,512]{1,0:T(8,128)(2,1)S(1)}) custom-call(f32[64,512]{1,0:T(8,128)S(1)} %get-tuple-element.45.lent_total, bf16[256,512]{1,0:T(8,128)(2,1)S(1)} %get-tuple-element.38.part, f32[64,512]{1,0:T(8,128)S(1)} %get-tuple-element.46.ahead, ...), custom_call_target="tpu_custom_call" | custom-call | flops 1000000000 | bytes 3000000 | tf_op jit(solution)/shard_map/pallas_call | solution.py:251
  33.4 0.5 %collective-permute-start.10 = (bf16[64,512]{1,0:T(8,128)(2,1)S(1)}, bf16[64,512]{1,0:T(8,128)(2,1)S(1)}, u32[]{:S(2)}, u32[]{:S(2)}) collective-permute-start(bf16[64,512]{1,0:T(8,128)(2,1)S(1)} %get-tuple-element.60), channel_id=1, source_target_pairs={{0,2},{2,0},{1,3},{3,1},{4,6},{6,4},{5,7},{7,5},{8,10},{10,8},{9,1... | collective-permute-start | bytes 196616 | tf_op jit(solution)/shard_map/ppermute | solution.py:278
  33.9 0.1 collective-permute-start.9
  34.0 2.9 %collective-permute-start.8 = (bf16[64,512]{1,0:T(8,128)(2,1)S(1)}, bf16[64,512]{1,0:T(8,128)(2,1)S(1)}, u32[]{:S(2)}, u32[]{:S(2)}) collective-permute-start(bf16[64,512]{1,0:T(8,128)(2,1)S(1)} %get-tuple-element.60), channel_id=1, source_target_pairs={{4,8},{8,4},{12,0},{0,12},{5,9},{9,5},{13,1},{1,13},{6,10},{10,6},... | collective-permute-start | bytes 196616 | tf_op jit(solution)/shard_map/ppermute | solution.py:287
  37.0 1.9 %shard_map.117 = (bf16[256,512]{1,0:T(8,128)(2,1)S(1)}, f32[512,512]{1,0:T(8,128)S(1)}, f32[256,512]{1,0:T(8,128)S(1)}) custom-call(f32[256,512]{1,0:T(8,128)S(1)} %get-tuple-element.44.total, bf16[256,256]{1,0:T(8,128)(2,1)S(1)} %get-tuple-element.49.spread, bf16[256,512]{1,0:T(8,128)(2,1)S(1)} %get-tuple-element.50.notes, ...), custom_call_target="tpu_custom_call" | custom-call | flops 1000000000 | bytes 3000000 | tf_op jit(solution)/shard_map/pallas_call | solution.py:251
  38.9 1.3 %collective-permute-done.8.rest_0_ = bf16[64,512]{1,0:T(8,128)(2,1)S(1)} collective-permute-done((bf16[64,512]{1,0:T(8,128)(2,1)S(1)}, bf16[64,512]{1,0:T(8,128)(2,1)S(1)}, u32[]{:S(2)}, u32[]{:S(2)}) %collective-permute-start.8) | collective-permute-done | bytes 65568 | tf_op jit(solution)/shard_map/ppermute | solution.py:287
  40.2 2.6 %shard_map.118 = bf16[256,512]{1,0:T(8,128)(2,1)} custom-call(f32[512,512]{1,0:T(8,128)S(1)} %get-tuple-element.55.pre, f32[256,512]{1,0:T(8,128)S(1)} %get-tuple-element.56.ahead, bf16[512,192]{1,0:T(8,128)(2,1)S(1)} %get-tuple-element.57.picks, bf16[256,512]{1,0:T(8,128)(2,1)S(1)} %get-tuple-element.58.spread, bf16[256,512]{1,0:T(8,128)(2,1)S(1)} %get-tuple-element.59.mid, ...), custom_call_target="tpu_custom_call" | custom-call | flops 1000000000 | bytes 3000000 | tf_op jit(solution)/shard_map/pallas_call | solution.py:251
  (18 shorter events, 0.0 us)
Async XLA Ops:
  0.0 5.6 %copy-start.2 = (bf16[512,512]{1,0:T(8,128)(2,1)S(1)}, bf16[512,512]{1,0:T(8,128)(2,1)}, u32[]{:S(2)}) copy-start(bf16[512,512]{1,0:T(8,128)(2,1)} %latent_ref.3) | copy-start | bytes 1572868
  0.0 10.9 %collective-permute-start = (bf16[13,256,512]{2,1,0:T(8,128)(2,1)}, bf16[13,256,512]{2,1,0:T(8,128)(2,1)S(1)}, u32[]{:S(2)}, u32[]{:S(2)}) collective-permute-start(bf16[13,256,512]{2,1,0:T(8,128)(2,1)} %mine.13), channel_id=1, source_target_pairs={{0,1},{1,0},{2,3},{3,2},{4,5},{5,4},{6,7},{7,6},{8,9},{9,8},{10,11... | collective-permute-start | bytes 10223624 | tf_op jit(solution)/shard_map/ppermute | solution.py:264
  1.8 14.0 %collective-permute-start.1 = (bf16[528,128]{1,0:T(8,128)(2,1)S(1)}, bf16[528,128]{1,0:T(8,128)(2,1)S(1)}, u32[]{:S(2)}, u32[]{:S(2)}) collective-permute-start(bf16[528,128]{1,0:T(8,128)(2,1)S(1)} %get-tuple-element.36), channel_id=1, source_target_pairs={{0,8},{2,10},{4,12},{6,14},{8,0},{10,2},{12,4},{14,6},{1,9},{3,11}... | collective-permute-start | bytes 405512 | tf_op jit(solution)/shard_map/ppermute | solution.py:273
  5.6 12.0 %copy-start = (bf16[13,256,512]{2,1,0:T(8,128)(2,1)S(1)}, bf16[13,256,512]{2,1,0:T(8,128)(2,1)}, u32[]{:S(2)}) copy-start(bf16[13,256,512]{2,1,0:T(8,128)(2,1)} %mine.13) | copy-start | bytes 10223620
  5.6 12.0 %copy-start.1 = (bf16[256,512]{1,0:T(8,128)(2,1)S(1)}, bf16[256,512]{1,0:T(8,128)(2,1)}, u32[]{:S(2)}) copy-start(bf16[256,512]{1,0:T(8,128)(2,1)} %mesh.3) | copy-start | bytes 786436
  5.6 12.0 %copy-start.3 = (bf16[512,512]{1,0:T(8,128)(2,1)S(1)}, bf16[512,512]{1,0:T(8,128)(2,1)}, u32[]{:S(2)}) copy-start(bf16[512,512]{1,0:T(8,128)(2,1)} %edges.1) | copy-start | bytes 1572868
  5.6 12.0 %copy-start.4 = (f32[4,512]{1,0:T(4,128)S(1)}, f32[4,512]{1,0:T(4,128)}, u32[]{:S(2)}) copy-start(f32[4,512]{1,0:T(4,128)} %biases.11) | copy-start | bytes 24580
  5.6 12.0 %copy-start.6 = (s32[64]{0:T(128)S(1)}, s32[64]{0:T(128)}, u32[]{:S(2)}) copy-start(s32[64]{0:T(128)} %param.18) | copy-start | bytes 772
  5.6 12.0 %copy-start.7 = (s32[512]{0:T(512)S(1)}, s32[512]{0:T(512)}, u32[]{:S(2)}) copy-start(s32[512]{0:T(512)} %param.16) | copy-start | bytes 6148
  5.6 12.0 %copy-start.8 = (s32[512]{0:T(512)S(1)}, s32[512]{0:T(512)}, u32[]{:S(2)}) copy-start(s32[512]{0:T(512)} %param.17) | copy-start | bytes 6148
  6.1 13.8 %collective-permute-start.2 = (bf16[528,128]{1,0:T(8,128)(2,1)S(1)}, bf16[528,128]{1,0:T(8,128)(2,1)S(1)}, u32[]{:S(2)}, u32[]{:S(2)}) collective-permute-start(bf16[528,128]{1,0:T(8,128)(2,1)S(1)} %get-tuple-element.39), channel_id=1, source_target_pairs={{0,4},{2,6},{4,8},{6,10},{8,12},{10,14},{12,0},{14,2},{1,5},{3,7},... | collective-permute-start | bytes 405512 | tf_op jit(solution)/shard_map/ppermute | solution.py:273
  7.7 17.3 %collective-permute-start.3 = (bf16[528,128]{1,0:T(8,128)(2,1)S(1)}, bf16[528,128]{1,0:T(8,128)(2,1)S(1)}, u32[]{:S(2)}, u32[]{:S(2)}) collective-permute-start(bf16[528,128]{1,0:T(8,128)(2,1)S(1)} %get-tuple-element.40), channel_id=1, source_target_pairs={{0,12},{2,14},{4,0},{6,2},{8,4},{10,6},{12,8},{14,10},{1,13},{3,15... | collective-permute-start | bytes 405512 | tf_op jit(solution)/shard_map/ppermute | solution.py:273
  9.9 16.5 %collective-permute-start.4 = (bf16[528,128]{1,0:T(8,128)(2,1)S(1)}, bf16[528,128]{1,0:T(8,128)(2,1)S(1)}, u32[]{:S(2)}, u32[]{:S(2)}) collective-permute-start(bf16[528,128]{1,0:T(8,128)(2,1)S(1)} %get-tuple-element.41), channel_id=1, source_target_pairs={{0,14},{2,12},{4,2},{6,0},{8,6},{10,4},{12,10},{14,8},{1,15},{3,13... | collective-permute-start | bytes 405512 | tf_op jit(solution)/shard_map/ppermute | solution.py:273
  11.5 14.9 %collective-permute-start.5 = (bf16[528,128]{1,0:T(8,128)(2,1)S(1)}, bf16[528,128]{1,0:T(8,128)(2,1)S(1)}, u32[]{:S(2)}, u32[]{:S(2)}) collective-permute-start(bf16[528,128]{1,0:T(8,128)(2,1)S(1)} %get-tuple-element.42), channel_id=1, source_target_pairs={{0,6},{2,4},{4,10},{6,8},{8,14},{10,12},{12,2},{14,0},{1,7},{3,5},... | collective-permute-start | bytes 405512 | tf_op jit(solution)/shard_map/ppermute | solution.py:273
  15.8 12.0 %collective-permute-start.6 = (bf16[528,128]{1,0:T(8,128)(2,1)S(1)}, bf16[528,128]{1,0:T(8,128)(2,1)S(1)}, u32[]{:S(2)}, u32[]{:S(2)}) collective-permute-start(bf16[528,128]{1,0:T(8,128)(2,1)S(1)} %get-tuple-element.43), channel_id=1, source_target_pairs={{0,2},{2,0},{4,6},{6,4},{8,10},{10,8},{12,14},{14,12},{1,3},{3,1},... | collective-permute-start | bytes 405512 | tf_op jit(solution)/shard_map/ppermute | solution.py:273
  19.9 11.8 %collective-permute-start.7 = (bf16[528,128]{1,0:T(8,128)(2,1)S(1)}, bf16[528,128]{1,0:T(8,128)(2,1)S(1)}, u32[]{:S(2)}, u32[]{:S(2)}) collective-permute-start(bf16[528,128]{1,0:T(8,128)(2,1)S(1)} %get-tuple-element.48), channel_id=1, source_target_pairs={{0,10},{2,8},{4,14},{6,12},{8,2},{10,0},{12,6},{14,4},{1,11},{3,9}... | collective-permute-start | bytes 405512 | tf_op jit(solution)/shard_map/ppermute | solution.py:273
  27.8 3.9 %copy-start.5 = (f32[4,512]{1,0:T(4,128)S(1)}, f32[4,512]{1,0:T(4,128)}, u32[]{:S(2)}) copy-start(f32[4,512]{1,0:T(4,128)} %gains.5) | copy-start | bytes 24580
  33.4 5.6 %collective-permute-start.10 = (bf16[64,512]{1,0:T(8,128)(2,1)S(1)}, bf16[64,512]{1,0:T(8,128)(2,1)S(1)}, u32[]{:S(2)}, u32[]{:S(2)}) collective-permute-start(bf16[64,512]{1,0:T(8,128)(2,1)S(1)} %get-tuple-element.60), channel_id=1, source_target_pairs={{0,2},{2,0},{1,3},{3,1},{4,6},{6,4},{5,7},{7,5},{8,10},{10,8},{9,1... | collective-permute-start | bytes 196616 | tf_op jit(solution)/shard_map/ppermute | solution.py:278
  33.9 5.0 %collective-permute-start.9 = (bf16[64,512]{1,0:T(8,128)(2,1)S(1)}, bf16[64,512]{1,0:T(8,128)(2,1)S(1)}, u32[]{:S(2)}, u32[]{:S(2)}) collective-permute-start(bf16[64,512]{1,0:T(8,128)(2,1)S(1)} %get-tuple-element.60), channel_id=1, source_target_pairs={{0,4},{4,0},{8,12},{12,8},{1,5},{5,1},{9,13},{13,9},{2,6},{6,2},{1... | collective-permute-start | bytes 196616 | tf_op jit(solution)/shard_map/ppermute | solution.py:287
  34.0 6.2 %collective-permute-start.8 = (bf16[64,512]{1,0:T(8,128)(2,1)S(1)}, bf16[64,512]{1,0:T(8,128)(2,1)S(1)}, u32[]{:S(2)}, u32[]{:S(2)}) collective-permute-start(bf16[64,512]{1,0:T(8,128)(2,1)S(1)} %get-tuple-element.60), channel_id=1, source_target_pairs={{4,8},{8,4},{12,0},{0,12},{5,9},{9,5},{13,1},{1,13},{6,10},{10,6},... | collective-permute-start | bytes 196616 | tf_op jit(solution)/shard_map/ppermute | solution.py:287

commit v7 on v6

--- a/solution.py
+++ b/solution.py
@@ -88,18 +88,27 @@
 def place_kernel(owners, capacity, exchange, step, owner_in, target_in, latent_in, *rest):
     out, place_out, aims_out, owner_ref, target_ref, latent_ref, sems = rest
     rows, width = latent_ref.shape
-    pairs = ((owner_in, owner_ref), (target_in, target_ref), (latent_in, latent_ref))
+    half = rows // 2
+    pairs = [(owner_in, owner_ref), (target_in, target_ref)]
+    for i in range(2):
+        pairs.append([ref.at[pl.ds(i * half, half), :] for ref in (latent_in, latent_ref)])
     copies = [pltpu.make_async_copy(*pair, sems.at[i]) for i, pair in enumerate(pairs)]
     for copy in copies:
         copy.start()
     number = lax.broadcasted_iota(jnp.int32, (max(16, owners), rows), 0)
     before = as_bf16(
-        lax.broadcasted_iota(jnp.int32, (rows, rows), 0)
-        < lax.broadcasted_iota(jnp.int32, (rows, rows), 1)
+        lax.broadcasted_iota(jnp.int32, (LANES, LANES), 0)
+        < lax.broadcasted_iota(jnp.int32, (LANES, LANES), 1)
     )
     copies[0].wait()
     named = number == owner_ref[...]
-    rank = mm(as_bf16(named), before).astype(jnp.int32)
+    ones = jnp.where(named, 1.0, 0.0)
+    ranks, ahead = [], jnp.zeros((named.shape[0], 1), F32)
+    for i in range(rows // LANES):
+        block = ones[:, i * LANES : (i + 1) * LANES]
+        ranks.append(mm(block.astype(BF16), before) + ahead)
+        ahead = ahead + jnp.sum(block, axis=1, keepdims=True)
+    rank = jnp.concatenate(ranks, axis=1).astype(jnp.int32)
     place = jnp.sum(jnp.where(named, number * capacity + rank, 0), axis=0, keepdims=True)
     copies[1].wait()
     aims = jnp.concatenate(
@@ -112,6 +121,7 @@
     place_out[...] = place
     aims_out[...] = aims
     copies[2].wait()
+    copies[3].wait()
     packed(place, aims, latent_ref[...], base_of(step, capacity, exchange), out)
 
 
@@ -341,7 +351,7 @@
             pltpu.VMEM((1, rows_dev), jnp.int32),
             pltpu.VMEM((2, rows_dev), jnp.int32),
             pltpu.VMEM((rows_dev, width), BF16),
-            pltpu.SemaphoreType.DMA((3,)),
+            pltpu.SemaphoreType.DMA((4,)),
         ],
         flops=10**9,
         moved=2 * 10**6,

time: 42.9 us -> 42.9 us (level)
  no operation moved by 1% of the time
where the time goes in v7:
time: 42.9 us; the launch traced here: 42.7 us
  starting transfers between devices  21.5 us (50%)
  Pallas kernels  14.8 us (34%)
  waiting for transfers between devices  6.18 us (14%)
    ppermute x7, starting transfers between devices, moved(): return lax.ppermute(value, ('lat', 'lon'), pairs)  17.4 us
    pallas_call x10, Pallas kernels, call(): pl.pallas_call(kernel, out_shape=[jax.ShapeDtypeStruct(shape, kind) for s...  14.8 us
    ppermute x7, waiting for transfers between devices, moved(): return lax.ppermute(value, ('lat', 'lon'), pairs)  4.9 us
    ppermute x2, starting transfers between devices, paired(): return lax.ppermute(value, axis, pairs)  3.08 us
    ppermute x2, waiting for transfers between devices, paired(): return lax.ppermute(value, axis, pairs)  1.27 us
  transfers between devices with their start and end apart: 11, of which 3 were waited for; matrix products, arithmetic and copies ran while one was open for 0% of the time, Pallas kernels for 25%

profile of v7, /device:TPU:0, one launch (start us, length us, event | category | flops | bytes accessed | tf_op | source)
XLA Modules:
  0.0 42.7 jit_solution(6576588152441889972)
XLA Ops:
  0.0 0.5 %collective-permute-start = (bf16[13,256,512]{2,1,0:T(8,128)(2,1)}, bf16[13,256,512]{2,1,0:T(8,128)(2,1)S(1)}, u32[]{:S(2)}, u32[]{:S(2)}) collective-permute-start(bf16[13,256,512]{2,1,0:T(8,128)(2,1)} %mine.13), channel_id=1, source_target_pairs={{0,1},{1,0},{2,3},{3,2},{4,5},{5,4},{6,7},{7,6},{8,9},{9,8},{10,11... | collective-permute-start | bytes 10223624 | tf_op jit(solution)/shard_map/ppermute | solution.py:274
  0.5 1.3 %shard_map.109 = (bf16[528,128]{1,0:T(8,128)(2,1)S(1)}, s32[1,512]{1,0:T(1,128)S(1)}, bf16[16,512]{1,0:T(8,128)(2,1)S(1)}) custom-call(s32[1,512]{1,0:T(1,128)} %bitcast.11, s32[2,512]{1,0:T(2,128)} %bitcast.10, bf16[512,512]{1,0:T(8,128)(2,1)} %latent_ref.3), custom_call_target="tpu_custom_call" | custom-call | flops 1000000000 | bytes 2000000 | tf_op jit(solution)/shard_map/pallas_call | solution.py:261
  1.8 3.7 %collective-permute-start.1 = (bf16[528,128]{1,0:T(8,128)(2,1)S(1)}, bf16[528,128]{1,0:T(8,128)(2,1)S(1)}, u32[]{:S(2)}, u32[]{:S(2)}) collective-permute-start(bf16[528,128]{1,0:T(8,128)(2,1)S(1)} %get-tuple-element.36), channel_id=1, source_target_pairs={{0,8},{2,10},{4,12},{6,14},{8,0},{10,2},{12,4},{14,6},{1,9},{3,11}... | collective-permute-start | bytes 405512 | tf_op jit(solution)/shard_map/ppermute | solution.py:283
  5.5 0.0 copy-start.4
  5.5 0.0 copy-start.6
  5.6 0.0 copy-start.7
  5.6 0.0 copy-start.8
  5.6 0.5 %shard_map.112 = (bf16[528,128]{1,0:T(8,128)(2,1)S(1)}, bf16[528,128]{1,0:T(8,128)(2,1)S(1)}, bf16[528,128]{1,0:T(8,128)(2,1)S(1)}) custom-call(s32[1,512]{1,0:T(1,128)S(1)} %get-tuple-element.33.place_ref, bf16[16,512]{1,0:T(8,128)(2,1)S(1)} %get-tuple-element.34.aims_ref.after, bf16[512,512]{1,0:T(8,128)(2,1)S(1)} %copy-done.2, ...), custom_call_target="tpu_custom_call" | custom-call | flops 1000000000 | bytes 2000000 | tf_op jit(solution)/shard_map/pallas_call | solution.py:261
  6.0 1.6 %collective-permute-start.2 = (bf16[528,128]{1,0:T(8,128)(2,1)S(1)}, bf16[528,128]{1,0:T(8,128)(2,1)S(1)}, u32[]{:S(2)}, u32[]{:S(2)}) collective-permute-start(bf16[528,128]{1,0:T(8,128)(2,1)S(1)} %get-tuple-element.39), channel_id=1, source_target_pairs={{0,4},{2,6},{4,8},{6,10},{8,12},{10,14},{12,0},{14,2},{1,5},{3,7},... | collective-permute-start | bytes 405512 | tf_op jit(solution)/shard_map/ppermute | solution.py:283
  7.7 2.2 %collective-permute-start.3 = (bf16[528,128]{1,0:T(8,128)(2,1)S(1)}, bf16[528,128]{1,0:T(8,128)(2,1)S(1)}, u32[]{:S(2)}, u32[]{:S(2)}) collective-permute-start(bf16[528,128]{1,0:T(8,128)(2,1)S(1)} %get-tuple-element.40), channel_id=1, source_target_pairs={{0,12},{2,14},{4,0},{6,2},{8,4},{10,6},{12,8},{14,10},{1,13},{3,15... | collective-permute-start | bytes 405512 | tf_op jit(solution)/shard_map/ppermute | solution.py:283
  9.9 0.9 %collective-permute-start.4 = (bf16[528,128]{1,0:T(8,128)(2,1)S(1)}, bf16[528,128]{1,0:T(8,128)(2,1)S(1)}, u32[]{:S(2)}, u32[]{:S(2)}) collective-permute-start(bf16[528,128]{1,0:T(8,128)(2,1)S(1)} %get-tuple-element.41), channel_id=1, source_target_pairs={{0,14},{2,12},{4,2},{6,0},{8,6},{10,4},{12,10},{14,8},{1,15},{3,13... | collective-permute-start | bytes 405512 | tf_op jit(solution)/shard_map/ppermute | solution.py:283
  10.8 0.6 %shard_map.110 = (bf16[528,128]{1,0:T(8,128)(2,1)S(1)}, bf16[528,128]{1,0:T(8,128)(2,1)S(1)}, bf16[528,128]{1,0:T(8,128)(2,1)S(1)}, bf16[528,128]{1,0:T(8,128)(2,1)S(1)}) custom-call(s32[1,512]{1,0:T(1,128)S(1)} %get-tuple-element.33.place_ref, bf16[16,512]{1,0:T(8,128)(2,1)S(1)} %get-tuple-element.34.aims_ref.after, bf16[512,512]{1,0:T(8,128)(2,1)S(1)} %copy-done.2, ...), custom_call_target="tpu_custom_call" | custom-call | flops 1000000000 | bytes 2000000 | tf_op jit(solution)/shard_map/pallas_call | solution.py:261
  11.4 2.0 %collective-permute-start.5 = (bf16[528,128]{1,0:T(8,128)(2,1)S(1)}, bf16[528,128]{1,0:T(8,128)(2,1)S(1)}, u32[]{:S(2)}, u32[]{:S(2)}) collective-permute-start(bf16[528,128]{1,0:T(8,128)(2,1)S(1)} %get-tuple-element.42), channel_id=1, source_target_pairs={{0,6},{2,4},{4,10},{6,8},{8,14},{10,12},{12,2},{14,0},{1,7},{3,5},... | collective-permute-start | bytes 405512 | tf_op jit(solution)/shard_map/ppermute | solution.py:283
  13.5 2.3 %collective-permute-done.1.rest_1_ = bf16[528,128]{1,0:T(8,128)(2,1)S(1)} collective-permute-done((bf16[528,128]{1,0:T(8,128)(2,1)S(1)}, bf16[528,128]{1,0:T(8,128)(2,1)S(1)}, u32[]{:S(2)}, u32[]{:S(2)}) %collective-permute-start.1) | collective-permute-done | bytes 135200 | tf_op jit(solution)/shard_map/ppermute | solution.py:283
  15.8 1.7 %collective-permute-start.6 = (bf16[528,128]{1,0:T(8,128)(2,1)S(1)}, bf16[528,128]{1,0:T(8,128)(2,1)S(1)}, u32[]{:S(2)}, u32[]{:S(2)}) collective-permute-start(bf16[528,128]{1,0:T(8,128)(2,1)S(1)} %get-tuple-element.43), channel_id=1, source_target_pairs={{0,2},{2,0},{4,6},{6,4},{8,10},{10,8},{12,14},{14,12},{1,3},{3,1},... | collective-permute-start | bytes 405512 | tf_op jit(solution)/shard_map/ppermute | solution.py:283
  17.6 2.3 %shard_map.111 = (f32[256,512]{1,0:T(8,128)S(1)}, bf16[256,512]{1,0:T(8,128)(2,1)S(1)}, f32[256,512]{1,0:T(8,128)S(1)}, f32[64,512]{1,0:T(8,128)S(1)}, bf16[64,5...) custom-call(bf16[13,256,512]{2,1,0:T(8,128)(2,1)S(1)} %copy-done, ...), custom_call_target="tpu_custom_call" | custom-call | flops 500000000 | bytes 3000000 | tf_op jit(solution)/shard_map/pallas_call | solution.py:261
  19.9 0.0 collective-permute-done.2.rest_0_
  19.9 5.1 %collective-permute-start.7 = (bf16[528,128]{1,0:T(8,128)(2,1)S(1)}, bf16[528,128]{1,0:T(8,128)(2,1)S(1)}, u32[]{:S(2)}, u32[]{:S(2)}) collective-permute-start(bf16[528,128]{1,0:T(8,128)(2,1)S(1)} %get-tuple-element.48), channel_id=1, source_target_pairs={{0,10},{2,8},{4,14},{6,12},{8,2},{10,0},{12,6},{14,4},{1,11},{3,9}... | collective-permute-start | bytes 405512 | tf_op jit(solution)/shard_map/ppermute | solution.py:283
  25.0 0.0 collective-permute-done.3.rest_1_
  25.0 1.4 %shard_map.113.total = f32[256,512]{1,0:T(8,128)S(1)} custom-call(f32[256,512]{1,0:T(8,128)S(1)} %get-tuple-element.37.total, bf16[256,512]{1,0:T(8,128)(2,1)S(1)} %get-tuple-element.38.part, bf16[13,256,512]{2,1,0:T(8,128)(2,1)S(1)} %copy-done, bf16[13,256,512]{2,1,0:T(8,128)(2,1)S(1)} %collective-permute-done.after.other, f32[4,512]{1,0:T(4,128)S(1)} %copy-done.4, ...), custom_call_target="tpu_custom_call" | custom-call | flops 800000000 | bytes 2000000 | tf_op jit(solution)/shard_map/pallas_call | solution.py:261
  26.4 0.0 collective-permute-done.4.rest_0_
  26.4 1.4 %shard_map.114.total = f32[256,512]{1,0:T(8,128)S(1)} custom-call(f32[256,512]{1,0:T(8,128)S(1)} %shard_map.113.total, bf16[256,512]{1,0:T(8,128)(2,1)S(1)} %get-tuple-element.38.part, bf16[13,256,512]{2,1,0:T(8,128)(2,1)S(1)} %copy-done, bf16[13,256,512]{2,1,0:T(8,128)(2,1)S(1)} %collective-permute-done.after.other, f32[4,512]{1,0:T(4,128)S(1)} %copy-done.4, ...), custom_call_target="tpu_custom_call" | custom-call | flops 800000000 | bytes 2000000 | tf_op jit(solution)/shard_map/pallas_call | solution.py:261
  27.8 0.0 copy-start.5
  27.8 1.3 %shard_map.115 = (f32[256,512]{1,0:T(8,128)S(1)}, f32[64,512]{1,0:T(8,128)S(1)}) custom-call(f32[256,512]{1,0:T(8,128)S(1)} %shard_map.114.total, bf16[256,512]{1,0:T(8,128)(2,1)S(1)} %get-tuple-element.38.part, bf16[13,256,512]{2,1,0:T(8,128)(2,1)S(1)} %copy-done, bf16[13,256,512]{2,1,0:T(8,128)(2,1)S(1)} %collective-permute-done.after.other, ...), custom_call_target="tpu_custom_call" | custom-call | flops 1000000000 | bytes 2000000 | tf_op jit(solution)/shard_map/pallas_call | solution.py:261
  29.1 2.6 %collective-permute-done.7.rest_0_ = bf16[528,128]{1,0:T(8,128)(2,1)S(1)} collective-permute-done((bf16[528,128]{1,0:T(8,128)(2,1)S(1)}, bf16[528,128]{1,0:T(8,128)(2,1)S(1)}, u32[]{:S(2)}, u32[]{:S(2)}) %collective-permute-start.7) | collective-permute-done | bytes 135200 | tf_op jit(solution)/shard_map/ppermute | solution.py:283
  31.6 1.7 %shard_map.116 = (bf16[256,256]{1,0:T(8,128)(2,1)S(1)}, bf16[256,512]{1,0:T(8,128)(2,1)S(1)}, bf16[64,512]{1,0:T(8,128)(2,1)S(1)}) custom-call(f32[64,512]{1,0:T(8,128)S(1)} %get-tuple-element.45.lent_total, bf16[256,512]{1,0:T(8,128)(2,1)S(1)} %get-tuple-element.38.part, f32[64,512]{1,0:T(8,128)S(1)} %get-tuple-element.46.ahead, ...), custom_call_target="tpu_custom_call" | custom-call | flops 1000000000 | bytes 3000000 | tf_op jit(solution)/shard_map/pallas_call | solution.py:261
  33.3 0.5 %collective-permute-start.10 = (bf16[64,512]{1,0:T(8,128)(2,1)S(1)}, bf16[64,512]{1,0:T(8,128)(2,1)S(1)}, u32[]{:S(2)}, u32[]{:S(2)}) collective-permute-start(bf16[64,512]{1,0:T(8,128)(2,1)S(1)} %get-tuple-element.60), channel_id=1, source_target_pairs={{0,2},{2,0},{1,3},{3,1},{4,6},{6,4},{5,7},{7,5},{8,10},{10,8},{9,1... | collective-permute-start | bytes 196616 | tf_op jit(solution)/shard_map/ppermute | solution.py:288
  33.9 0.1 collective-permute-start.9
  34.0 2.9 %collective-permute-start.8 = (bf16[64,512]{1,0:T(8,128)(2,1)S(1)}, bf16[64,512]{1,0:T(8,128)(2,1)S(1)}, u32[]{:S(2)}, u32[]{:S(2)}) collective-permute-start(bf16[64,512]{1,0:T(8,128)(2,1)S(1)} %get-tuple-element.60), channel_id=1, source_target_pairs={{4,8},{8,4},{12,0},{0,12},{5,9},{9,5},{13,1},{1,13},{6,10},{10,6},... | collective-permute-start | bytes 196616 | tf_op jit(solution)/shard_map/ppermute | solution.py:297
  36.9 1.9 %shard_map.117 = (bf16[256,512]{1,0:T(8,128)(2,1)S(1)}, f32[512,512]{1,0:T(8,128)S(1)}, f32[256,512]{1,0:T(8,128)S(1)}) custom-call(f32[256,512]{1,0:T(8,128)S(1)} %get-tuple-element.44.total, bf16[256,256]{1,0:T(8,128)(2,1)S(1)} %get-tuple-element.49.spread, bf16[256,512]{1,0:T(8,128)(2,1)S(1)} %get-tuple-element.50.notes, ...), custom_call_target="tpu_custom_call" | custom-call | flops 1000000000 | bytes 3000000 | tf_op jit(solution)/shard_map/pallas_call | solution.py:261
  38.9 1.3 %collective-permute-done.8.rest_0_ = bf16[64,512]{1,0:T(8,128)(2,1)S(1)} collective-permute-done((bf16[64,512]{1,0:T(8,128)(2,1)S(1)}, bf16[64,512]{1,0:T(8,128)(2,1)S(1)}, u32[]{:S(2)}, u32[]{:S(2)}) %collective-permute-start.8) | collective-permute-done | bytes 65568 | tf_op jit(solution)/shard_map/ppermute | solution.py:297
  40.2 2.6 %shard_map.118 = bf16[256,512]{1,0:T(8,128)(2,1)} custom-call(f32[512,512]{1,0:T(8,128)S(1)} %get-tuple-element.55.pre, f32[256,512]{1,0:T(8,128)S(1)} %get-tuple-element.56.ahead, bf16[512,192]{1,0:T(8,128)(2,1)S(1)} %get-tuple-element.57.picks, bf16[256,512]{1,0:T(8,128)(2,1)S(1)} %get-tuple-element.58.spread, bf16[256,512]{1,0:T(8,128)(2,1)S(1)} %get-tuple-element.59.mid, ...), custom_call_target="tpu_custom_call" | custom-call | flops 1000000000 | bytes 3000000 | tf_op jit(solution)/shard_map/pallas_call | solution.py:261
  (18 shorter events, 0.0 us)
Async XLA Ops:
  0.0 5.5 %copy-start.2 = (bf16[512,512]{1,0:T(8,128)(2,1)S(1)}, bf16[512,512]{1,0:T(8,128)(2,1)}, u32[]{:S(2)}) copy-start(bf16[512,512]{1,0:T(8,128)(2,1)} %latent_ref.3) | copy-start | bytes 1572868
  0.0 10.8 %collective-permute-start = (bf16[13,256,512]{2,1,0:T(8,128)(2,1)}, bf16[13,256,512]{2,1,0:T(8,128)(2,1)S(1)}, u32[]{:S(2)}, u32[]{:S(2)}) collective-permute-start(bf16[13,256,512]{2,1,0:T(8,128)(2,1)} %mine.13), channel_id=1, source_target_pairs={{0,1},{1,0},{2,3},{3,2},{4,5},{5,4},{6,7},{7,6},{8,9},{9,8},{10,11... | collective-permute-start | bytes 10223624 | tf_op jit(solution)/shard_map/ppermute | solution.py:274
  1.8 14.0 %collective-permute-start.1 = (bf16[528,128]{1,0:T(8,128)(2,1)S(1)}, bf16[528,128]{1,0:T(8,128)(2,1)S(1)}, u32[]{:S(2)}, u32[]{:S(2)}) collective-permute-start(bf16[528,128]{1,0:T(8,128)(2,1)S(1)} %get-tuple-element.36), channel_id=1, source_target_pairs={{0,8},{2,10},{4,12},{6,14},{8,0},{10,2},{12,4},{14,6},{1,9},{3,11}... | collective-permute-start | bytes 405512 | tf_op jit(solution)/shard_map/ppermute | solution.py:283
  5.5 12.0 %copy-start = (bf16[13,256,512]{2,1,0:T(8,128)(2,1)S(1)}, bf16[13,256,512]{2,1,0:T(8,128)(2,1)}, u32[]{:S(2)}) copy-start(bf16[13,256,512]{2,1,0:T(8,128)(2,1)} %mine.13) | copy-start | bytes 10223620
  5.5 12.0 %copy-start.1 = (bf16[256,512]{1,0:T(8,128)(2,1)S(1)}, bf16[256,512]{1,0:T(8,128)(2,1)}, u32[]{:S(2)}) copy-start(bf16[256,512]{1,0:T(8,128)(2,1)} %mesh.3) | copy-start | bytes 786436
  5.5 12.0 %copy-start.3 = (bf16[512,512]{1,0:T(8,128)(2,1)S(1)}, bf16[512,512]{1,0:T(8,128)(2,1)}, u32[]{:S(2)}) copy-start(bf16[512,512]{1,0:T(8,128)(2,1)} %edges.1) | copy-start | bytes 1572868
  5.5 12.0 %copy-start.4 = (f32[4,512]{1,0:T(4,128)S(1)}, f32[4,512]{1,0:T(4,128)}, u32[]{:S(2)}) copy-start(f32[4,512]{1,0:T(4,128)} %biases.11) | copy-start | bytes 24580
  5.5 12.0 %copy-start.6 = (s32[64]{0:T(128)S(1)}, s32[64]{0:T(128)}, u32[]{:S(2)}) copy-start(s32[64]{0:T(128)} %param.18) | copy-start | bytes 772
  5.6 12.0 %copy-start.7 = (s32[512]{0:T(512)S(1)}, s32[512]{0:T(512)}, u32[]{:S(2)}) copy-start(s32[512]{0:T(512)} %param.16) | copy-start | bytes 6148
  5.6 12.0 %copy-start.8 = (s32[512]{0:T(512)S(1)}, s32[512]{0:T(512)}, u32[]{:S(2)}) copy-start(s32[512]{0:T(512)} %param.17) | copy-start | bytes 6148
  6.0 13.8 %collective-permute-start.2 = (bf16[528,128]{1,0:T(8,128)(2,1)S(1)}, bf16[528,128]{1,0:T(8,128)(2,1)S(1)}, u32[]{:S(2)}, u32[]{:S(2)}) collective-permute-start(bf16[528,128]{1,0:T(8,128)(2,1)S(1)} %get-tuple-element.39), channel_id=1, source_target_pairs={{0,4},{2,6},{4,8},{6,10},{8,12},{10,14},{12,0},{14,2},{1,5},{3,7},... | collective-permute-start | bytes 405512 | tf_op jit(solution)/shard_map/ppermute | solution.py:283
  7.7 17.3 %collective-permute-start.3 = (bf16[528,128]{1,0:T(8,128)(2,1)S(1)}, bf16[528,128]{1,0:T(8,128)(2,1)S(1)}, u32[]{:S(2)}, u32[]{:S(2)}) collective-permute-start(bf16[528,128]{1,0:T(8,128)(2,1)S(1)} %get-tuple-element.40), channel_id=1, source_target_pairs={{0,12},{2,14},{4,0},{6,2},{8,4},{10,6},{12,8},{14,10},{1,13},{3,15... | collective-permute-start | bytes 405512 | tf_op jit(solution)/shard_map/ppermute | solution.py:283
  9.9 16.4 %collective-permute-start.4 = (bf16[528,128]{1,0:T(8,128)(2,1)S(1)}, bf16[528,128]{1,0:T(8,128)(2,1)S(1)}, u32[]{:S(2)}, u32[]{:S(2)}) collective-permute-start(bf16[528,128]{1,0:T(8,128)(2,1)S(1)} %get-tuple-element.41), channel_id=1, source_target_pairs={{0,14},{2,12},{4,2},{6,0},{8,6},{10,4},{12,10},{14,8},{1,15},{3,13... | collective-permute-start | bytes 405512 | tf_op jit(solution)/shard_map/ppermute | solution.py:283
  11.4 14.9 %collective-permute-start.5 = (bf16[528,128]{1,0:T(8,128)(2,1)S(1)}, bf16[528,128]{1,0:T(8,128)(2,1)S(1)}, u32[]{:S(2)}, u32[]{:S(2)}) collective-permute-start(bf16[528,128]{1,0:T(8,128)(2,1)S(1)} %get-tuple-element.42), channel_id=1, source_target_pairs={{0,6},{2,4},{4,10},{6,8},{8,14},{10,12},{12,2},{14,0},{1,7},{3,5},... | collective-permute-start | bytes 405512 | tf_op jit(solution)/shard_map/ppermute | solution.py:283
  15.8 12.0 %collective-permute-start.6 = (bf16[528,128]{1,0:T(8,128)(2,1)S(1)}, bf16[528,128]{1,0:T(8,128)(2,1)S(1)}, u32[]{:S(2)}, u32[]{:S(2)}) collective-permute-start(bf16[528,128]{1,0:T(8,128)(2,1)S(1)} %get-tuple-element.43), channel_id=1, source_target_pairs={{0,2},{2,0},{4,6},{6,4},{8,10},{10,8},{12,14},{14,12},{1,3},{3,1},... | collective-permute-start | bytes 405512 | tf_op jit(solution)/shard_map/ppermute | solution.py:283
  19.9 11.8 %collective-permute-start.7 = (bf16[528,128]{1,0:T(8,128)(2,1)S(1)}, bf16[528,128]{1,0:T(8,128)(2,1)S(1)}, u32[]{:S(2)}, u32[]{:S(2)}) collective-permute-start(bf16[528,128]{1,0:T(8,128)(2,1)S(1)} %get-tuple-element.48), channel_id=1, source_target_pairs={{0,10},{2,8},{4,14},{6,12},{8,2},{10,0},{12,6},{14,4},{1,11},{3,9}... | collective-permute-start | bytes 405512 | tf_op jit(solution)/shard_map/ppermute | solution.py:283
  27.8 3.9 %copy-start.5 = (f32[4,512]{1,0:T(4,128)S(1)}, f32[4,512]{1,0:T(4,128)}, u32[]{:S(2)}) copy-start(f32[4,512]{1,0:T(4,128)} %gains.5) | copy-start | bytes 24580
  33.3 5.6 %collective-permute-start.10 = (bf16[64,512]{1,0:T(8,128)(2,1)S(1)}, bf16[64,512]{1,0:T(8,128)(2,1)S(1)}, u32[]{:S(2)}, u32[]{:S(2)}) collective-permute-start(bf16[64,512]{1,0:T(8,128)(2,1)S(1)} %get-tuple-element.60), channel_id=1, source_target_pairs={{0,2},{2,0},{1,3},{3,1},{4,6},{6,4},{5,7},{7,5},{8,10},{10,8},{9,1... | collective-permute-start | bytes 196616 | tf_op jit(solution)/shard_map/ppermute | solution.py:288
  33.9 5.0 %collective-permute-start.9 = (bf16[64,512]{1,0:T(8,128)(2,1)S(1)}, bf16[64,512]{1,0:T(8,128)(2,1)S(1)}, u32[]{:S(2)}, u32[]{:S(2)}) collective-permute-start(bf16[64,512]{1,0:T(8,128)(2,1)S(1)} %get-tuple-element.60), channel_id=1, source_target_pairs={{0,4},{4,0},{8,12},{12,8},{1,5},{5,1},{9,13},{13,9},{2,6},{6,2},{1... | collective-permute-start | bytes 196616 | tf_op jit(solution)/shard_map/ppermute | solution.py:297
  34.0 6.2 %collective-permute-start.8 = (bf16[64,512]{1,0:T(8,128)(2,1)S(1)}, bf16[64,512]{1,0:T(8,128)(2,1)S(1)}, u32[]{:S(2)}, u32[]{:S(2)}) collective-permute-start(bf16[64,512]{1,0:T(8,128)(2,1)S(1)} %get-tuple-element.60), channel_id=1, source_target_pairs={{4,8},{8,4},{12,0},{0,12},{5,9},{9,5},{13,1},{1,13},{6,10},{10,6},... | collective-permute-start | bytes 196616 | tf_op jit(solution)/shard_map/ppermute | solution.py:297

commit v8 on v6

--- a/solution.py
+++ b/solution.py
@@ -236,6 +236,7 @@
 
 def process_kernel(pre, ahead, picks, spread, mid, gains, mine, other, *rest):
     *lent, out = rest
+    lent = [lent[0], lent[-1], *lent[1:-1]]
     maps = (mine, other)
     table = jnp.concatenate([ref[...] for ref in lent], axis=0)
     hidden = silu(pre[...] + mm(picks[...], table))
@@ -426,7 +427,7 @@
     (out,) = call(
         process_kernel,
         [((nodes, width), BF16)],
-        (pre, ahead, picks, edge_spread, mid, gains, weights, other, *halo),
+        (pre, ahead, picks, edge_spread, mid, gains, weights, other, halo[0], *halo[2:], halo[1]),
         [VMEM] * (8 + pieces),
         flops=10**9,
         moved=3 * 10**6,

time: 42.9 us -> 42.9 us (level)
  no operation moved by 1% of the time
where the time goes in v8:
time: 42.9 us; the launch traced here: 42.7 us
  starting transfers between devices  21.5 us (50%)
  Pallas kernels  14.9 us (35%)
  waiting for transfers between devices  6.05 us (14%)
    ppermute x7, starting transfers between devices, moved(): return lax.ppermute(value, ('lat', 'lon'), pairs)  17.4 us
    pallas_call x10, Pallas kernels, call(): pl.pallas_call(kernel, out_shape=[jax.ShapeDtypeStruct(shape, kind) for s...  14.9 us
    ppermute x7, waiting for transfers between devices, moved(): return lax.ppermute(value, ('lat', 'lon'), pairs)  4.9 us
    ppermute x2, starting transfers between devices, paired(): return lax.ppermute(value, axis, pairs)  3.06 us
    ppermute x2, waiting for transfers between devices, paired(): return lax.ppermute(value, axis, pairs)  1.15 us
  transfers between devices with their start and end apart: 11, of which 3 were waited for; matrix products, arithmetic and copies ran while one was open for 0% of the time, Pallas kernels for 25%

profile of v8, /device:TPU:0, one launch (start us, length us, event | category | flops | bytes accessed | tf_op | source)
XLA Modules:
  0.0 42.7 jit_solution(17195419278043312929)
XLA Ops:
  0.0 0.5 %collective-permute-start = (bf16[13,256,512]{2,1,0:T(8,128)(2,1)}, bf16[13,256,512]{2,1,0:T(8,128)(2,1)S(1)}, u32[]{:S(2)}, u32[]{:S(2)}) collective-permute-start(bf16[13,256,512]{2,1,0:T(8,128)(2,1)} %mine.13), channel_id=1, source_target_pairs={{0,1},{1,0},{2,3},{3,2},{4,5},{5,4},{6,7},{7,6},{8,9},{9,8},{10,11... | collective-permute-start | bytes 10223624 | tf_op jit(solution)/shard_map/ppermute | solution.py:265
  0.5 1.4 %shard_map.109 = (bf16[528,128]{1,0:T(8,128)(2,1)S(1)}, s32[1,512]{1,0:T(1,128)S(1)}, bf16[16,512]{1,0:T(8,128)(2,1)S(1)}) custom-call(s32[1,512]{1,0:T(1,128)} %bitcast.11, s32[2,512]{1,0:T(2,128)} %bitcast.10, bf16[512,512]{1,0:T(8,128)(2,1)} %latent_ref.3), custom_call_target="tpu_custom_call" | custom-call | flops 1000000000 | bytes 2000000 | tf_op jit(solution)/shard_map/pallas_call | solution.py:252
  1.8 3.7 %collective-permute-start.1 = (bf16[528,128]{1,0:T(8,128)(2,1)S(1)}, bf16[528,128]{1,0:T(8,128)(2,1)S(1)}, u32[]{:S(2)}, u32[]{:S(2)}) collective-permute-start(bf16[528,128]{1,0:T(8,128)(2,1)S(1)} %get-tuple-element.36), channel_id=1, source_target_pairs={{0,8},{2,10},{4,12},{6,14},{8,0},{10,2},{12,4},{14,6},{1,9},{3,11}... | collective-permute-start | bytes 405512 | tf_op jit(solution)/shard_map/ppermute | solution.py:274
  5.6 0.0 copy-start.4
  5.6 0.0 copy-start.6
  5.6 0.0 copy-start.7
  5.6 0.0 copy-start.8
  5.6 0.5 %shard_map.112 = (bf16[528,128]{1,0:T(8,128)(2,1)S(1)}, bf16[528,128]{1,0:T(8,128)(2,1)S(1)}, bf16[528,128]{1,0:T(8,128)(2,1)S(1)}) custom-call(s32[1,512]{1,0:T(1,128)S(1)} %get-tuple-element.33.place_ref, bf16[16,512]{1,0:T(8,128)(2,1)S(1)} %get-tuple-element.34.aims_ref.after, bf16[512,512]{1,0:T(8,128)(2,1)S(1)} %copy-done.2, ...), custom_call_target="tpu_custom_call" | custom-call | flops 1000000000 | bytes 2000000 | tf_op jit(solution)/shard_map/pallas_call | solution.py:252
  6.1 1.6 %collective-permute-start.2 = (bf16[528,128]{1,0:T(8,128)(2,1)S(1)}, bf16[528,128]{1,0:T(8,128)(2,1)S(1)}, u32[]{:S(2)}, u32[]{:S(2)}) collective-permute-start(bf16[528,128]{1,0:T(8,128)(2,1)S(1)} %get-tuple-element.39), channel_id=1, source_target_pairs={{0,4},{2,6},{4,8},{6,10},{8,12},{10,14},{12,0},{14,2},{1,5},{3,7},... | collective-permute-start | bytes 405512 | tf_op jit(solution)/shard_map/ppermute | solution.py:274
  7.7 2.2 %collective-permute-start.3 = (bf16[528,128]{1,0:T(8,128)(2,1)S(1)}, bf16[528,128]{1,0:T(8,128)(2,1)S(1)}, u32[]{:S(2)}, u32[]{:S(2)}) collective-permute-start(bf16[528,128]{1,0:T(8,128)(2,1)S(1)} %get-tuple-element.40), channel_id=1, source_target_pairs={{0,12},{2,14},{4,0},{6,2},{8,4},{10,6},{12,8},{14,10},{1,13},{3,15... | collective-permute-start | bytes 405512 | tf_op jit(solution)/shard_map/ppermute | solution.py:274
  9.9 0.9 %collective-permute-start.4 = (bf16[528,128]{1,0:T(8,128)(2,1)S(1)}, bf16[528,128]{1,0:T(8,128)(2,1)S(1)}, u32[]{:S(2)}, u32[]{:S(2)}) collective-permute-start(bf16[528,128]{1,0:T(8,128)(2,1)S(1)} %get-tuple-element.41), channel_id=1, source_target_pairs={{0,14},{2,12},{4,2},{6,0},{8,6},{10,4},{12,10},{14,8},{1,15},{3,13... | collective-permute-start | bytes 405512 | tf_op jit(solution)/shard_map/ppermute | solution.py:274
  10.9 0.0 collective-permute-done.after.other
  10.9 0.6 %shard_map.110 = (bf16[528,128]{1,0:T(8,128)(2,1)S(1)}, bf16[528,128]{1,0:T(8,128)(2,1)S(1)}, bf16[528,128]{1,0:T(8,128)(2,1)S(1)}, bf16[528,128]{1,0:T(8,128)(2,1)S(1)}) custom-call(s32[1,512]{1,0:T(1,128)S(1)} %get-tuple-element.33.place_ref, bf16[16,512]{1,0:T(8,128)(2,1)S(1)} %get-tuple-element.34.aims_ref.after, bf16[512,512]{1,0:T(8,128)(2,1)S(1)} %copy-done.2, ...), custom_call_target="tpu_custom_call" | custom-call | flops 1000000000 | bytes 2000000 | tf_op jit(solution)/shard_map/pallas_call | solution.py:252
  11.5 2.0 %collective-permute-start.5 = (bf16[528,128]{1,0:T(8,128)(2,1)S(1)}, bf16[528,128]{1,0:T(8,128)(2,1)S(1)}, u32[]{:S(2)}, u32[]{:S(2)}) collective-permute-start(bf16[528,128]{1,0:T(8,128)(2,1)S(1)} %get-tuple-element.42), channel_id=1, source_target_pairs={{0,6},{2,4},{4,10},{6,8},{8,14},{10,12},{12,2},{14,0},{1,7},{3,5},... | collective-permute-start | bytes 405512 | tf_op jit(solution)/shard_map/ppermute | solution.py:274
  13.5 2.3 %collective-permute-done.1.rest_1_ = bf16[528,128]{1,0:T(8,128)(2,1)S(1)} collective-permute-done((bf16[528,128]{1,0:T(8,128)(2,1)S(1)}, bf16[528,128]{1,0:T(8,128)(2,1)S(1)}, u32[]{:S(2)}, u32[]{:S(2)}) %collective-permute-start.1) | collective-permute-done | bytes 135200 | tf_op jit(solution)/shard_map/ppermute | solution.py:274
  15.8 1.7 %collective-permute-start.6 = (bf16[528,128]{1,0:T(8,128)(2,1)S(1)}, bf16[528,128]{1,0:T(8,128)(2,1)S(1)}, u32[]{:S(2)}, u32[]{:S(2)}) collective-permute-start(bf16[528,128]{1,0:T(8,128)(2,1)S(1)} %get-tuple-element.43), channel_id=1, source_target_pairs={{0,2},{2,0},{4,6},{6,4},{8,10},{10,8},{12,14},{14,12},{1,3},{3,1},... | collective-permute-start | bytes 405512 | tf_op jit(solution)/shard_map/ppermute | solution.py:274
  17.6 2.3 %shard_map.111 = (f32[256,512]{1,0:T(8,128)S(1)}, bf16[256,512]{1,0:T(8,128)(2,1)S(1)}, f32[256,512]{1,0:T(8,128)S(1)}, f32[64,512]{1,0:T(8,128)S(1)}, bf16[64,5...) custom-call(bf16[13,256,512]{2,1,0:T(8,128)(2,1)S(1)} %copy-done, ...), custom_call_target="tpu_custom_call" | custom-call | flops 500000000 | bytes 3000000 | tf_op jit(solution)/shard_map/pallas_call | solution.py:252
  19.9 0.0 collective-permute-done.2.rest_0_
  19.9 5.1 %collective-permute-start.7 = (bf16[528,128]{1,0:T(8,128)(2,1)S(1)}, bf16[528,128]{1,0:T(8,128)(2,1)S(1)}, u32[]{:S(2)}, u32[]{:S(2)}) collective-permute-start(bf16[528,128]{1,0:T(8,128)(2,1)S(1)} %get-tuple-element.48), channel_id=1, source_target_pairs={{0,10},{2,8},{4,14},{6,12},{8,2},{10,0},{12,6},{14,4},{1,11},{3,9}... | collective-permute-start | bytes 405512 | tf_op jit(solution)/shard_map/ppermute | solution.py:274
  25.0 1.4 %shard_map.113.total = f32[256,512]{1,0:T(8,128)S(1)} custom-call(f32[256,512]{1,0:T(8,128)S(1)} %get-tuple-element.37.total, bf16[256,512]{1,0:T(8,128)(2,1)S(1)} %get-tuple-element.38.part, bf16[13,256,512]{2,1,0:T(8,128)(2,1)S(1)} %copy-done, bf16[13,256,512]{2,1,0:T(8,128)(2,1)S(1)} %collective-permute-done.after.other, f32[4,512]{1,0:T(4,128)S(1)} %copy-done.4, ...), custom_call_target="tpu_custom_call" | custom-call | flops 800000000 | bytes 2000000 | tf_op jit(solution)/shard_map/pallas_call | solution.py:252
  26.4 0.0 collective-permute-done.4.rest_0_
  26.4 1.4 %shard_map.114.total = f32[256,512]{1,0:T(8,128)S(1)} custom-call(f32[256,512]{1,0:T(8,128)S(1)} %shard_map.113.total, bf16[256,512]{1,0:T(8,128)(2,1)S(1)} %get-tuple-element.38.part, bf16[13,256,512]{2,1,0:T(8,128)(2,1)S(1)} %copy-done, bf16[13,256,512]{2,1,0:T(8,128)(2,1)S(1)} %collective-permute-done.after.other, f32[4,512]{1,0:T(4,128)S(1)} %copy-done.4, ...), custom_call_target="tpu_custom_call" | custom-call | flops 800000000 | bytes 2000000 | tf_op jit(solution)/shard_map/pallas_call | solution.py:252
  27.8 0.0 copy-start.5
  27.8 1.3 %shard_map.115 = (f32[256,512]{1,0:T(8,128)S(1)}, f32[64,512]{1,0:T(8,128)S(1)}) custom-call(f32[256,512]{1,0:T(8,128)S(1)} %shard_map.114.total, bf16[256,512]{1,0:T(8,128)(2,1)S(1)} %get-tuple-element.38.part, bf16[13,256,512]{2,1,0:T(8,128)(2,1)S(1)} %copy-done, bf16[13,256,512]{2,1,0:T(8,128)(2,1)S(1)} %collective-permute-done.after.other, ...), custom_call_target="tpu_custom_call" | custom-call | flops 1000000000 | bytes 2000000 | tf_op jit(solution)/shard_map/pallas_call | solution.py:252
  29.1 2.6 %collective-permute-done.7.rest_0_ = bf16[528,128]{1,0:T(8,128)(2,1)S(1)} collective-permute-done((bf16[528,128]{1,0:T(8,128)(2,1)S(1)}, bf16[528,128]{1,0:T(8,128)(2,1)S(1)}, u32[]{:S(2)}, u32[]{:S(2)}) %collective-permute-start.7) | collective-permute-done | bytes 135200 | tf_op jit(solution)/shard_map/ppermute | solution.py:274
  31.7 1.7 %shard_map.116 = (bf16[256,256]{1,0:T(8,128)(2,1)S(1)}, bf16[256,512]{1,0:T(8,128)(2,1)S(1)}, bf16[64,512]{1,0:T(8,128)(2,1)S(1)}) custom-call(f32[64,512]{1,0:T(8,128)S(1)} %get-tuple-element.45.lent_total, bf16[256,512]{1,0:T(8,128)(2,1)S(1)} %get-tuple-element.38.part, f32[64,512]{1,0:T(8,128)S(1)} %get-tuple-element.46.ahead, ...), custom_call_target="tpu_custom_call" | custom-call | flops 1000000000 | bytes 3000000 | tf_op jit(solution)/shard_map/pallas_call | solution.py:252
  33.4 0.1 collective-permute-start.10
  33.4 0.6 %collective-permute-start.9 = (bf16[64,512]{1,0:T(8,128)(2,1)S(1)}, bf16[64,512]{1,0:T(8,128)(2,1)S(1)}, u32[]{:S(2)}, u32[]{:S(2)}) collective-permute-start(bf16[64,512]{1,0:T(8,128)(2,1)S(1)} %get-tuple-element.60), channel_id=1, source_target_pairs={{0,2},{2,0},{1,3},{3,1},{4,6},{6,4},{5,7},{7,5},{8,10},{10,8},{9,1... | collective-permute-start | bytes 196616 | tf_op jit(solution)/shard_map/ppermute | solution.py:279
  34.0 3.0 %collective-permute-start.8 = (bf16[64,512]{1,0:T(8,128)(2,1)S(1)}, bf16[64,512]{1,0:T(8,128)(2,1)S(1)}, u32[]{:S(2)}, u32[]{:S(2)}) collective-permute-start(bf16[64,512]{1,0:T(8,128)(2,1)S(1)} %get-tuple-element.60), channel_id=1, source_target_pairs={{4,8},{8,4},{12,0},{0,12},{5,9},{9,5},{13,1},{1,13},{6,10},{10,6},... | collective-permute-start | bytes 196616 | tf_op jit(solution)/shard_map/ppermute | solution.py:288
  37.0 1.9 %shard_map.117 = (bf16[256,512]{1,0:T(8,128)(2,1)S(1)}, f32[512,512]{1,0:T(8,128)S(1)}, f32[256,512]{1,0:T(8,128)S(1)}) custom-call(f32[256,512]{1,0:T(8,128)S(1)} %get-tuple-element.44.total, bf16[256,256]{1,0:T(8,128)(2,1)S(1)} %get-tuple-element.49.spread, bf16[256,512]{1,0:T(8,128)(2,1)S(1)} %get-tuple-element.50.notes, ...), custom_call_target="tpu_custom_call" | custom-call | flops 1000000000 | bytes 3000000 | tf_op jit(solution)/shard_map/pallas_call | solution.py:252
  39.0 1.1 %collective-permute-done.8.rest_0_ = bf16[64,512]{1,0:T(8,128)(2,1)S(1)} collective-permute-done((bf16[64,512]{1,0:T(8,128)(2,1)S(1)}, bf16[64,512]{1,0:T(8,128)(2,1)S(1)}, u32[]{:S(2)}, u32[]{:S(2)}) %collective-permute-start.8) | collective-permute-done | bytes 65568 | tf_op jit(solution)/shard_map/ppermute | solution.py:288
  40.2 2.5 %shard_map.118 = bf16[256,512]{1,0:T(8,128)(2,1)} custom-call(f32[512,512]{1,0:T(8,128)S(1)} %get-tuple-element.55.pre, f32[256,512]{1,0:T(8,128)S(1)} %get-tuple-element.56.ahead, bf16[512,192]{1,0:T(8,128)(2,1)S(1)} %get-tuple-element.57.picks, bf16[256,512]{1,0:T(8,128)(2,1)S(1)} %get-tuple-element.58.spread, bf16[256,512]{1,0:T(8,128)(2,1)S(1)} %get-tuple-element.59.mid, ...), custom_call_target="tpu_custom_call" | custom-call | flops 1000000000 | bytes 3000000 | tf_op jit(solution)/shard_map/pallas_call | solution.py:252
  (18 shorter events, 0.0 us)
Async XLA Ops:
  0.0 5.6 %copy-start.2 = (bf16[512,512]{1,0:T(8,128)(2,1)S(1)}, bf16[512,512]{1,0:T(8,128)(2,1)}, u32[]{:S(2)}) copy-start(bf16[512,512]{1,0:T(8,128)(2,1)} %latent_ref.3) | copy-start | bytes 1572868
  0.0 10.9 %collective-permute-start = (bf16[13,256,512]{2,1,0:T(8,128)(2,1)}, bf16[13,256,512]{2,1,0:T(8,128)(2,1)S(1)}, u32[]{:S(2)}, u32[]{:S(2)}) collective-permute-start(bf16[13,256,512]{2,1,0:T(8,128)(2,1)} %mine.13), channel_id=1, source_target_pairs={{0,1},{1,0},{2,3},{3,2},{4,5},{5,4},{6,7},{7,6},{8,9},{9,8},{10,11... | collective-permute-start | bytes 10223624 | tf_op jit(solution)/shard_map/ppermute | solution.py:265
  1.8 14.0 %collective-permute-start.1 = (bf16[528,128]{1,0:T(8,128)(2,1)S(1)}, bf16[528,128]{1,0:T(8,128)(2,1)S(1)}, u32[]{:S(2)}, u32[]{:S(2)}) collective-permute-start(bf16[528,128]{1,0:T(8,128)(2,1)S(1)} %get-tuple-element.36), channel_id=1, source_target_pairs={{0,8},{2,10},{4,12},{6,14},{8,0},{10,2},{12,4},{14,6},{1,9},{3,11}... | collective-permute-start | bytes 405512 | tf_op jit(solution)/shard_map/ppermute | solution.py:274
  5.6 12.0 %copy-start = (bf16[13,256,512]{2,1,0:T(8,128)(2,1)S(1)}, bf16[13,256,512]{2,1,0:T(8,128)(2,1)}, u32[]{:S(2)}) copy-start(bf16[13,256,512]{2,1,0:T(8,128)(2,1)} %mine.13) | copy-start | bytes 10223620
  5.6 12.0 %copy-start.1 = (bf16[256,512]{1,0:T(8,128)(2,1)S(1)}, bf16[256,512]{1,0:T(8,128)(2,1)}, u32[]{:S(2)}) copy-start(bf16[256,512]{1,0:T(8,128)(2,1)} %mesh.3) | copy-start | bytes 786436
  5.6 12.0 %copy-start.3 = (bf16[512,512]{1,0:T(8,128)(2,1)S(1)}, bf16[512,512]{1,0:T(8,128)(2,1)}, u32[]{:S(2)}) copy-start(bf16[512,512]{1,0:T(8,128)(2,1)} %edges.1) | copy-start | bytes 1572868
  5.6 12.0 %copy-start.4 = (f32[4,512]{1,0:T(4,128)S(1)}, f32[4,512]{1,0:T(4,128)}, u32[]{:S(2)}) copy-start(f32[4,512]{1,0:T(4,128)} %biases.11) | copy-start | bytes 24580
  5.6 12.0 %copy-start.6 = (s32[64]{0:T(128)S(1)}, s32[64]{0:T(128)}, u32[]{:S(2)}) copy-start(s32[64]{0:T(128)} %param.18) | copy-start | bytes 772
  5.6 12.0 %copy-start.7 = (s32[512]{0:T(512)S(1)}, s32[512]{0:T(512)}, u32[]{:S(2)}) copy-start(s32[512]{0:T(512)} %param.16) | copy-start | bytes 6148
  5.6 12.0 %copy-start.8 = (s32[512]{0:T(512)S(1)}, s32[512]{0:T(512)}, u32[]{:S(2)}) copy-start(s32[512]{0:T(512)} %param.17) | copy-start | bytes 6148
  6.1 13.8 %collective-permute-start.2 = (bf16[528,128]{1,0:T(8,128)(2,1)S(1)}, bf16[528,128]{1,0:T(8,128)(2,1)S(1)}, u32[]{:S(2)}, u32[]{:S(2)}) collective-permute-start(bf16[528,128]{1,0:T(8,128)(2,1)S(1)} %get-tuple-element.39), channel_id=1, source_target_pairs={{0,4},{2,6},{4,8},{6,10},{8,12},{10,14},{12,0},{14,2},{1,5},{3,7},... | collective-permute-start | bytes 405512 | tf_op jit(solution)/shard_map/ppermute | solution.py:274
  7.7 17.3 %collective-permute-start.3 = (bf16[528,128]{1,0:T(8,128)(2,1)S(1)}, bf16[528,128]{1,0:T(8,128)(2,1)S(1)}, u32[]{:S(2)}, u32[]{:S(2)}) collective-permute-start(bf16[528,128]{1,0:T(8,128)(2,1)S(1)} %get-tuple-element.40), channel_id=1, source_target_pairs={{0,12},{2,14},{4,0},{6,2},{8,4},{10,6},{12,8},{14,10},{1,13},{3,15... | collective-permute-start | bytes 405512 | tf_op jit(solution)/shard_map/ppermute | solution.py:274
  9.9 16.5 %collective-permute-start.4 = (bf16[528,128]{1,0:T(8,128)(2,1)S(1)}, bf16[528,128]{1,0:T(8,128)(2,1)S(1)}, u32[]{:S(2)}, u32[]{:S(2)}) collective-permute-start(bf16[528,128]{1,0:T(8,128)(2,1)S(1)} %get-tuple-element.41), channel_id=1, source_target_pairs={{0,14},{2,12},{4,2},{6,0},{8,6},{10,4},{12,10},{14,8},{1,15},{3,13... | collective-permute-start | bytes 405512 | tf_op jit(solution)/shard_map/ppermute | solution.py:274
  11.5 14.9 %collective-permute-start.5 = (bf16[528,128]{1,0:T(8,128)(2,1)S(1)}, bf16[528,128]{1,0:T(8,128)(2,1)S(1)}, u32[]{:S(2)}, u32[]{:S(2)}) collective-permute-start(bf16[528,128]{1,0:T(8,128)(2,1)S(1)} %get-tuple-element.42), channel_id=1, source_target_pairs={{0,6},{2,4},{4,10},{6,8},{8,14},{10,12},{12,2},{14,0},{1,7},{3,5},... | collective-permute-start | bytes 405512 | tf_op jit(solution)/shard_map/ppermute | solution.py:274
  15.8 12.0 %collective-permute-start.6 = (bf16[528,128]{1,0:T(8,128)(2,1)S(1)}, bf16[528,128]{1,0:T(8,128)(2,1)S(1)}, u32[]{:S(2)}, u32[]{:S(2)}) collective-permute-start(bf16[528,128]{1,0:T(8,128)(2,1)S(1)} %get-tuple-element.43), channel_id=1, source_target_pairs={{0,2},{2,0},{4,6},{6,4},{8,10},{10,8},{12,14},{14,12},{1,3},{3,1},... | collective-permute-start | bytes 405512 | tf_op jit(solution)/shard_map/ppermute | solution.py:274
  19.9 11.8 %collective-permute-start.7 = (bf16[528,128]{1,0:T(8,128)(2,1)S(1)}, bf16[528,128]{1,0:T(8,128)(2,1)S(1)}, u32[]{:S(2)}, u32[]{:S(2)}) collective-permute-start(bf16[528,128]{1,0:T(8,128)(2,1)S(1)} %get-tuple-element.48), channel_id=1, source_target_pairs={{0,10},{2,8},{4,14},{6,12},{8,2},{10,0},{12,6},{14,4},{1,11},{3,9}... | collective-permute-start | bytes 405512 | tf_op jit(solution)/shard_map/ppermute | solution.py:274
  27.8 3.9 %copy-start.5 = (f32[4,512]{1,0:T(4,128)S(1)}, f32[4,512]{1,0:T(4,128)}, u32[]{:S(2)}) copy-start(f32[4,512]{1,0:T(4,128)} %gains.5) | copy-start | bytes 24580
  33.4 5.6 %collective-permute-start.10 = (bf16[64,512]{1,0:T(8,128)(2,1)S(1)}, bf16[64,512]{1,0:T(8,128)(2,1)S(1)}, u32[]{:S(2)}, u32[]{:S(2)}) collective-permute-start(bf16[64,512]{1,0:T(8,128)(2,1)S(1)} %get-tuple-element.60), channel_id=1, source_target_pairs={{0,4},{4,0},{8,12},{12,8},{1,5},{5,1},{9,13},{13,9},{2,6},{6,2},{1... | collective-permute-start | bytes 196616 | tf_op jit(solution)/shard_map/ppermute | solution.py:288
  33.4 5.6 %collective-permute-start.9 = (bf16[64,512]{1,0:T(8,128)(2,1)S(1)}, bf16[64,512]{1,0:T(8,128)(2,1)S(1)}, u32[]{:S(2)}, u32[]{:S(2)}) collective-permute-start(bf16[64,512]{1,0:T(8,128)(2,1)S(1)} %get-tuple-element.60), channel_id=1, source_target_pairs={{0,2},{2,0},{1,3},{3,1},{4,6},{6,4},{5,7},{7,5},{8,10},{10,8},{9,1... | collective-permute-start | bytes 196616 | tf_op jit(solution)/shard_map/ppermute | solution.py:279
  34.0 6.1 %collective-permute-start.8 = (bf16[64,512]{1,0:T(8,128)(2,1)S(1)}, bf16[64,512]{1,0:T(8,128)(2,1)S(1)}, u32[]{:S(2)}, u32[]{:S(2)}) collective-permute-start(bf16[64,512]{1,0:T(8,128)(2,1)S(1)} %get-tuple-element.60), channel_id=1, source_target_pairs={{4,8},{8,4},{12,0},{0,12},{5,9},{9,5},{13,1},{1,13},{6,10},{10,6},... | collective-permute-start | bytes 196616 | tf_op jit(solution)/shard_map/ppermute | solution.py:288
